TPU v7x, 32 devices: a whole 2x2x4 slice. The times are simulated.
32 devices in a mesh: groups: 2 (over x), view: 16 (over z, y, core).
Axes of the slice: x: 2, y: 2, z: 4, core: 2. Of those that a mesh axis runs over, the one named last changes fastest.
Arguments:
- images: bfloat16 [32, 4, 32, 64, 256], P(('groups', 'view')), parts along dimension 0, may hold values from 0.5 to 2
- start_estimate: float32 [512, 64, 256], P(('groups', 'view')), parts along dimension 0, may hold values from 0.5 to 1.5
- view_order: int32 [4], replicated, may hold values from 0 to 3, each once
- psf_ranks: int32 [4], replicated, may hold values from 2 to 6, as said below
- depth_taps: float32 [4, 6, 17], replicated, may hold values from 0.05 to 1
- row_taps: float32 [4, 6, 17], replicated, may hold values from 0.05 to 1
- col_taps: float32 [4, 6, 17], replicated, may hold values from 0.05 to 1
- rank_weight: float32 [4, 6], replicated, may hold values from 0.1 to 1
Outputs:
- estimate: float32 [512, 64, 256], P(('groups', 'view')), parts along dimension 0
There are 2 independent parts, one for each index of `groups`. A program takes and returns all parts, laid end to end along the dimension named above; an argument that names none is the same for every part. Nothing has to cross between parts.
Inputs may be any that keep to these rules, and one draw needn't show every extreme that they name: `view_order`: each view appears exactly once. `psf_ranks`: some view uses 6 terms and some view uses 2.
All inputs are finite; a program needn't handle non-finite values.
Results may differ from a plain program's by a relative error of at most 0.0012.
Values sent between devices are 32-bit elements; how exact they have to be, the bound alone decides.
No kernel may reach another device: no remote copies, remote signals or barrier semaphores. Data moves between devices by JAX's collectives and lax.ppermute only.
A program may use at most 64 MiB of HBM per device.

v0:
```python
import jax
import jax.numpy as jnp
from jax import lax
from jax.experimental import pallas as pl
from jax.experimental.pallas import tpu as pltpu
from jax.sharding import PartitionSpec as P

STEPS = 4
PLANES = 16
MARGIN = 8
HALF = 8
ROWS = 64
COLS = 256
GROUP = 8
QUAD = 4
TILE = 256

F32 = jnp.float32
BF16 = jnp.bfloat16
VMEM = pl.BlockSpec(memory_space=pltpu.VMEM)
SMEM = pl.BlockSpec(memory_space=pltpu.SMEM)
COST = pl.CostEstimate(flops=2**20, bytes_accessed=2**10, transcendentals=0)
HBM = pl.BlockSpec(memory_space=pltpu.HBM)


def dot(a, b):
    return jnp.dot(a, b, preferred_element_type=F32)


def iota(shape, dim):
    return lax.broadcasted_iota(jnp.int32, shape, dim)


def loop(count, body):
    def step(i, carry):
        body(i)
        return carry

    lax.fori_loop(0, count, step, 0)


def build_kernel(
    place, order, live, weight, depth_taps, row_taps, col_taps, images,
    depth_f, depth_a, row_f, row_a, col_f, col_a, *rest,
):
    slabs, ends = rest[:STEPS], rest[STEPS : 2 * STEPS]
    held, ahead, back, sems = rest[2 * STEPS :]
    copies = [
        pltpu.make_async_copy(images.at[0, step], slabs[step], sems.at[step])
        for step in range(STEPS)
    ]
    for copy in copies:
        copy.start()
    position, devices = place[0], place[1]
    for step in range(STEPS):
        block = lax.rem(position + (devices - step), devices)
        ends[step][0] = jnp.full((1, COLS), (block > 0).astype(F32))
        ends[step][1] = jnp.full((1, COLS), (block < devices - 1).astype(F32))
    views = order.shape[0]
    ranks, count = depth_taps.shape[1:]
    margin = count // 2
    view = order[lax.rem(position, views)]
    square = (TILE, TILE)

    def normal(taps):
        values = taps[view]
        return values / jnp.sum(values, axis=1, keepdims=True)

    rank = iota((ranks, 1), 0)
    weights = jnp.zeros((ranks, 1), F32)
    for r in range(ranks):
        weights = jnp.where(rank == r, weight[view, r], weights)
    weights = jnp.where(rank < live[view], weights, 0.0)
    weights = weights / jnp.sum(weights, axis=0, keepdims=True)

    def placed(values, place, to):
        held[...] = jnp.zeros(held.shape, F32)
        held[0:ranks, 0:count] = values
        k = iota((held.shape[1], TILE), 0)
        picks = (k < count) & (iota((held.shape[1], TILE), 1) == place(k))
        to[...] = dot(held[...].astype(BF16), picks.astype(F32).astype(BF16))

    def rolled(rows, r, n):
        full = jnp.broadcast_to(rows[pl.ds(r, 1)], (n, TILE))
        return pltpu.roll(full, 0, 1, stride=1, stride_axis=0)

    placed(normal(depth_taps) * weights, lambda k: GROUP * k, ahead)
    placed(normal(depth_taps) * weights, lambda k: GROUP * (count - 1 - k), back)

    def depth(r):
        depth_f[r] = rolled(ahead, r, PLANES * GROUP).astype(BF16)
        depth_a[r] = rolled(back, r, PLANES * GROUP).astype(BF16)

    loop(ranks, depth)
    i, j = iota(square, 0), iota(square, 1)
    near = jnp.abs(j - i) <= margin
    placed(normal(col_taps), lambda k: (margin - k) & (TILE - 1), ahead)
    placed(normal(col_taps), lambda k: (k - margin) & (TILE - 1), back)

    def col(r):
        col_f[r] = jnp.where(near, rolled(ahead, r, TILE), 0.0).astype(BF16)
        col_a[r] = jnp.where(near, rolled(back, r, TILE), 0.0).astype(BF16)

    loop(ranks, col)
    close = near & ((i >> 6) == (j >> 6))
    order_columns = ROWS * ((j >> 3) & (QUAD - 1)) + GROUP * (j >> 5) + (j & (GROUP - 1))
    order_columns = (i == order_columns).astype(F32).astype(BF16)
    placed(normal(row_taps), lambda k: (k - margin) & (TILE - 1), ahead)
    placed(normal(row_taps), lambda k: (margin - k) & (TILE - 1), back)

    def row(r):
        band = jnp.where(close, rolled(ahead, r, TILE), 0.0).astype(BF16)
        row_f[r] = dot(band, order_columns).astype(BF16)
        band = jnp.where(close, rolled(back, r, TILE), 0.0).astype(BF16)
        row_a[r] = dot(band, order_columns).astype(BF16)

    loop(ranks, row)
    for copy in copies:
        copy.wait()


def build(place, view_order, psf_ranks, rank_weight, depth_taps, row_taps, col_taps, images):
    ranks = depth_taps.shape[1]
    depth = jax.ShapeDtypeStruct((ranks, PLANES * GROUP, TILE), BF16)
    square = jax.ShapeDtypeStruct((ranks, TILE, TILE), BF16)
    slab = jax.ShapeDtypeStruct(images.shape[2:], BF16)
    ends = jax.ShapeDtypeStruct((2, 1, COLS), F32)
    out = pl.pallas_call(
        build_kernel,
        out_shape=[depth, depth] + [square] * 4 + [slab] * STEPS + [ends] * STEPS,
        in_specs=[SMEM] * 4 + [VMEM] * 3 + [HBM],
        out_specs=[VMEM] * (6 + 2 * STEPS),
        scratch_shapes=[
            pltpu.VMEM((8, 128), F32),
            pltpu.VMEM((8, TILE), F32),
            pltpu.VMEM((8, TILE), F32),
            pltpu.SemaphoreType.DMA((STEPS,)),
        ],
        compiler_params=pltpu.CompilerParams(vmem_limit_bytes=20 * 2**20),
        name="build",
    )(place, view_order, psf_ranks, rank_weight, depth_taps, row_taps, col_taps, images)
    return out[:6], out[6 : 6 + STEPS], out[6 + STEPS :]


def depth_pass(cells_of, op, planes, spread):
    ranks = op.shape[0]
    groups = ROWS // GROUP // 4
    lhs = op[:, 0 : planes * GROUP, :].reshape(ranks * planes * GROUP, TILE)

    def half(i):
        for g in range(groups):
            at = pl.multiple_of((i * groups + g) * GROUP, GROUP)
            cells = cells_of(pl.ds(at, GROUP))
            out = dot(lhs, cells.reshape(TILE, COLS).astype(BF16)).astype(BF16)
            out = out.reshape(ranks, planes // QUAD, QUAD * GROUP, COLS)
            to = pl.ds(pl.multiple_of(at * QUAD, QUAD * GROUP), QUAD * GROUP)
            spread[:, 0 : planes // QUAD, to, :] = out

    loop(4, half)


def row_pass(spread, op, mixed, t):
    rows = pl.ds(pl.multiple_of(t * TILE, TILE), TILE)
    for r in range(op.shape[0]):
        mixed[rows, r * COLS : (r + 1) * COLS] = dot(op[r], spread[r, t]).astype(BF16)


def col_pass(mixed, op, t):
    ranks = op.shape[0]
    rows = pl.ds(pl.multiple_of(t * TILE, TILE), TILE)
    return dot(mixed[rows, :], op[...].reshape(ranks * COLS, COLS)).reshape(QUAD, ROWS, COLS)


def window(refs, scales=None):
    def read(y):
        parts, left = [], 2 * PLANES
        for i, (ref, at) in enumerate(refs):
            n = min(left, ref.shape[0] - at)
            cells = ref[at : at + n, y, :]
            if scales is not None and scales[i] is not None:
                cells = cells * scales[i]
            parts.append(cells)
            left -= n
        while left > 0:
            n = min(left, parts[0].shape[0])
            parts.append(parts[0][:n])
            left -= n
        return jnp.concatenate(parts, axis=0)

    return read


def call(kernel, name, arrays, shared, ops, outs, scratch):
    out = [jax.ShapeDtypeStruct((n, ROWS, COLS), F32) for n in outs]
    return pl.pallas_call(
        kernel,
        out_shape=out,
        in_specs=[VMEM] * (len(arrays) + len(shared) + len(ops)),
        out_specs=[VMEM] * len(out),
        scratch_shapes=[pltpu.VMEM(shape, BF16) for shape in scratch],
        compiler_params=pltpu.CompilerParams(vmem_limit_bytes=20 * 2**20),
        cost_estimate=COST,
        name=name,
    )(*arrays, *shared, *ops)


def upper_ratio(own, above, shared, ops):
    parts = len(own) + len(above)
    tiles = PLANES // QUAD

    def kernel(*refs):
        slab, ends, depth, row, col, ratio, spread, mixed = refs[parts:]
        live = ends[1]
        scales = [None] * len(own) + [live] * len(above)
        cells = window([(ref, 0) for ref in refs[:parts]], scales)
        depth_pass(cells, depth, PLANES, spread)

        def pair(i):
            for t in (i,):
                row_pass(spread, row, mixed, t)
            for t in (i,):
                planes = pl.ds(t * QUAD, QUAD)
                seen = slab[pl.ds(PLANES + t * QUAD, QUAD)].astype(F32)
                ratio[planes] = seen / col_pass(mixed, col, t)

        loop(tiles, pair)
        ratio[HALF:] = ratio[HALF:] * live

    ranks = ops[0].shape[0]
    scratch = [(ranks, tiles, TILE, COLS), (tiles * TILE, ranks * COLS)]
    return call(kernel, "upper", own + above, shared, ops[0::2], [PLANES], scratch)[0]


def half_update(start, below, own, ratios, shared, ops):
    parts = len(below) + len(own)
    given = parts + len(ratios)
    tiles = HALF // QUAD

    def kernel(*refs):
        slab, ends, depth_f, depth_a, row_f, row_a, col_f, col_a = refs[given : given + 8]
        ratio, updated, spread, mixed = refs[given + 8 :]
        live = ends[0]
        scales = [live] * len(below) + [None] * len(own)

        def divide(t):
            row_pass(spread, row_f, mixed, t)
            seen = slab[pl.ds(start + t * QUAD, QUAD)].astype(F32)
            value = seen / col_pass(mixed, col_f, t)
            ratio[pl.ds(t * QUAD, QUAD)] = value * live if start == 0 else value

        def back(t):
            row_pass(spread, row_a, mixed, t)
            planes = pl.ds(t * QUAD, QUAD)
            updated[planes] = refs[parts - 1][planes] * col_pass(mixed, col_a, t)

        depth_pass(window([(ref, 0) for ref in refs[:parts]], scales), depth_f, HALF, spread)
        loop(tiles, divide)
        cells = window([(ref, 0) for ref in (ratio,) + refs[parts:given]])
        depth_pass(cells, depth_a, HALF, spread)
        loop(tiles, back)

    ranks = ops[0].shape[0]
    scratch = [(ranks, tiles, TILE, COLS), (tiles * TILE, ranks * COLS)]
    return call(kernel, "half", below + own + ratios, shared, ops, [HALF, HALF], scratch)


def placed_half(half, start, whole=None):
    extra = [] if whole is None else [whole]

    def kernel(*refs):
        half, out, sem = refs[0], refs[-2], refs[-1]
        copy = pltpu.make_async_copy(half, out.at[pl.ds(start, HALF)], sem)
        copy.start()
        copy.wait()

    return pl.pallas_call(
        kernel,
        out_shape=jax.ShapeDtypeStruct((PLANES, ROWS, COLS), F32),
        in_specs=[VMEM] + [HBM] * len(extra),
        out_specs=HBM,
        scratch_shapes=[pltpu.SemaphoreType.DMA],
        input_output_aliases={1: 0} if extra else {},
        compiler_params=pltpu.CompilerParams(vmem_limit_bytes=20 * 2**20),
        cost_estimate=COST,
        name="place",
    )(half, *extra)


def shards(
    images, start_estimate, view_order, psf_ranks, depth_taps, row_taps, col_taps, rank_weight
):
    count = lax.axis_size("view")

    def send(cells, by, relayed=None, skip=()):
        pairs = []
        for i in range(count):
            way = relayed[1] if relayed and i % 4 == relayed[0] else by
            if i not in skip:
                pairs.append((i, (i + way) % count))
        return lax.ppermute(cells, "view", pairs)

    above = [send(start_estimate, -1)]
    place = jnp.stack([lax.axis_index("view"), count]).astype(jnp.int32)
    ops, slabs, ends = build(
        place, view_order, psf_ranks, rank_weight, depth_taps, row_taps, col_taps, images
    )
    own_lo, own_hi = start_estimate[:HALF], start_estimate[HALF:]
    early_hi, _ = lax.optimization_barrier((own_hi, ops[0]))
    below_hi = send(early_hi, 1, skip=(count - 1,))
    early_lo, _ = lax.optimization_barrier((own_lo, above[0]))
    below_lo = send(early_lo, 1)

    for step in range(STEPS):
        last = step == STEPS - 1
        shared = [slabs[step], ends[step]]
        ratio_up = upper_ratio([own_lo, own_hi], above, shared, ops)
        ratio_mid, hi = half_update(HALF, [below_hi], [own_lo, own_hi], [ratio_up], shared, ops)
        next_hi = send(hi, 1 - STEPS, (1, 1)) if last else send(hi, 1)
        _, lo = half_update(
            0, [below_lo, below_hi], [own_lo], [ratio_mid, ratio_up], shared, ops
        )
        above = [lo, hi]
        if last:
            next_hi, _ = lax.optimization_barrier((next_hi, lo))
            own_lo = send(lo, 1 - STEPS)
            own_hi = send(next_hi, 0, (2, -STEPS))
        else:
            own_lo, own_hi = send(lo, 1), next_hi
            below_hi = send(own_hi, 1)
            below_lo = send(own_lo, 1)
    return placed_half(own_hi, HALF, placed_half(own_lo, 0))


def solution(mesh):
    in_specs = (
        P(("groups", "view"), None, None, None, None),
        P(("groups", "view"), None, None),
        P(),
        P(),
        P(),
        P(),
        P(),
        P(),
    )
    out_specs = P(("groups", "view"), None, None)
    return jax.shard_map(shards, mesh=mesh, in_specs=in_specs, out_specs=out_specs, check_vma=False)
```

profile of v0, /device:TPU:28, one launch (start us, length us, event | category | flops | bytes accessed | tf_op | source)
XLA Modules:
  0.0 133.6 jit_solution(12234233222891878924)
XLA Ops:
  0.0 0.7 copy.10.depth_taps
  0.7 0.7 copy.11.row_taps
  1.4 0.7 copy.12.col_taps
  2.1 0.1 pad_add_fusion.place
  2.2 2.2 %copy-done = bf16[1,4,32,64,256]{4,3,2,1,0:T(8,128)(2,1)S(1)} copy-done((bf16[1,4,32,64,256]{4,3,2,1,0:T(8,128)(2,1)S(1)}, bf16[1,4,32,64,256]{4,3,2,1,0:T(8,128)(2,1)}, u32[]{:S(2)}) %copy-start) | copy-done | bytes 4194328
  4.4 0.7 copy-done.1
  5.1 0.7 copy-done.2
  5.7 0.7 copy-done.3
  6.4 4.6 %build.1 = (bf16[6,128,256]{2,1,0:T(8,128)(2,1)S(1)}, bf16[6,128,256]{2,1,0:T(8,128)(2,1)S(1)}, bf16[6,256,256]{2,1,0:T(8,128)(2,1)S(1)}, bf16[6,256,256]{2,1,0:...) custom-call(s32[2]{0:T(128)S(1)} %pad_add_fusion.place, ...), custom_call_target="tpu_custom_call" | custom-call | tf_op jit(solution)/shard_map/build/pallas_call | solution.py:128
  11.0 0.1 fusion
  11.1 2.4 %collective-permute-start = (f32[8,64,256]{2,1,0:T(8,128)S(1)}, f32[8,64,256]{2,1,0:T(8,128)S(1)}, u32[]{:S(2)}, u32[]{:S(2)}) collective-permute-start(f32[8,64,256]{2,1,0:T(8,128)S(1)} %get-tuple-element.35.refs_1_.refs_2_), channel_id=1, source_target_pairs={{0,1},{1,2},{2,3},{3,4},{4,5},{5,6},{6,7},{7,8},{8,9},{9,10},{10,1... | collective-permute-start | bytes 1572872 | tf_op jit(solution)/shard_map/ppermute | solution.py:300
  13.5 3.6 %collective-permute-start.4 = (f32[8,64,256]{2,1,0:T(8,128)S(1)}, f32[8,64,256]{2,1,0:T(8,128)S(1)}, u32[]{:S(2)}, u32[]{:S(2)}) collective-permute-start(f32[8,64,256]{2,1,0:T(8,128)S(1)} %get-tuple-element.44.refs_0_.refs_1_.refs_2_), channel_id=1, source_target_pairs={{0,1},{1,2},{2,3},{3,4},{4,5},{5,6},{6,7},{7,8},{8,9},{9,10},{10,1... | collective-permute-start | bytes 1572872 | tf_op jit(solution)/shard_map/ppermute | solution.py:300
  17.1 4.4 %upper.4.refs_3_.refs_4_ = f32[16,64,256]{2,1,0:T(8,128)S(1)} custom-call(f32[8,64,256]{2,1,0:T(8,128)S(1)} %get-tuple-element.44.refs_0_.refs_1_.refs_2_, f32[8,64,256]{2,1,0:T(8,128)S(1)} %get-tuple-element.35.refs_1_.refs_2_, f32[16,64,256]{2,1,0:T(8,128)S(1)} %collective-permute-done.1.refs_2_, ...), custom_call_target="tpu_custom_call" | custom-call | flops 1048576 | bytes 1024 | tf_op jit(solution)/shard_map/upper/pallas_call | solution.py:195
  21.5 1.3 collective-permute-done.refs_0_.refs_1_
  22.8 5.0 %half.8 = (f32[8,64,256]{2,1,0:T(8,128)S(1)}, f32[8,64,256]{2,1,0:T(8,128)S(1)}) custom-call(f32[8,64,256]{2,1,0:T(8,128)S(1)} %collective-permute-done.refs_0_.refs_1_, f32[8,64,256]{2,1,0:T(8,128)S(1)} %get-tuple-element.44.refs_0_.refs_1_.refs_2_, f32[8,64,256]{2,1,0:T(8,128)S(1)} %get-tuple-element.35.refs_1_.refs_2_, ...), custom_call_target="tpu_custom_call" | custom-call | flops 1048576 | bytes 1024 | tf_op jit(solution)/shard_map/half/pallas_call | solution.py:195
  27.8 0.1 collective-permute-start.2
  27.9 0.5 collective-permute-done.4.refs_0_
  28.4 5.5 %half.9 = (f32[8,64,256]{2,1,0:T(8,128)}, f32[8,64,256]{2,1,0:T(8,128)S(1)}) custom-call(f32[8,64,256]{2,1,0:T(8,128)S(1)} %collective-permute-done.4.refs_0_, f32[8,64,256]{2,1,0:T(8,128)S(1)} %collective-permute-done.refs_0_.refs_1_, f32[8,64,256]{2,1,0:T(8,128)S(1)} %get-tuple-element.44.refs_0_.refs_1_.refs_2_, ...), custom_call_target="tpu_custom_call" | custom-call | flops 1048576 | bytes 1024 | tf_op jit(solution)/shard_map/half/pallas_call | solution.py:195
  33.9 2.6 %collective-permute-done.2.refs_1_.refs_2_ = f32[8,64,256]{2,1,0:T(8,128)S(1)} collective-permute-done((f32[8,64,256]{2,1,0:T(8,128)S(1)}, f32[8,64,256]{2,1,0:T(8,128)S(1)}, u32[]{:S(2)}, u32[]{:S(2)}) %collective-permute-start.2) | collective-permute-done | bytes 524320 | tf_op jit(solution)/shard_map/ppermute | solution.py:300
  36.5 6.0 %collective-permute-done.5.refs_0_.refs_1_.refs_2_ = f32[8,64,256]{2,1,0:T(8,128)S(1)} collective-permute-done((f32[8,64,256]{2,1,0:T(8,128)S(1)}, f32[8,64,256]{2,1,0:T(8,128)S(1)}, u32[]{:S(2)}, u32[]{:S(2)}) %collective-permute-start.5) | collective-permute-done | bytes 524320 | tf_op jit(solution)/shard_map/ppermute | solution.py:300
  42.5 4.4 %upper.5.refs_3_.refs_4_ = f32[16,64,256]{2,1,0:T(8,128)S(1)} custom-call(f32[8,64,256]{2,1,0:T(8,128)S(1)} %collective-permute-done.5.refs_0_.refs_1_.refs_2_, f32[8,64,256]{2,1,0:T(8,128)S(1)} %collective-permute-done.2.refs_1_.refs_2_, f32[8,64,256]{2,1,0:T(8,128)S(1)} %get-tuple-element.46.refs_2_, f32[8,64,256]{2,1,0:T(8,128)S(1)} %get-tuple-element.43.refs_3_, ...), custom_call_target="tpu_custom_call" | custom-call | flops 1048576 | bytes 1024 | tf_op jit(solution)/shard_map/upper/pallas_call | solution.py:195
  46.9 1.2 collective-permute-done.3.refs_0_.refs_1_
  48.1 5.0 %half.10 = (f32[8,64,256]{2,1,0:T(8,128)S(1)}, f32[8,64,256]{2,1,0:T(8,128)S(1)}) custom-call(f32[8,64,256]{2,1,0:T(8,128)S(1)} %collective-permute-done.3.refs_0_.refs_1_, f32[8,64,256]{2,1,0:T(8,128)S(1)} %collective-permute-done.5.refs_0_.refs_1_.refs_2_, f32[8,64,256]{2,1,0:T(8,128)S(1)} %collective-permute-done.2.refs_1_.refs_2_, ...), custom_call_target="tpu_custom_call" | custom-call | flops 1048576 | bytes 1024 | tf_op jit(solution)/shard_map/half/pallas_call | solution.py:195
  53.1 1.6 %collective-permute-start.6 = (f32[8,64,256]{2,1,0:T(8,128)S(1)}, f32[8,64,256]{2,1,0:T(8,128)S(1)}, u32[]{:S(2)}, u32[]{:S(2)}) collective-permute-start(f32[8,64,256]{2,1,0:T(8,128)S(1)} %get-tuple-element.49.refs_3_), channel_id=1, source_target_pairs={{0,1},{1,2},{2,3},{3,4},{4,5},{5,6},{6,7},{7,8},{8,9},{9,10},{10,1... | collective-permute-start | bytes 1572872 | tf_op jit(solution)/shard_map/ppermute | solution.py:300
  54.7 5.5 %half.11 = (f32[8,64,256]{2,1,0:T(8,128)}, f32[8,64,256]{2,1,0:T(8,128)S(1)}) custom-call(f32[8,64,256]{2,1,0:T(8,128)S(1)} %collective-permute-done.8.refs_0_, f32[8,64,256]{2,1,0:T(8,128)S(1)} %collective-permute-done.3.refs_0_.refs_1_, f32[8,64,256]{2,1,0:T(8,128)S(1)} %collective-permute-done.5.refs_0_.refs_1_.refs_2_, ...), custom_call_target="tpu_custom_call" | custom-call | flops 1048576 | bytes 1024 | tf_op jit(solution)/shard_map/half/pallas_call | solution.py:195
  60.1 1.2 collective-permute-start.9
  61.3 0.4 collective-permute-done.6.refs_1_.refs_2_
  61.8 0.2 collective-permute-start.7
  62.0 6.8 %collective-permute-done.9.refs_0_.refs_1_.refs_2_ = f32[8,64,256]{2,1,0:T(8,128)S(1)} collective-permute-done((f32[8,64,256]{2,1,0:T(8,128)S(1)}, f32[8,64,256]{2,1,0:T(8,128)S(1)}, u32[]{:S(2)}, u32[]{:S(2)}) %collective-permute-start.9) | collective-permute-done | bytes 524320 | tf_op jit(solution)/shard_map/ppermute | solution.py:300
  68.8 4.4 %upper.6.refs_3_.refs_4_ = f32[16,64,256]{2,1,0:T(8,128)S(1)} custom-call(f32[8,64,256]{2,1,0:T(8,128)S(1)} %collective-permute-done.9.refs_0_.refs_1_.refs_2_, f32[8,64,256]{2,1,0:T(8,128)S(1)} %collective-permute-done.6.refs_1_.refs_2_, f32[8,64,256]{2,1,0:T(8,128)S(1)} %get-tuple-element.51.refs_2_, f32[8,64,256]{2,1,0:T(8,128)S(1)} %get-tuple-element.49.refs_3_, ...), custom_call_target="tpu_custom_call" | custom-call | flops 1048576 | bytes 1024 | tf_op jit(solution)/shard_map/upper/pallas_call | solution.py:195
  73.2 1.2 collective-permute-done.7.refs_0_.refs_1_
  74.4 5.0 %half.12 = (f32[8,64,256]{2,1,0:T(8,128)S(1)}, f32[8,64,256]{2,1,0:T(8,128)S(1)}) custom-call(f32[8,64,256]{2,1,0:T(8,128)S(1)} %collective-permute-done.7.refs_0_.refs_1_, f32[8,64,256]{2,1,0:T(8,128)S(1)} %collective-permute-done.9.refs_0_.refs_1_.refs_2_, f32[8,64,256]{2,1,0:T(8,128)S(1)} %collective-permute-done.6.refs_1_.refs_2_, ...), custom_call_target="tpu_custom_call" | custom-call | flops 1048576 | bytes 1024 | tf_op jit(solution)/shard_map/half/pallas_call | solution.py:195
  79.4 3.4 %collective-permute-start.10 = (f32[8,64,256]{2,1,0:T(8,128)S(1)}, f32[8,64,256]{2,1,0:T(8,128)S(1)}, u32[]{:S(2)}, u32[]{:S(2)}) collective-permute-start(f32[8,64,256]{2,1,0:T(8,128)S(1)} %get-tuple-element.54.refs_3_), channel_id=1, source_target_pairs={{0,1},{1,2},{2,3},{3,4},{4,5},{5,6},{6,7},{7,8},{8,9},{9,10},{10,1... | collective-permute-start | bytes 1572872 | tf_op jit(solution)/shard_map/ppermute | solution.py:300
  82.8 5.5 %half.13 = (f32[8,64,256]{2,1,0:T(8,128)}, f32[8,64,256]{2,1,0:T(8,128)S(1)}) custom-call(f32[8,64,256]{2,1,0:T(8,128)S(1)} %collective-permute-done.12.refs_0_, f32[8,64,256]{2,1,0:T(8,128)S(1)} %collective-permute-done.7.refs_0_.refs_1_, f32[8,64,256]{2,1,0:T(8,128)S(1)} %collective-permute-done.9.refs_0_.refs_1_.refs_2_, ...), custom_call_target="tpu_custom_call" | custom-call | flops 1048576 | bytes 1024 | tf_op jit(solution)/shard_map/half/pallas_call | solution.py:195
  88.2 1.2 collective-permute-start.13
  89.4 0.7 collective-permute-start.11
  90.1 6.8 %collective-permute-done.13.refs_0_.refs_1_.refs_2_ = f32[8,64,256]{2,1,0:T(8,128)S(1)} collective-permute-done((f32[8,64,256]{2,1,0:T(8,128)S(1)}, f32[8,64,256]{2,1,0:T(8,128)S(1)}, u32[]{:S(2)}, u32[]{:S(2)}) %collective-permute-start.13) | collective-permute-done | bytes 524320 | tf_op jit(solution)/shard_map/ppermute | solution.py:300
  96.8 4.4 %upper.7.refs_3_.refs_4_ = f32[16,64,256]{2,1,0:T(8,128)S(1)} custom-call(f32[8,64,256]{2,1,0:T(8,128)S(1)} %collective-permute-done.13.refs_0_.refs_1_.refs_2_, f32[8,64,256]{2,1,0:T(8,128)S(1)} %collective-permute-done.10.refs_1_.refs_2_, f32[8,64,256]{2,1,0:T(8,128)S(1)} %get-tuple-element.56.refs_2_, f32[8,64,256]{2,1,0:T(8,128)S(1)} %get-tuple-element.54.refs_3_, ...), custom_call_target="tpu_custom_call" | custom-call | flops 1048576 | bytes 1024 | tf_op jit(solution)/shard_map/upper/pallas_call | solution.py:195
  101.3 1.2 collective-permute-done.11.refs_0_.refs_1_
  102.4 5.0 %half.14 = (f32[8,64,256]{2,1,0:T(8,128)S(1)}, f32[8,64,256]{2,1,0:T(8,128)S(1)}) custom-call(f32[8,64,256]{2,1,0:T(8,128)S(1)} %collective-permute-done.11.refs_0_.refs_1_, f32[8,64,256]{2,1,0:T(8,128)S(1)} %collective-permute-done.13.refs_0_.refs_1_.refs_2_, f32[8,64,256]{2,1,0:T(8,128)S(1)} %collective-permute-done.10.refs_1_.refs_2_, ...), custom_call_target="tpu_custom_call" | custom-call | flops 1048576 | bytes 1024 | tf_op jit(solution)/shard_map/half/pallas_call | solution.py:195
  107.5 0.5 collective-permute-done.15.refs_0_
  108.1 5.5 %half.15 = (f32[8,64,256]{2,1,0:T(8,128)}, f32[8,64,256]{2,1,0:T(8,128)S(1)}) custom-call(f32[8,64,256]{2,1,0:T(8,128)S(1)} %collective-permute-done.15.refs_0_, f32[8,64,256]{2,1,0:T(8,128)S(1)} %collective-permute-done.11.refs_0_.refs_1_, f32[8,64,256]{2,1,0:T(8,128)S(1)} %collective-permute-done.13.refs_0_.refs_1_.refs_2_, ...), custom_call_target="tpu_custom_call" | custom-call | flops 1048576 | bytes 1024 | tf_op jit(solution)/shard_map/half/pallas_call | solution.py:195
  113.5 2.6 %collective-permute-done.14 = f32[8,64,256]{2,1,0:T(8,128)S(1)} collective-permute-done((f32[8,64,256]{2,1,0:T(8,128)S(1)}, f32[8,64,256]{2,1,0:T(8,128)S(1)}, u32[]{:S(2)}, u32[]{:S(2)}) %collective-permute-start.14) | collective-permute-done | bytes 524320 | tf_op jit(solution)/shard_map/ppermute | solution.py:300
  116.1 1.9 %collective-permute-start.16 = (f32[8,64,256]{2,1,0:T(8,128)S(1)}, f32[8,64,256]{2,1,0:T(8,128)S(1)}, u32[]{:S(2)}, u32[]{:S(2)}) collective-permute-start(f32[8,64,256]{2,1,0:T(8,128)S(1)} %collective-permute-done.14), channel_id=1, source_target_pairs={{0,0},{1,1},{2,14},{3,3},{4,4},{5,5},{6,2},{7,7},{8,8},{9,9},{10,6... | collective-permute-start | bytes 1572872 | tf_op jit(solution)/shard_map/ppermute | solution.py:300
  118.1 12.1 %collective-permute-done.17.refs_0_ = f32[8,64,256]{2,1,0:T(8,128)S(1)} collective-permute-done((f32[8,64,256]{2,1,0:T(8,128)S(1)}, f32[8,64,256]{2,1,0:T(8,128)S(1)}, u32[]{:S(2)}, u32[]{:S(2)}) %collective-permute-start.17) | collective-permute-done | bytes 524320 | tf_op jit(solution)/shard_map/ppermute | solution.py:300
  130.2 0.8 place.2.refs_1_
  131.0 1.6 %collective-permute-done.16.refs_0_ = f32[8,64,256]{2,1,0:T(8,128)S(1)} collective-permute-done((f32[8,64,256]{2,1,0:T(8,128)S(1)}, f32[8,64,256]{2,1,0:T(8,128)S(1)}, u32[]{:S(2)}, u32[]{:S(2)}) %collective-permute-start.16) | collective-permute-done | bytes 524320 | tf_op jit(solution)/shard_map/ppermute | solution.py:300
  132.6 0.8 place.3
  (18 shorter events, 0.1 us)
Async XLA Ops:
  0.0 13.5 %collective-permute-start.1 = (f32[16,64,256]{2,1,0:T(8,128)}, f32[16,64,256]{2,1,0:T(8,128)S(1)}, u32[]{:S(2)}, u32[]{:S(2)}) collective-permute-start(f32[16,64,256]{2,1,0:T(8,128)} %param.9), channel_id=1, source_target_pairs={{0,15},{1,0},{2,1},{3,2},{4,3},{5,4},{6,5},{7,6},{8,7},{9,8},{10,9... | collective-permute-start | bytes 3145736 | tf_op jit(solution)/shard_map/ppermute | solution.py:300
  2.2 2.2 %copy-start = (bf16[1,4,32,64,256]{4,3,2,1,0:T(8,128)(2,1)S(1)}, bf16[1,4,32,64,256]{4,3,2,1,0:T(8,128)(2,1)}, u32[]{:S(2)}) copy-start(bf16[1,4,32,64,256]{4,3,2,1,0:T(8,128)(2,1)} %images.1) | copy-start | bytes 12582916
  4.4 0.7 copy-start.1
  5.1 0.7 copy-start.2
  5.7 0.7 copy-start.3
  6.4 4.6 %copy-start.4 = (f32[16,64,256]{2,1,0:T(8,128)S(1)}, f32[16,64,256]{2,1,0:T(8,128)}, u32[]{:S(2)}) copy-start(f32[16,64,256]{2,1,0:T(8,128)} %param.9) | copy-start | bytes 3145732
  11.1 11.7 %collective-permute-start = (f32[8,64,256]{2,1,0:T(8,128)S(1)}, f32[8,64,256]{2,1,0:T(8,128)S(1)}, u32[]{:S(2)}, u32[]{:S(2)}) collective-permute-start(f32[8,64,256]{2,1,0:T(8,128)S(1)} %get-tuple-element.35.refs_1_.refs_2_), channel_id=1, source_target_pairs={{0,1},{1,2},{2,3},{3,4},{4,5},{5,6},{6,7},{7,8},{8,9},{9,10},{10,1... | collective-permute-start | bytes 1572872 | tf_op jit(solution)/shard_map/ppermute | solution.py:300
  13.5 14.9 %collective-permute-start.4 = (f32[8,64,256]{2,1,0:T(8,128)S(1)}, f32[8,64,256]{2,1,0:T(8,128)S(1)}, u32[]{:S(2)}, u32[]{:S(2)}) collective-permute-start(f32[8,64,256]{2,1,0:T(8,128)S(1)} %get-tuple-element.44.refs_0_.refs_1_.refs_2_), channel_id=1, source_target_pairs={{0,1},{1,2},{2,3},{3,4},{4,5},{5,6},{6,7},{7,8},{8,9},{9,10},{10,1... | collective-permute-start | bytes 1572872 | tf_op jit(solution)/shard_map/ppermute | solution.py:300
  27.8 8.7 %collective-permute-start.2 = (f32[8,64,256]{2,1,0:T(8,128)S(1)}, f32[8,64,256]{2,1,0:T(8,128)S(1)}, u32[]{:S(2)}, u32[]{:S(2)}) collective-permute-start(f32[8,64,256]{2,1,0:T(8,128)S(1)} %get-tuple-element.43.refs_3_), channel_id=1, source_target_pairs={{0,1},{1,2},{2,3},{3,4},{4,5},{5,6},{6,7},{7,8},{8,9},{9,10},{10,1... | collective-permute-start | bytes 1572872 | tf_op jit(solution)/shard_map/ppermute | solution.py:300
  33.8 8.6 %collective-permute-start.5 = (f32[8,64,256]{2,1,0:T(8,128)S(1)}, f32[8,64,256]{2,1,0:T(8,128)S(1)}, u32[]{:S(2)}, u32[]{:S(2)}) collective-permute-start(f32[8,64,256]{2,1,0:T(8,128)S(1)} %get-tuple-element.46.refs_2_), channel_id=1, source_target_pairs={{0,1},{1,2},{2,3},{3,4},{4,5},{5,6},{6,7},{7,8},{8,9},{9,10},{10,1... | collective-permute-start | bytes 1572872 | tf_op jit(solution)/shard_map/ppermute | solution.py:300
  36.4 11.6 %collective-permute-start.3 = (f32[8,64,256]{2,1,0:T(8,128)S(1)}, f32[8,64,256]{2,1,0:T(8,128)S(1)}, u32[]{:S(2)}, u32[]{:S(2)}) collective-permute-start(f32[8,64,256]{2,1,0:T(8,128)S(1)} %collective-permute-done.2.refs_1_.refs_2_), channel_id=1, source_target_pairs={{0,1},{1,2},{2,3},{3,4},{4,5},{5,6},{6,7},{7,8},{8,9},{9,10},{10,1... | collective-permute-start | bytes 1572872 | tf_op jit(solution)/shard_map/ppermute | solution.py:300
  42.5 12.2 %collective-permute-start.8 = (f32[8,64,256]{2,1,0:T(8,128)S(1)}, f32[8,64,256]{2,1,0:T(8,128)S(1)}, u32[]{:S(2)}, u32[]{:S(2)}) collective-permute-start(f32[8,64,256]{2,1,0:T(8,128)S(1)} %collective-permute-done.5.refs_0_.refs_1_.refs_2_), channel_id=1, source_target_pairs={{0,1},{1,2},{2,3},{3,4},{4,5},{5,6},{6,7},{7,8},{8,9},{9,10},{10,1... | collective-permute-start | bytes 1572872 | tf_op jit(solution)/shard_map/ppermute | solution.py:300
  53.1 8.7 %collective-permute-start.6 = (f32[8,64,256]{2,1,0:T(8,128)S(1)}, f32[8,64,256]{2,1,0:T(8,128)S(1)}, u32[]{:S(2)}, u32[]{:S(2)}) collective-permute-start(f32[8,64,256]{2,1,0:T(8,128)S(1)} %get-tuple-element.49.refs_3_), channel_id=1, source_target_pairs={{0,1},{1,2},{2,3},{3,4},{4,5},{5,6},{6,7},{7,8},{8,9},{9,10},{10,1... | collective-permute-start | bytes 1572872 | tf_op jit(solution)/shard_map/ppermute | solution.py:300
  60.1 8.6 %collective-permute-start.9 = (f32[8,64,256]{2,1,0:T(8,128)S(1)}, f32[8,64,256]{2,1,0:T(8,128)S(1)}, u32[]{:S(2)}, u32[]{:S(2)}) collective-permute-start(f32[8,64,256]{2,1,0:T(8,128)S(1)} %get-tuple-element.51.refs_2_), channel_id=1, source_target_pairs={{0,1},{1,2},{2,3},{3,4},{4,5},{5,6},{6,7},{7,8},{8,9},{9,10},{10,1... | collective-permute-start | bytes 1572872 | tf_op jit(solution)/shard_map/ppermute | solution.py:300
  61.8 12.6 %collective-permute-start.7 = (f32[8,64,256]{2,1,0:T(8,128)S(1)}, f32[8,64,256]{2,1,0:T(8,128)S(1)}, u32[]{:S(2)}, u32[]{:S(2)}) collective-permute-start(f32[8,64,256]{2,1,0:T(8,128)S(1)} %collective-permute-done.6.refs_1_.refs_2_), channel_id=1, source_target_pairs={{0,1},{1,2},{2,3},{3,4},{4,5},{5,6},{6,7},{7,8},{8,9},{9,10},{10,1... | collective-permute-start | bytes 1572872 | tf_op jit(solution)/shard_map/ppermute | solution.py:300
  68.8 14.0 %collective-permute-start.12 = (f32[8,64,256]{2,1,0:T(8,128)S(1)}, f32[8,64,256]{2,1,0:T(8,128)S(1)}, u32[]{:S(2)}, u32[]{:S(2)}) collective-permute-start(f32[8,64,256]{2,1,0:T(8,128)S(1)} %collective-permute-done.9.refs_0_.refs_1_.refs_2_), channel_id=1, source_target_pairs={{0,1},{1,2},{2,3},{3,4},{4,5},{5,6},{6,7},{7,8},{8,9},{9,10},{10,1... | collective-permute-start | bytes 1572872 | tf_op jit(solution)/shard_map/ppermute | solution.py:300
  79.4 10.0 %collective-permute-start.10 = (f32[8,64,256]{2,1,0:T(8,128)S(1)}, f32[8,64,256]{2,1,0:T(8,128)S(1)}, u32[]{:S(2)}, u32[]{:S(2)}) collective-permute-start(f32[8,64,256]{2,1,0:T(8,128)S(1)} %get-tuple-element.54.refs_3_), channel_id=1, source_target_pairs={{0,1},{1,2},{2,3},{3,4},{4,5},{5,6},{6,7},{7,8},{8,9},{9,10},{10,1... | collective-permute-start | bytes 1572872 | tf_op jit(solution)/shard_map/ppermute | solution.py:300
  88.2 8.6 %collective-permute-start.13 = (f32[8,64,256]{2,1,0:T(8,128)S(1)}, f32[8,64,256]{2,1,0:T(8,128)S(1)}, u32[]{:S(2)}, u32[]{:S(2)}) collective-permute-start(f32[8,64,256]{2,1,0:T(8,128)S(1)} %get-tuple-element.56.refs_2_), channel_id=1, source_target_pairs={{0,1},{1,2},{2,3},{3,4},{4,5},{5,6},{6,7},{7,8},{8,9},{9,10},{10,1... | collective-permute-start | bytes 1572872 | tf_op jit(solution)/shard_map/ppermute | solution.py:300
  89.4 13.0 %collective-permute-start.11 = (f32[8,64,256]{2,1,0:T(8,128)S(1)}, f32[8,64,256]{2,1,0:T(8,128)S(1)}, u32[]{:S(2)}, u32[]{:S(2)}) collective-permute-start(f32[8,64,256]{2,1,0:T(8,128)S(1)} %collective-permute-done.10.refs_1_.refs_2_), channel_id=1, source_target_pairs={{0,1},{1,2},{2,3},{3,4},{4,5},{5,6},{6,7},{7,8},{8,9},{9,10},{10,1... | collective-permute-start | bytes 1572872 | tf_op jit(solution)/shard_map/ppermute | solution.py:300
  96.8 11.2 %collective-permute-start.15 = (f32[8,64,256]{2,1,0:T(8,128)S(1)}, f32[8,64,256]{2,1,0:T(8,128)S(1)}, u32[]{:S(2)}, u32[]{:S(2)}) collective-permute-start(f32[8,64,256]{2,1,0:T(8,128)S(1)} %collective-permute-done.13.refs_0_.refs_1_.refs_2_), channel_id=1, source_target_pairs={{0,1},{1,2},{2,3},{3,4},{4,5},{5,6},{6,7},{7,8},{8,9},{9,10},{10,1... | collective-permute-start | bytes 1572872 | tf_op jit(solution)/shard_map/ppermute | solution.py:300
  107.5 8.7 %collective-permute-start.14 = (f32[8,64,256]{2,1,0:T(8,128)S(1)}, f32[8,64,256]{2,1,0:T(8,128)S(1)}, u32[]{:S(2)}, u32[]{:S(2)}) collective-permute-start(f32[8,64,256]{2,1,0:T(8,128)S(1)} %get-tuple-element.59), channel_id=1, source_target_pairs={{0,13},{1,2},{2,15},{3,0},{4,1},{5,6},{6,3},{7,4},{8,5},{9,10},{10... | collective-permute-start | bytes 1572872 | tf_op jit(solution)/shard_map/ppermute | solution.py:300
  113.5 16.7 %collective-permute-start.17 = (f32[8,64,256]{2,1,0:T(8,128)S(1)}, f32[8,64,256]{2,1,0:T(8,128)S(1)}, u32[]{:S(2)}, u32[]{:S(2)}) collective-permute-start(f32[8,64,256]{2,1,0:T(8,128)S(1)} %get-tuple-element.61), channel_id=1, source_target_pairs={{0,13},{1,14},{2,15},{3,0},{4,1},{5,2},{6,3},{7,4},{8,5},{9,6},{10... | collective-permute-start | bytes 1572872 | tf_op jit(solution)/shard_map/ppermute | solution.py:300
  116.1 16.5 %collective-permute-start.16 = (f32[8,64,256]{2,1,0:T(8,128)S(1)}, f32[8,64,256]{2,1,0:T(8,128)S(1)}, u32[]{:S(2)}, u32[]{:S(2)}) collective-permute-start(f32[8,64,256]{2,1,0:T(8,128)S(1)} %collective-permute-done.14), channel_id=1, source_target_pairs={{0,0},{1,1},{2,14},{3,3},{4,4},{5,5},{6,2},{7,7},{8,8},{9,9},{10,6... | collective-permute-start | bytes 1572872 | tf_op jit(solution)/shard_map/ppermute | solution.py:300
where the time goes:
time: 134 us
  Pallas kernels  65.8 us (49%)
  waiting for transfers between devices  44.9 us (34%)
  starting transfers between devices  16.2 us (12%)
  local copies, waits for them, and re-layouts  6.38 us (5%)
    pallas_call x12, Pallas kernels, call(): pl.pallas_call(kernel, out_shape=out, in_specs=[VMEM] * (len(arrays) + le...  59.6 us
    ppermute x18, waiting for transfers between devices, send(): return lax.ppermute(cells, 'view', pairs)  44.9 us
    ppermute x18, starting transfers between devices, send(): return lax.ppermute(cells, 'view', pairs)  16.2 us
    unnamed x13, local copies, waits for them, and re-layouts  6.31 us
    pallas_call x1, Pallas kernels, build(): pl.pallas_call(build_kernel, out_shape=[depth, depth] + [square] * 4 + [s...  4.57 us
  transfers between devices with their start and end apart: 18, of which 14 were waited for; matrix products, arithmetic and copies ran while one was open for 2% of the time, Pallas kernels for 49%

commit v1 on v0

--- a/solution.py
+++ b/solution.py
@@ -171,6 +171,29 @@
     return dot(mixed[rows, :], op[...].reshape(ranks * COLS, COLS)).reshape(QUAD, ROWS, COLS)
 
 
+def depth_whole(cells_of, op, planes, spread):
+    ranks = op.shape[0]
+    lhs = op[:, 0 : planes * GROUP, :].reshape(ranks * planes * GROUP, TILE)
+    for g in range(ROWS // GROUP):
+        cells = cells_of(slice(g * GROUP, (g + 1) * GROUP))
+        out = dot(lhs, cells.reshape(TILE, COLS).astype(BF16)).astype(BF16)
+        out = out.reshape(ranks, planes // QUAD, QUAD * GROUP, COLS)
+        spread[:, :, g * QUAD * GROUP : (g + 1) * QUAD * GROUP, :] = out
+
+
+def row_whole(spread, op, mixed, t):
+    for r in range(op.shape[0]):
+        mixed[t * TILE : (t + 1) * TILE, r * COLS : (r + 1) * COLS] = dot(
+            op[r], spread[r, t]
+        ).astype(BF16)
+
+
+def col_whole(mixed, op, t):
+    ranks = op.shape[0]
+    out = dot(mixed[t * TILE : (t + 1) * TILE, :], op[...].reshape(ranks * COLS, COLS))
+    return out.reshape(QUAD, ROWS, COLS)
+
+
 def window(refs, scales=None):
     def read(y):
         parts, left = [], 2 * PLANES
@@ -234,33 +257,42 @@
 def half_update(start, below, own, ratios, shared, ops):
     parts = len(below) + len(own)
     given = parts + len(ratios)
-    tiles = HALF // QUAD
 
     def kernel(*refs):
         slab, ends, depth_f, depth_a, row_f, row_a, col_f, col_a = refs[given : given + 8]
-        ratio, updated, spread, mixed = refs[given + 8 :]
+        ratio, updated, spread, mixed, spread_hi, mixed_hi, spread_lo, mixed_lo = refs[given + 8 :]
         live = ends[0]
         scales = [live] * len(below) + [None] * len(own)
 
         def divide(t):
-            row_pass(spread, row_f, mixed, t)
-            seen = slab[pl.ds(start + t * QUAD, QUAD)].astype(F32)
-            value = seen / col_pass(mixed, col_f, t)
-            ratio[pl.ds(t * QUAD, QUAD)] = value * live if start == 0 else value
-
-        def back(t):
-            row_pass(spread, row_a, mixed, t)
-            planes = pl.ds(t * QUAD, QUAD)
-            updated[planes] = refs[parts - 1][planes] * col_pass(mixed, col_a, t)
-
-        depth_pass(window([(ref, 0) for ref in refs[:parts]], scales), depth_f, HALF, spread)
-        loop(tiles, divide)
-        cells = window([(ref, 0) for ref in (ratio,) + refs[parts:given]])
-        depth_pass(cells, depth_a, HALF, spread)
-        loop(tiles, back)
+            planes = slice(t * QUAD, (t + 1) * QUAD)
+            seen = slab[start + t * QUAD : start + (t + 1) * QUAD].astype(F32)
+            value = seen / col_whole(mixed, col_f, t)
+            ratio[planes] = value * live if start == 0 else value
+
+        def back(t, mixed_t):
+            planes = slice(t * QUAD, (t + 1) * QUAD)
+            updated[planes] = refs[parts - 1][planes] * col_whole(mixed_t, col_a, 0)
+
+        ratio_refs = [(ref, 0) for ref in refs[parts:given]]
+        depth_whole(window([(ref, 0) for ref in refs[:parts]], scales), depth_f, HALF, spread)
+        row_whole(spread, row_f, mixed, 1)
+        divide(1)
+        row_whole(spread, row_f, mixed, 0)
+        depth_whole(window([(ratio, QUAD)] + ratio_refs), depth_a, QUAD, spread_hi)
+        divide(0)
+        row_whole(spread_hi, row_a, mixed_hi, 0)
+        depth_whole(window([(ratio, 0)] + ratio_refs), depth_a, QUAD, spread_lo)
+        back(1, mixed_hi)
+        row_whole(spread_lo, row_a, mixed_lo, 0)
+        back(0, mixed_lo)
 
     ranks = ops[0].shape[0]
-    scratch = [(ranks, tiles, TILE, COLS), (tiles * TILE, ranks * COLS)]
+    scratch = [
+        shape
+        for tiles in (2, 1, 1)
+        for shape in ((ranks, tiles, TILE, COLS), (tiles * TILE, ranks * COLS))
+    ]
     return call(kernel, "half", below + own + ratios, shared, ops, [HALF, HALF], scratch)
 
 

time: 134 us -> 127 us (0.948)
  Pallas kernels: 65.8 us -> 51.3 us
  starting transfers between devices: 16.2 us -> 22.9 us
    pallas_call x12, Pallas kernels: 59.6 us -> 45.2 us  [call(): pl.pallas_call(kernel, out_shape=out, in_specs=[VMEM] * (len(arrays) + le...]
    ppermute x18, starting transfers between devices: 16.2 us -> 22.9 us  [send(): return lax.ppermute(cells, 'view', pairs)]
  transfers between devices with their start and end apart: 18 -> 18, of which waited for: 14 -> 15; matrix products, arithmetic and copies ran while one was open for 2% -> 2% of each run, Pallas kernels for 49% -> 40%
where the time goes in v1:
time: 127 us; the launch traced here: 126 us
  Pallas kernels  51.3 us (40%)
  waiting for transfers between devices  45.3 us (36%)
  starting transfers between devices  22.9 us (18%)
  local copies, waits for them, and re-layouts  6.38 us (5%)
    ppermute x18, waiting for transfers between devices, send(): return lax.ppermute(cells, 'view', pairs)  45.3 us
    pallas_call x12, Pallas kernels, call(): pl.pallas_call(kernel, out_shape=out, in_specs=[VMEM] * (len(arrays) + le...  45.2 us
    ppermute x18, starting transfers between devices, send(): return lax.ppermute(cells, 'view', pairs)  22.9 us
    unnamed x13, local copies, waits for them, and re-layouts  6.31 us
    pallas_call x1, Pallas kernels, build(): pl.pallas_call(build_kernel, out_shape=[depth, depth] + [square] * 4 + [s...  4.57 us
  transfers between devices with their start and end apart: 18, of which 15 were waited for; matrix products, arithmetic and copies ran while one was open for 2% of the time, Pallas kernels for 40%

profile of v1, /device:TPU:28, one launch (start us, length us, event | category | flops | bytes accessed | tf_op | source)
XLA Modules:
  0.0 126.3 jit_solution(16100886517721492871)
XLA Ops:
  0.0 0.7 copy.10.depth_taps
  0.7 0.7 copy.11.row_taps
  1.4 0.7 copy.12.col_taps
  2.2 2.2 %copy-done = bf16[1,4,32,64,256]{4,3,2,1,0:T(8,128)(2,1)S(1)} copy-done((bf16[1,4,32,64,256]{4,3,2,1,0:T(8,128)(2,1)S(1)}, bf16[1,4,32,64,256]{4,3,2,1,0:T(8,128)(2,1)}, u32[]{:S(2)}) %copy-start) | copy-done | bytes 4194328
  4.4 0.7 copy-done.1
  5.1 0.7 copy-done.2
  5.7 0.7 copy-done.3
  6.4 4.6 %build.1 = (bf16[6,128,256]{2,1,0:T(8,128)(2,1)S(1)}, bf16[6,128,256]{2,1,0:T(8,128)(2,1)S(1)}, bf16[6,256,256]{2,1,0:T(8,128)(2,1)S(1)}, bf16[6,256,256]{2,1,0:...) custom-call(s32[2]{0:T(128)S(1)} %pad_add_fusion.place, ...), custom_call_target="tpu_custom_call" | custom-call | tf_op jit(solution)/shard_map/build/pallas_call | solution.py:128
  11.1 2.4 %collective-permute-start = (f32[8,64,256]{2,1,0:T(8,128)S(1)}, f32[8,64,256]{2,1,0:T(8,128)S(1)}, u32[]{:S(2)}, u32[]{:S(2)}) collective-permute-start(f32[8,64,256]{2,1,0:T(8,128)S(1)} %get-tuple-element.35.refs_1_.refs_2_), channel_id=1, source_target_pairs={{0,1},{1,2},{2,3},{3,4},{4,5},{5,6},{6,7},{7,8},{8,9},{9,10},{10,1... | collective-permute-start | bytes 1572872 | tf_op jit(solution)/shard_map/ppermute | solution.py:332
  13.5 3.6 %collective-permute-start.4 = (f32[8,64,256]{2,1,0:T(8,128)S(1)}, f32[8,64,256]{2,1,0:T(8,128)S(1)}, u32[]{:S(2)}, u32[]{:S(2)}) collective-permute-start(f32[8,64,256]{2,1,0:T(8,128)S(1)} %get-tuple-element.44.refs_0_.refs_1_.refs_2_), channel_id=1, source_target_pairs={{0,1},{1,2},{2,3},{3,4},{4,5},{5,6},{6,7},{7,8},{8,9},{9,10},{10,1... | collective-permute-start | bytes 1572872 | tf_op jit(solution)/shard_map/ppermute | solution.py:332
  17.1 4.4 %upper.4.refs_3_.refs_4_ = f32[16,64,256]{2,1,0:T(8,128)S(1)} custom-call(f32[8,64,256]{2,1,0:T(8,128)S(1)} %get-tuple-element.44.refs_0_.refs_1_.refs_2_, f32[8,64,256]{2,1,0:T(8,128)S(1)} %get-tuple-element.35.refs_1_.refs_2_, f32[16,64,256]{2,1,0:T(8,128)S(1)} %collective-permute-done.1.refs_2_, ...), custom_call_target="tpu_custom_call" | custom-call | flops 1048576 | bytes 1024 | tf_op jit(solution)/shard_map/upper/pallas_call | solution.py:218
  21.5 1.3 %collective-permute-done.refs_0_.refs_1_ = f32[8,64,256]{2,1,0:T(8,128)S(1)} collective-permute-done((f32[8,64,256]{2,1,0:T(8,128)S(1)}, f32[8,64,256]{2,1,0:T(8,128)S(1)}, u32[]{:S(2)}, u32[]{:S(2)}) %collective-permute-start) | collective-permute-done | bytes 524320 | tf_op jit(solution)/shard_map/ppermute | solution.py:332
  22.8 3.4 %half.8 = (f32[8,64,256]{2,1,0:T(8,128)S(1)}, f32[8,64,256]{2,1,0:T(8,128)S(1)}) custom-call(f32[8,64,256]{2,1,0:T(8,128)S(1)} %collective-permute-done.refs_0_.refs_1_, f32[8,64,256]{2,1,0:T(8,128)S(1)} %get-tuple-element.44.refs_0_.refs_1_.refs_2_, f32[8,64,256]{2,1,0:T(8,128)S(1)} %get-tuple-element.35.refs_1_.refs_2_, ...), custom_call_target="tpu_custom_call" | custom-call | flops 1048576 | bytes 1024 | tf_op jit(solution)/shard_map/half/pallas_call | solution.py:218
  26.3 2.1 %collective-permute-done.4.refs_0_ = f32[8,64,256]{2,1,0:T(8,128)S(1)} collective-permute-done((f32[8,64,256]{2,1,0:T(8,128)S(1)}, f32[8,64,256]{2,1,0:T(8,128)S(1)}, u32[]{:S(2)}, u32[]{:S(2)}) %collective-permute-start.4) | collective-permute-done | bytes 524320 | tf_op jit(solution)/shard_map/ppermute | solution.py:332
  28.4 3.5 %half.9 = (f32[8,64,256]{2,1,0:T(8,128)}, f32[8,64,256]{2,1,0:T(8,128)S(1)}) custom-call(f32[8,64,256]{2,1,0:T(8,128)S(1)} %collective-permute-done.4.refs_0_, f32[8,64,256]{2,1,0:T(8,128)S(1)} %collective-permute-done.refs_0_.refs_1_, f32[8,64,256]{2,1,0:T(8,128)S(1)} %get-tuple-element.44.refs_0_.refs_1_.refs_2_, ...), custom_call_target="tpu_custom_call" | custom-call | flops 1048576 | bytes 1024 | tf_op jit(solution)/shard_map/half/pallas_call | solution.py:218
  31.9 2.9 %collective-permute-done.2.refs_1_.refs_2_ = f32[8,64,256]{2,1,0:T(8,128)S(1)} collective-permute-done((f32[8,64,256]{2,1,0:T(8,128)S(1)}, f32[8,64,256]{2,1,0:T(8,128)S(1)}, u32[]{:S(2)}, u32[]{:S(2)}) %collective-permute-start.2) | collective-permute-done | bytes 524320 | tf_op jit(solution)/shard_map/ppermute | solution.py:332
  34.9 5.7 %collective-permute-done.5.refs_0_.refs_1_.refs_2_ = f32[8,64,256]{2,1,0:T(8,128)S(1)} collective-permute-done((f32[8,64,256]{2,1,0:T(8,128)S(1)}, f32[8,64,256]{2,1,0:T(8,128)S(1)}, u32[]{:S(2)}, u32[]{:S(2)}) %collective-permute-start.5) | collective-permute-done | bytes 524320 | tf_op jit(solution)/shard_map/ppermute | solution.py:332
  40.5 4.4 %upper.5.refs_3_.refs_4_ = f32[16,64,256]{2,1,0:T(8,128)S(1)} custom-call(f32[8,64,256]{2,1,0:T(8,128)S(1)} %collective-permute-done.5.refs_0_.refs_1_.refs_2_, f32[8,64,256]{2,1,0:T(8,128)S(1)} %collective-permute-done.2.refs_1_.refs_2_, f32[8,64,256]{2,1,0:T(8,128)S(1)} %get-tuple-element.46.refs_2_, f32[8,64,256]{2,1,0:T(8,128)S(1)} %get-tuple-element.43.refs_3_, ...), custom_call_target="tpu_custom_call" | custom-call | flops 1048576 | bytes 1024 | tf_op jit(solution)/shard_map/upper/pallas_call | solution.py:218
  44.9 1.2 collective-permute-done.3.refs_0_.refs_1_
  46.1 3.4 %half.10 = (f32[8,64,256]{2,1,0:T(8,128)S(1)}, f32[8,64,256]{2,1,0:T(8,128)S(1)}) custom-call(f32[8,64,256]{2,1,0:T(8,128)S(1)} %collective-permute-done.3.refs_0_.refs_1_, f32[8,64,256]{2,1,0:T(8,128)S(1)} %collective-permute-done.5.refs_0_.refs_1_.refs_2_, f32[8,64,256]{2,1,0:T(8,128)S(1)} %collective-permute-done.2.refs_1_.refs_2_, ...), custom_call_target="tpu_custom_call" | custom-call | flops 1048576 | bytes 1024 | tf_op jit(solution)/shard_map/half/pallas_call | solution.py:218
  49.5 1.6 %collective-permute-start.6 = (f32[8,64,256]{2,1,0:T(8,128)S(1)}, f32[8,64,256]{2,1,0:T(8,128)S(1)}, u32[]{:S(2)}, u32[]{:S(2)}) collective-permute-start(f32[8,64,256]{2,1,0:T(8,128)S(1)} %get-tuple-element.49.refs_3_), channel_id=1, source_target_pairs={{0,1},{1,2},{2,3},{3,4},{4,5},{5,6},{6,7},{7,8},{8,9},{9,10},{10,1... | collective-permute-start | bytes 1572872 | tf_op jit(solution)/shard_map/ppermute | solution.py:332
  51.1 0.6 collective-permute-done.8.refs_0_
  51.7 3.5 %half.11 = (f32[8,64,256]{2,1,0:T(8,128)}, f32[8,64,256]{2,1,0:T(8,128)S(1)}) custom-call(f32[8,64,256]{2,1,0:T(8,128)S(1)} %collective-permute-done.8.refs_0_, f32[8,64,256]{2,1,0:T(8,128)S(1)} %collective-permute-done.3.refs_0_.refs_1_, f32[8,64,256]{2,1,0:T(8,128)S(1)} %collective-permute-done.5.refs_0_.refs_1_.refs_2_, ...), custom_call_target="tpu_custom_call" | custom-call | flops 1048576 | bytes 1024 | tf_op jit(solution)/shard_map/half/pallas_call | solution.py:218
  55.2 0.6 collective-permute-start.9
  55.8 2.4 %collective-permute-done.6.refs_1_.refs_2_ = f32[8,64,256]{2,1,0:T(8,128)S(1)} collective-permute-done((f32[8,64,256]{2,1,0:T(8,128)S(1)}, f32[8,64,256]{2,1,0:T(8,128)S(1)}, u32[]{:S(2)}, u32[]{:S(2)}) %collective-permute-start.6) | collective-permute-done | bytes 524320 | tf_op jit(solution)/shard_map/ppermute | solution.py:332
  58.4 5.5 %collective-permute-done.9.refs_0_.refs_1_.refs_2_ = f32[8,64,256]{2,1,0:T(8,128)S(1)} collective-permute-done((f32[8,64,256]{2,1,0:T(8,128)S(1)}, f32[8,64,256]{2,1,0:T(8,128)S(1)}, u32[]{:S(2)}, u32[]{:S(2)}) %collective-permute-start.9) | collective-permute-done | bytes 524320 | tf_op jit(solution)/shard_map/ppermute | solution.py:332
  63.9 0.3 collective-permute-start.12
  64.1 4.4 %upper.6.refs_3_.refs_4_ = f32[16,64,256]{2,1,0:T(8,128)S(1)} custom-call(f32[8,64,256]{2,1,0:T(8,128)S(1)} %collective-permute-done.9.refs_0_.refs_1_.refs_2_, f32[8,64,256]{2,1,0:T(8,128)S(1)} %collective-permute-done.6.refs_1_.refs_2_, f32[8,64,256]{2,1,0:T(8,128)S(1)} %get-tuple-element.51.refs_2_, f32[8,64,256]{2,1,0:T(8,128)S(1)} %get-tuple-element.49.refs_3_, ...), custom_call_target="tpu_custom_call" | custom-call | flops 1048576 | bytes 1024 | tf_op jit(solution)/shard_map/upper/pallas_call | solution.py:218
  68.6 0.9 collective-permute-done.7.refs_0_.refs_1_
  69.5 3.4 %half.12 = (f32[8,64,256]{2,1,0:T(8,128)S(1)}, f32[8,64,256]{2,1,0:T(8,128)S(1)}) custom-call(f32[8,64,256]{2,1,0:T(8,128)S(1)} %collective-permute-done.7.refs_0_.refs_1_, f32[8,64,256]{2,1,0:T(8,128)S(1)} %collective-permute-done.9.refs_0_.refs_1_.refs_2_, f32[8,64,256]{2,1,0:T(8,128)S(1)} %collective-permute-done.6.refs_1_.refs_2_, ...), custom_call_target="tpu_custom_call" | custom-call | flops 1048576 | bytes 1024 | tf_op jit(solution)/shard_map/half/pallas_call | solution.py:218
  72.9 4.6 %collective-permute-start.10 = (f32[8,64,256]{2,1,0:T(8,128)S(1)}, f32[8,64,256]{2,1,0:T(8,128)S(1)}, u32[]{:S(2)}, u32[]{:S(2)}) collective-permute-start(f32[8,64,256]{2,1,0:T(8,128)S(1)} %get-tuple-element.54.refs_3_), channel_id=1, source_target_pairs={{0,1},{1,2},{2,3},{3,4},{4,5},{5,6},{6,7},{7,8},{8,9},{9,10},{10,1... | collective-permute-start | bytes 1572872 | tf_op jit(solution)/shard_map/ppermute | solution.py:332
  77.5 3.4 %half.13 = (f32[8,64,256]{2,1,0:T(8,128)}, f32[8,64,256]{2,1,0:T(8,128)S(1)}) custom-call(f32[8,64,256]{2,1,0:T(8,128)S(1)} %collective-permute-done.12.refs_0_, f32[8,64,256]{2,1,0:T(8,128)S(1)} %collective-permute-done.7.refs_0_.refs_1_, f32[8,64,256]{2,1,0:T(8,128)S(1)} %collective-permute-done.9.refs_0_.refs_1_.refs_2_, ...), custom_call_target="tpu_custom_call" | custom-call | flops 1048576 | bytes 1024 | tf_op jit(solution)/shard_map/half/pallas_call | solution.py:218
  80.9 1.2 collective-permute-start.13
  82.2 2.6 %collective-permute-start.11 = (f32[8,64,256]{2,1,0:T(8,128)S(1)}, f32[8,64,256]{2,1,0:T(8,128)S(1)}, u32[]{:S(2)}, u32[]{:S(2)}) collective-permute-start(f32[8,64,256]{2,1,0:T(8,128)S(1)} %collective-permute-done.10.refs_1_.refs_2_), channel_id=1, source_target_pairs={{0,1},{1,2},{2,3},{3,4},{4,5},{5,6},{6,7},{7,8},{8,9},{9,10},{10,1... | collective-permute-start | bytes 1572872 | tf_op jit(solution)/shard_map/ppermute | solution.py:332
  84.8 4.8 %collective-permute-done.13.refs_0_.refs_1_.refs_2_ = f32[8,64,256]{2,1,0:T(8,128)S(1)} collective-permute-done((f32[8,64,256]{2,1,0:T(8,128)S(1)}, f32[8,64,256]{2,1,0:T(8,128)S(1)}, u32[]{:S(2)}, u32[]{:S(2)}) %collective-permute-start.13) | collective-permute-done | bytes 524320 | tf_op jit(solution)/shard_map/ppermute | solution.py:332
  89.6 0.8 collective-permute-start.15
  90.4 4.4 %upper.7.refs_3_.refs_4_ = f32[16,64,256]{2,1,0:T(8,128)S(1)} custom-call(f32[8,64,256]{2,1,0:T(8,128)S(1)} %collective-permute-done.13.refs_0_.refs_1_.refs_2_, f32[8,64,256]{2,1,0:T(8,128)S(1)} %collective-permute-done.10.refs_1_.refs_2_, f32[8,64,256]{2,1,0:T(8,128)S(1)} %get-tuple-element.56.refs_2_, f32[8,64,256]{2,1,0:T(8,128)S(1)} %get-tuple-element.54.refs_3_, ...), custom_call_target="tpu_custom_call" | custom-call | flops 1048576 | bytes 1024 | tf_op jit(solution)/shard_map/upper/pallas_call | solution.py:218
  94.8 0.4 collective-permute-done.11.refs_0_.refs_1_
  95.2 3.4 %half.14 = (f32[8,64,256]{2,1,0:T(8,128)S(1)}, f32[8,64,256]{2,1,0:T(8,128)S(1)}) custom-call(f32[8,64,256]{2,1,0:T(8,128)S(1)} %collective-permute-done.11.refs_0_.refs_1_, f32[8,64,256]{2,1,0:T(8,128)S(1)} %collective-permute-done.13.refs_0_.refs_1_.refs_2_, f32[8,64,256]{2,1,0:T(8,128)S(1)} %collective-permute-done.10.refs_1_.refs_2_, ...), custom_call_target="tpu_custom_call" | custom-call | flops 1048576 | bytes 1024 | tf_op jit(solution)/shard_map/half/pallas_call | solution.py:218
  98.7 1.6 %collective-permute-start.14 = (f32[8,64,256]{2,1,0:T(8,128)S(1)}, f32[8,64,256]{2,1,0:T(8,128)S(1)}, u32[]{:S(2)}, u32[]{:S(2)}) collective-permute-start(f32[8,64,256]{2,1,0:T(8,128)S(1)} %get-tuple-element.59), channel_id=1, source_target_pairs={{0,13},{1,2},{2,15},{3,0},{4,1},{5,6},{6,3},{7,4},{8,5},{9,10},{10... | collective-permute-start | bytes 1572872 | tf_op jit(solution)/shard_map/ppermute | solution.py:332
  100.3 0.6 collective-permute-done.15.refs_0_
  100.8 3.4 %half.15 = (f32[8,64,256]{2,1,0:T(8,128)}, f32[8,64,256]{2,1,0:T(8,128)S(1)}) custom-call(f32[8,64,256]{2,1,0:T(8,128)S(1)} %collective-permute-done.15.refs_0_, f32[8,64,256]{2,1,0:T(8,128)S(1)} %collective-permute-done.11.refs_0_.refs_1_, f32[8,64,256]{2,1,0:T(8,128)S(1)} %collective-permute-done.13.refs_0_.refs_1_.refs_2_, ...), custom_call_target="tpu_custom_call" | custom-call | flops 1048576 | bytes 1024 | tf_op jit(solution)/shard_map/half/pallas_call | solution.py:218
  104.3 3.0 %collective-permute-done.14 = f32[8,64,256]{2,1,0:T(8,128)S(1)} collective-permute-done((f32[8,64,256]{2,1,0:T(8,128)S(1)}, f32[8,64,256]{2,1,0:T(8,128)S(1)}, u32[]{:S(2)}, u32[]{:S(2)}) %collective-permute-start.14) | collective-permute-done | bytes 524320 | tf_op jit(solution)/shard_map/ppermute | solution.py:332
  107.3 3.2 %collective-permute-start.16 = (f32[8,64,256]{2,1,0:T(8,128)S(1)}, f32[8,64,256]{2,1,0:T(8,128)S(1)}, u32[]{:S(2)}, u32[]{:S(2)}) collective-permute-start(f32[8,64,256]{2,1,0:T(8,128)S(1)} %collective-permute-done.14), channel_id=1, source_target_pairs={{0,0},{1,1},{2,14},{3,3},{4,4},{5,5},{6,2},{7,7},{8,8},{9,9},{10,6... | collective-permute-start | bytes 1572872 | tf_op jit(solution)/shard_map/ppermute | solution.py:332
  110.6 10.8 %collective-permute-done.17.refs_0_ = f32[8,64,256]{2,1,0:T(8,128)S(1)} collective-permute-done((f32[8,64,256]{2,1,0:T(8,128)S(1)}, f32[8,64,256]{2,1,0:T(8,128)S(1)}, u32[]{:S(2)}, u32[]{:S(2)}) %collective-permute-start.17) | collective-permute-done | bytes 524320 | tf_op jit(solution)/shard_map/ppermute | solution.py:332
  121.3 0.8 place.2.refs_1_
  122.1 3.2 %collective-permute-done.16.refs_0_ = f32[8,64,256]{2,1,0:T(8,128)S(1)} collective-permute-done((f32[8,64,256]{2,1,0:T(8,128)S(1)}, f32[8,64,256]{2,1,0:T(8,128)S(1)}, u32[]{:S(2)}, u32[]{:S(2)}) %collective-permute-start.16) | collective-permute-done | bytes 524320 | tf_op jit(solution)/shard_map/ppermute | solution.py:332
  125.3 0.8 place.3
  (18 shorter events, 0.5 us)
Async XLA Ops:
  0.0 13.5 %collective-permute-start.1 = (f32[16,64,256]{2,1,0:T(8,128)}, f32[16,64,256]{2,1,0:T(8,128)S(1)}, u32[]{:S(2)}, u32[]{:S(2)}) collective-permute-start(f32[16,64,256]{2,1,0:T(8,128)} %param.9), channel_id=1, source_target_pairs={{0,15},{1,0},{2,1},{3,2},{4,3},{5,4},{6,5},{7,6},{8,7},{9,8},{10,9... | collective-permute-start | bytes 3145736 | tf_op jit(solution)/shard_map/ppermute | solution.py:332
  2.2 2.2 %copy-start = (bf16[1,4,32,64,256]{4,3,2,1,0:T(8,128)(2,1)S(1)}, bf16[1,4,32,64,256]{4,3,2,1,0:T(8,128)(2,1)}, u32[]{:S(2)}) copy-start(bf16[1,4,32,64,256]{4,3,2,1,0:T(8,128)(2,1)} %images.1) | copy-start | bytes 12582916
  4.4 0.7 copy-start.1
  5.1 0.7 copy-start.2
  5.7 0.7 copy-start.3
  6.4 4.6 %copy-start.4 = (f32[16,64,256]{2,1,0:T(8,128)S(1)}, f32[16,64,256]{2,1,0:T(8,128)}, u32[]{:S(2)}) copy-start(f32[16,64,256]{2,1,0:T(8,128)} %param.9) | copy-start | bytes 3145732
  11.1 11.7 %collective-permute-start = (f32[8,64,256]{2,1,0:T(8,128)S(1)}, f32[8,64,256]{2,1,0:T(8,128)S(1)}, u32[]{:S(2)}, u32[]{:S(2)}) collective-permute-start(f32[8,64,256]{2,1,0:T(8,128)S(1)} %get-tuple-element.35.refs_1_.refs_2_), channel_id=1, source_target_pairs={{0,1},{1,2},{2,3},{3,4},{4,5},{5,6},{6,7},{7,8},{8,9},{9,10},{10,1... | collective-permute-start | bytes 1572872 | tf_op jit(solution)/shard_map/ppermute | solution.py:332
  13.5 14.9 %collective-permute-start.4 = (f32[8,64,256]{2,1,0:T(8,128)S(1)}, f32[8,64,256]{2,1,0:T(8,128)S(1)}, u32[]{:S(2)}, u32[]{:S(2)}) collective-permute-start(f32[8,64,256]{2,1,0:T(8,128)S(1)} %get-tuple-element.44.refs_0_.refs_1_.refs_2_), channel_id=1, source_target_pairs={{0,1},{1,2},{2,3},{3,4},{4,5},{5,6},{6,7},{7,8},{8,9},{9,10},{10,1... | collective-permute-start | bytes 1572872 | tf_op jit(solution)/shard_map/ppermute | solution.py:332
  26.2 8.7 %collective-permute-start.2 = (f32[8,64,256]{2,1,0:T(8,128)S(1)}, f32[8,64,256]{2,1,0:T(8,128)S(1)}, u32[]{:S(2)}, u32[]{:S(2)}) collective-permute-start(f32[8,64,256]{2,1,0:T(8,128)S(1)} %get-tuple-element.43.refs_3_), channel_id=1, source_target_pairs={{0,1},{1,2},{2,3},{3,4},{4,5},{5,6},{6,7},{7,8},{8,9},{9,10},{10,1... | collective-permute-start | bytes 1572872 | tf_op jit(solution)/shard_map/ppermute | solution.py:332
  31.8 8.7 %collective-permute-start.5 = (f32[8,64,256]{2,1,0:T(8,128)S(1)}, f32[8,64,256]{2,1,0:T(8,128)S(1)}, u32[]{:S(2)}, u32[]{:S(2)}) collective-permute-start(f32[8,64,256]{2,1,0:T(8,128)S(1)} %get-tuple-element.46.refs_2_), channel_id=1, source_target_pairs={{0,1},{1,2},{2,3},{3,4},{4,5},{5,6},{6,7},{7,8},{8,9},{9,10},{10,1... | collective-permute-start | bytes 1572872 | tf_op jit(solution)/shard_map/ppermute | solution.py:332
  34.8 11.3 %collective-permute-start.3 = (f32[8,64,256]{2,1,0:T(8,128)S(1)}, f32[8,64,256]{2,1,0:T(8,128)S(1)}, u32[]{:S(2)}, u32[]{:S(2)}) collective-permute-start(f32[8,64,256]{2,1,0:T(8,128)S(1)} %collective-permute-done.2.refs_1_.refs_2_), channel_id=1, source_target_pairs={{0,1},{1,2},{2,3},{3,4},{4,5},{5,6},{6,7},{7,8},{8,9},{9,10},{10,1... | collective-permute-start | bytes 1572872 | tf_op jit(solution)/shard_map/ppermute | solution.py:332
  40.5 11.2 %collective-permute-start.8 = (f32[8,64,256]{2,1,0:T(8,128)S(1)}, f32[8,64,256]{2,1,0:T(8,128)S(1)}, u32[]{:S(2)}, u32[]{:S(2)}) collective-permute-start(f32[8,64,256]{2,1,0:T(8,128)S(1)} %collective-permute-done.5.refs_0_.refs_1_.refs_2_), channel_id=1, source_target_pairs={{0,1},{1,2},{2,3},{3,4},{4,5},{5,6},{6,7},{7,8},{8,9},{9,10},{10,1... | collective-permute-start | bytes 1572872 | tf_op jit(solution)/shard_map/ppermute | solution.py:332
  49.5 8.7 %collective-permute-start.6 = (f32[8,64,256]{2,1,0:T(8,128)S(1)}, f32[8,64,256]{2,1,0:T(8,128)S(1)}, u32[]{:S(2)}, u32[]{:S(2)}) collective-permute-start(f32[8,64,256]{2,1,0:T(8,128)S(1)} %get-tuple-element.49.refs_3_), channel_id=1, source_target_pairs={{0,1},{1,2},{2,3},{3,4},{4,5},{5,6},{6,7},{7,8},{8,9},{9,10},{10,1... | collective-permute-start | bytes 1572872 | tf_op jit(solution)/shard_map/ppermute | solution.py:332
  55.2 8.7 %collective-permute-start.9 = (f32[8,64,256]{2,1,0:T(8,128)S(1)}, f32[8,64,256]{2,1,0:T(8,128)S(1)}, u32[]{:S(2)}, u32[]{:S(2)}) collective-permute-start(f32[8,64,256]{2,1,0:T(8,128)S(1)} %get-tuple-element.51.refs_2_), channel_id=1, source_target_pairs={{0,1},{1,2},{2,3},{3,4},{4,5},{5,6},{6,7},{7,8},{8,9},{9,10},{10,1... | collective-permute-start | bytes 1572872 | tf_op jit(solution)/shard_map/ppermute | solution.py:332
  58.2 11.3 %collective-permute-start.7 = (f32[8,64,256]{2,1,0:T(8,128)S(1)}, f32[8,64,256]{2,1,0:T(8,128)S(1)}, u32[]{:S(2)}, u32[]{:S(2)}) collective-permute-start(f32[8,64,256]{2,1,0:T(8,128)S(1)} %collective-permute-done.6.refs_1_.refs_2_), channel_id=1, source_target_pairs={{0,1},{1,2},{2,3},{3,4},{4,5},{5,6},{6,7},{7,8},{8,9},{9,10},{10,1... | collective-permute-start | bytes 1572872 | tf_op jit(solution)/shard_map/ppermute | solution.py:332
  63.9 13.6 %collective-permute-start.12 = (f32[8,64,256]{2,1,0:T(8,128)S(1)}, f32[8,64,256]{2,1,0:T(8,128)S(1)}, u32[]{:S(2)}, u32[]{:S(2)}) collective-permute-start(f32[8,64,256]{2,1,0:T(8,128)S(1)} %collective-permute-done.9.refs_0_.refs_1_.refs_2_), channel_id=1, source_target_pairs={{0,1},{1,2},{2,3},{3,4},{4,5},{5,6},{6,7},{7,8},{8,9},{9,10},{10,1... | collective-permute-start | bytes 1572872 | tf_op jit(solution)/shard_map/ppermute | solution.py:332
  72.9 9.2 %collective-permute-start.10 = (f32[8,64,256]{2,1,0:T(8,128)S(1)}, f32[8,64,256]{2,1,0:T(8,128)S(1)}, u32[]{:S(2)}, u32[]{:S(2)}) collective-permute-start(f32[8,64,256]{2,1,0:T(8,128)S(1)} %get-tuple-element.54.refs_3_), channel_id=1, source_target_pairs={{0,1},{1,2},{2,3},{3,4},{4,5},{5,6},{6,7},{7,8},{8,9},{9,10},{10,1... | collective-permute-start | bytes 1572872 | tf_op jit(solution)/shard_map/ppermute | solution.py:332
  80.9 8.7 %collective-permute-start.13 = (f32[8,64,256]{2,1,0:T(8,128)S(1)}, f32[8,64,256]{2,1,0:T(8,128)S(1)}, u32[]{:S(2)}, u32[]{:S(2)}) collective-permute-start(f32[8,64,256]{2,1,0:T(8,128)S(1)} %get-tuple-element.56.refs_2_), channel_id=1, source_target_pairs={{0,1},{1,2},{2,3},{3,4},{4,5},{5,6},{6,7},{7,8},{8,9},{9,10},{10,1... | collective-permute-start | bytes 1572872 | tf_op jit(solution)/shard_map/ppermute | solution.py:332
  82.2 13.1 %collective-permute-start.11 = (f32[8,64,256]{2,1,0:T(8,128)S(1)}, f32[8,64,256]{2,1,0:T(8,128)S(1)}, u32[]{:S(2)}, u32[]{:S(2)}) collective-permute-start(f32[8,64,256]{2,1,0:T(8,128)S(1)} %collective-permute-done.10.refs_1_.refs_2_), channel_id=1, source_target_pairs={{0,1},{1,2},{2,3},{3,4},{4,5},{5,6},{6,7},{7,8},{8,9},{9,10},{10,1... | collective-permute-start | bytes 1572872 | tf_op jit(solution)/shard_map/ppermute | solution.py:332
  89.6 11.2 %collective-permute-start.15 = (f32[8,64,256]{2,1,0:T(8,128)S(1)}, f32[8,64,256]{2,1,0:T(8,128)S(1)}, u32[]{:S(2)}, u32[]{:S(2)}) collective-permute-start(f32[8,64,256]{2,1,0:T(8,128)S(1)} %collective-permute-done.13.refs_0_.refs_1_.refs_2_), channel_id=1, source_target_pairs={{0,1},{1,2},{2,3},{3,4},{4,5},{5,6},{6,7},{7,8},{8,9},{9,10},{10,1... | collective-permute-start | bytes 1572872 | tf_op jit(solution)/shard_map/ppermute | solution.py:332
  98.7 8.7 %collective-permute-start.14 = (f32[8,64,256]{2,1,0:T(8,128)S(1)}, f32[8,64,256]{2,1,0:T(8,128)S(1)}, u32[]{:S(2)}, u32[]{:S(2)}) collective-permute-start(f32[8,64,256]{2,1,0:T(8,128)S(1)} %get-tuple-element.59), channel_id=1, source_target_pairs={{0,13},{1,2},{2,15},{3,0},{4,1},{5,6},{6,3},{7,4},{8,5},{9,10},{10... | collective-permute-start | bytes 1572872 | tf_op jit(solution)/shard_map/ppermute | solution.py:332
  104.3 17.0 %collective-permute-start.17 = (f32[8,64,256]{2,1,0:T(8,128)S(1)}, f32[8,64,256]{2,1,0:T(8,128)S(1)}, u32[]{:S(2)}, u32[]{:S(2)}) collective-permute-start(f32[8,64,256]{2,1,0:T(8,128)S(1)} %get-tuple-element.61), channel_id=1, source_target_pairs={{0,13},{1,14},{2,15},{3,0},{4,1},{5,2},{6,3},{7,4},{8,5},{9,6},{10... | collective-permute-start | bytes 1572872 | tf_op jit(solution)/shard_map/ppermute | solution.py:332
  107.3 18.0 %collective-permute-start.16 = (f32[8,64,256]{2,1,0:T(8,128)S(1)}, f32[8,64,256]{2,1,0:T(8,128)S(1)}, u32[]{:S(2)}, u32[]{:S(2)}) collective-permute-start(f32[8,64,256]{2,1,0:T(8,128)S(1)} %collective-permute-done.14), channel_id=1, source_target_pairs={{0,0},{1,1},{2,14},{3,3},{4,4},{5,5},{6,2},{7,7},{8,8},{9,9},{10,6... | collective-permute-start | bytes 1572872 | tf_op jit(solution)/shard_map/ppermute | solution.py:332

commit v2 on v1

--- a/solution.py
+++ b/solution.py
@@ -296,26 +296,27 @@
     return call(kernel, "half", below + own + ratios, shared, ops, [HALF, HALF], scratch)
 
 
-def placed_half(half, start, whole=None):
-    extra = [] if whole is None else [whole]
-
-    def kernel(*refs):
-        half, out, sem = refs[0], refs[-2], refs[-1]
-        copy = pltpu.make_async_copy(half, out.at[pl.ds(start, HALF)], sem)
-        copy.start()
-        copy.wait()
+def whole(lo, hi):
+    def kernel(lo, hi, out, sems):
+        copies = [
+            pltpu.make_async_copy(half, out.at[pl.ds(i * HALF, HALF)], sems.at[i])
+            for i, half in enumerate((lo, hi))
+        ]
+        for copy in copies:
+            copy.start()
+        for copy in copies:
+            copy.wait()
 
     return pl.pallas_call(
         kernel,
         out_shape=jax.ShapeDtypeStruct((PLANES, ROWS, COLS), F32),
-        in_specs=[VMEM] + [HBM] * len(extra),
+        in_specs=[VMEM] * 2,
         out_specs=HBM,
-        scratch_shapes=[pltpu.SemaphoreType.DMA],
-        input_output_aliases={1: 0} if extra else {},
+        scratch_shapes=[pltpu.SemaphoreType.DMA((2,))],
         compiler_params=pltpu.CompilerParams(vmem_limit_bytes=20 * 2**20),
         cost_estimate=COST,
-        name="place",
-    )(half, *extra)
+        name="whole",
+    )(lo, hi)
 
 
 def shards(
@@ -340,7 +341,7 @@
     early_hi, _ = lax.optimization_barrier((own_hi, ops[0]))
     below_hi = send(early_hi, 1, skip=(count - 1,))
     early_lo, _ = lax.optimization_barrier((own_lo, above[0]))
-    below_lo = send(early_lo, 1)
+    below_lo = send(early_lo, 1, skip=(count - 1,))
 
     for step in range(STEPS):
         last = step == STEPS - 1
@@ -360,7 +361,7 @@
             own_lo, own_hi = send(lo, 1), next_hi
             below_hi = send(own_hi, 1)
             below_lo = send(own_lo, 1)
-    return placed_half(own_hi, HALF, placed_half(own_lo, 0))
+    return whole(own_lo, own_hi)
 
 
 def solution(mesh):

time: 127 us -> 127 us (level)
  transfers between devices with their start and end apart: 18 -> 18, of which waited for: 15 -> 15; matrix products, arithmetic and copies ran while one was open for 2% -> 2% of each run, Pallas kernels for 40% -> 39%
where the time goes in v2:
time: 127 us
  Pallas kernels  50.7 us (40%)
  waiting for transfers between devices  46.5 us (37%)
  starting transfers between devices  22.4 us (18%)
  local copies, waits for them, and re-layouts  6.38 us (5%)
    ppermute x18, waiting for transfers between devices, send(): return lax.ppermute(cells, 'view', pairs)  46.5 us
    pallas_call x12, Pallas kernels, call(): pl.pallas_call(kernel, out_shape=out, in_specs=[VMEM] * (len(arrays) + le...  45.2 us
    ppermute x18, starting transfers between devices, send(): return lax.ppermute(cells, 'view', pairs)  22.4 us
    unnamed x13, local copies, waits for them, and re-layouts  6.31 us
    pallas_call x1, Pallas kernels, build(): pl.pallas_call(build_kernel, out_shape=[depth, depth] + [square] * 4 + [s...  4.57 us
  transfers between devices with their start and end apart: 18, of which 15 were waited for; matrix products, arithmetic and copies ran while one was open for 2% of the time, Pallas kernels for 39%

profile of v2, /device:TPU:28, one launch (start us, length us, event | category | flops | bytes accessed | tf_op | source)
XLA Modules:
  0.0 126.5 jit_solution(4084271403801730000)
XLA Ops:
  0.0 0.7 copy.9.depth_taps
  0.7 0.7 copy.10.row_taps
  1.4 0.7 copy.11.col_taps
  2.1 0.1 pad_add_fusion.place
  2.2 2.2 %copy-done = bf16[1,4,32,64,256]{4,3,2,1,0:T(8,128)(2,1)S(1)} copy-done((bf16[1,4,32,64,256]{4,3,2,1,0:T(8,128)(2,1)S(1)}, bf16[1,4,32,64,256]{4,3,2,1,0:T(8,128)(2,1)}, u32[]{:S(2)}) %copy-start) | copy-done | bytes 4194328
  4.4 0.7 copy-done.1
  5.1 0.7 copy-done.2
  5.7 0.7 copy-done.3
  6.4 4.6 %build.1 = (bf16[6,128,256]{2,1,0:T(8,128)(2,1)S(1)}, bf16[6,128,256]{2,1,0:T(8,128)(2,1)S(1)}, bf16[6,256,256]{2,1,0:T(8,128)(2,1)S(1)}, bf16[6,256,256]{2,1,0:...) custom-call(s32[2]{0:T(128)S(1)} %pad_add_fusion.place, ...), custom_call_target="tpu_custom_call" | custom-call | tf_op jit(solution)/shard_map/build/pallas_call | solution.py:128
  11.0 0.1 fusion
  11.1 2.4 %collective-permute-start.2 = (f32[8,64,256]{2,1,0:T(8,128)S(1)}, f32[8,64,256]{2,1,0:T(8,128)S(1)}, u32[]{:S(2)}, u32[]{:S(2)}) collective-permute-start(f32[8,64,256]{2,1,0:T(8,128)S(1)} %get-tuple-element.36.refs_1_.refs_2_), channel_id=1, source_target_pairs={{0,1},{1,2},{2,3},{3,4},{4,5},{5,6},{6,7},{7,8},{8,9},{9,10},{10,1... | collective-permute-start | bytes 1572872 | tf_op jit(solution)/shard_map/ppermute | solution.py:333
  13.5 5.5 %collective-permute-start.1 = (f32[8,64,256]{2,1,0:T(8,128)S(1)}, f32[8,64,256]{2,1,0:T(8,128)S(1)}, u32[]{:S(2)}, u32[]{:S(2)}) collective-permute-start(f32[8,64,256]{2,1,0:T(8,128)S(1)} %get-tuple-element.34.refs_0_.refs_1_.refs_2_), channel_id=1, source_target_pairs={{0,1},{1,2},{2,3},{3,4},{4,5},{5,6},{6,7},{7,8},{8,9},{9,10},{10,1... | collective-permute-start | bytes 1572872 | tf_op jit(solution)/shard_map/ppermute | solution.py:333
  19.0 4.4 %upper.4.refs_3_.refs_4_ = f32[16,64,256]{2,1,0:T(8,128)S(1)} custom-call(f32[8,64,256]{2,1,0:T(8,128)S(1)} %get-tuple-element.34.refs_0_.refs_1_.refs_2_, f32[8,64,256]{2,1,0:T(8,128)S(1)} %get-tuple-element.36.refs_1_.refs_2_, f32[16,64,256]{2,1,0:T(8,128)S(1)} %collective-permute-done.refs_2_, ...), custom_call_target="tpu_custom_call" | custom-call | flops 1048576 | bytes 1024 | tf_op jit(solution)/shard_map/upper/pallas_call | solution.py:218
  23.4 3.4 %half.8 = (f32[8,64,256]{2,1,0:T(8,128)S(1)}, f32[8,64,256]{2,1,0:T(8,128)S(1)}) custom-call(f32[8,64,256]{2,1,0:T(8,128)S(1)} %collective-permute-done.2.refs_0_.refs_1_, f32[8,64,256]{2,1,0:T(8,128)S(1)} %get-tuple-element.34.refs_0_.refs_1_.refs_2_, f32[8,64,256]{2,1,0:T(8,128)S(1)} %get-tuple-element.36.refs_1_.refs_2_, ...), custom_call_target="tpu_custom_call" | custom-call | flops 1048576 | bytes 1024 | tf_op jit(solution)/shard_map/half/pallas_call | solution.py:218
  26.9 1.5 %collective-permute-done.1.refs_0_ = f32[8,64,256]{2,1,0:T(8,128)S(1)} collective-permute-done((f32[8,64,256]{2,1,0:T(8,128)S(1)}, f32[8,64,256]{2,1,0:T(8,128)S(1)}, u32[]{:S(2)}, u32[]{:S(2)}) %collective-permute-start.1) | collective-permute-done | bytes 524320 | tf_op jit(solution)/shard_map/ppermute | solution.py:333
  28.4 3.5 %half.9 = (f32[8,64,256]{2,1,0:T(8,128)}, f32[8,64,256]{2,1,0:T(8,128)S(1)}) custom-call(f32[8,64,256]{2,1,0:T(8,128)S(1)} %collective-permute-done.1.refs_0_, f32[8,64,256]{2,1,0:T(8,128)S(1)} %collective-permute-done.2.refs_0_.refs_1_, f32[8,64,256]{2,1,0:T(8,128)S(1)} %get-tuple-element.34.refs_0_.refs_1_.refs_2_, ...), custom_call_target="tpu_custom_call" | custom-call | flops 1048576 | bytes 1024 | tf_op jit(solution)/shard_map/half/pallas_call | solution.py:218
  31.9 3.6 %collective-permute-done.5.refs_1_.refs_2_ = f32[8,64,256]{2,1,0:T(8,128)S(1)} collective-permute-done((f32[8,64,256]{2,1,0:T(8,128)S(1)}, f32[8,64,256]{2,1,0:T(8,128)S(1)}, u32[]{:S(2)}, u32[]{:S(2)}) %collective-permute-start.5) | collective-permute-done | bytes 524320 | tf_op jit(solution)/shard_map/ppermute | solution.py:333
  35.5 5.6 %collective-permute-done.3.refs_0_.refs_1_.refs_2_ = f32[8,64,256]{2,1,0:T(8,128)S(1)} collective-permute-done((f32[8,64,256]{2,1,0:T(8,128)S(1)}, f32[8,64,256]{2,1,0:T(8,128)S(1)}, u32[]{:S(2)}, u32[]{:S(2)}) %collective-permute-start.3) | collective-permute-done | bytes 524320 | tf_op jit(solution)/shard_map/ppermute | solution.py:333
  41.1 4.4 %upper.5.refs_3_.refs_4_ = f32[16,64,256]{2,1,0:T(8,128)S(1)} custom-call(f32[8,64,256]{2,1,0:T(8,128)S(1)} %collective-permute-done.3.refs_0_.refs_1_.refs_2_, f32[8,64,256]{2,1,0:T(8,128)S(1)} %collective-permute-done.5.refs_1_.refs_2_, f32[8,64,256]{2,1,0:T(8,128)S(1)} %get-tuple-element.45.refs_2_, f32[8,64,256]{2,1,0:T(8,128)S(1)} %get-tuple-element.46.refs_3_, ...), custom_call_target="tpu_custom_call" | custom-call | flops 1048576 | bytes 1024 | tf_op jit(solution)/shard_map/upper/pallas_call | solution.py:218
  45.6 1.2 collective-permute-done.6.refs_0_.refs_1_
  46.7 3.4 %half.10 = (f32[8,64,256]{2,1,0:T(8,128)S(1)}, f32[8,64,256]{2,1,0:T(8,128)S(1)}) custom-call(f32[8,64,256]{2,1,0:T(8,128)S(1)} %collective-permute-done.6.refs_0_.refs_1_, f32[8,64,256]{2,1,0:T(8,128)S(1)} %collective-permute-done.3.refs_0_.refs_1_.refs_2_, f32[8,64,256]{2,1,0:T(8,128)S(1)} %collective-permute-done.5.refs_1_.refs_2_, ...), custom_call_target="tpu_custom_call" | custom-call | flops 1048576 | bytes 1024 | tf_op jit(solution)/shard_map/half/pallas_call | solution.py:218
  50.2 1.0 collective-permute-start.9
  51.1 1.2 collective-permute-done.4.refs_0_
  52.4 3.5 %half.11 = (f32[8,64,256]{2,1,0:T(8,128)}, f32[8,64,256]{2,1,0:T(8,128)S(1)}) custom-call(f32[8,64,256]{2,1,0:T(8,128)S(1)} %collective-permute-done.4.refs_0_, f32[8,64,256]{2,1,0:T(8,128)S(1)} %collective-permute-done.6.refs_0_.refs_1_, f32[8,64,256]{2,1,0:T(8,128)S(1)} %collective-permute-done.3.refs_0_.refs_1_.refs_2_, ...), custom_call_target="tpu_custom_call" | custom-call | flops 1048576 | bytes 1024 | tf_op jit(solution)/shard_map/half/pallas_call | solution.py:218
  55.8 0.1 collective-permute-start.7
  55.9 2.9 %collective-permute-done.9.refs_1_.refs_2_ = f32[8,64,256]{2,1,0:T(8,128)S(1)} collective-permute-done((f32[8,64,256]{2,1,0:T(8,128)S(1)}, f32[8,64,256]{2,1,0:T(8,128)S(1)}, u32[]{:S(2)}, u32[]{:S(2)}) %collective-permute-start.9) | collective-permute-done | bytes 524320 | tf_op jit(solution)/shard_map/ppermute | solution.py:333
  58.8 5.7 %collective-permute-done.7.refs_0_.refs_1_.refs_2_ = f32[8,64,256]{2,1,0:T(8,128)S(1)} collective-permute-done((f32[8,64,256]{2,1,0:T(8,128)S(1)}, f32[8,64,256]{2,1,0:T(8,128)S(1)}, u32[]{:S(2)}, u32[]{:S(2)}) %collective-permute-start.7) | collective-permute-done | bytes 524320 | tf_op jit(solution)/shard_map/ppermute | solution.py:333
  64.5 4.4 %upper.6.refs_3_.refs_4_ = f32[16,64,256]{2,1,0:T(8,128)S(1)} custom-call(f32[8,64,256]{2,1,0:T(8,128)S(1)} %collective-permute-done.7.refs_0_.refs_1_.refs_2_, f32[8,64,256]{2,1,0:T(8,128)S(1)} %collective-permute-done.9.refs_1_.refs_2_, f32[8,64,256]{2,1,0:T(8,128)S(1)} %get-tuple-element.50.refs_2_, f32[8,64,256]{2,1,0:T(8,128)S(1)} %get-tuple-element.51.refs_3_, ...), custom_call_target="tpu_custom_call" | custom-call | flops 1048576 | bytes 1024 | tf_op jit(solution)/shard_map/upper/pallas_call | solution.py:218
  68.9 1.2 collective-permute-done.10.refs_0_.refs_1_
  70.1 3.4 %half.12 = (f32[8,64,256]{2,1,0:T(8,128)S(1)}, f32[8,64,256]{2,1,0:T(8,128)S(1)}) custom-call(f32[8,64,256]{2,1,0:T(8,128)S(1)} %collective-permute-done.10.refs_0_.refs_1_, f32[8,64,256]{2,1,0:T(8,128)S(1)} %collective-permute-done.7.refs_0_.refs_1_.refs_2_, f32[8,64,256]{2,1,0:T(8,128)S(1)} %collective-permute-done.9.refs_1_.refs_2_, ...), custom_call_target="tpu_custom_call" | custom-call | flops 1048576 | bytes 1024 | tf_op jit(solution)/shard_map/half/pallas_call | solution.py:218
  73.5 3.9 %collective-permute-start.13 = (f32[8,64,256]{2,1,0:T(8,128)S(1)}, f32[8,64,256]{2,1,0:T(8,128)S(1)}, u32[]{:S(2)}, u32[]{:S(2)}) collective-permute-start(f32[8,64,256]{2,1,0:T(8,128)S(1)} %get-tuple-element.56.refs_3_), channel_id=1, source_target_pairs={{0,1},{1,2},{2,3},{3,4},{4,5},{5,6},{6,7},{7,8},{8,9},{9,10},{10,1... | collective-permute-start | bytes 1572872 | tf_op jit(solution)/shard_map/ppermute | solution.py:333
  77.5 3.4 %half.13 = (f32[8,64,256]{2,1,0:T(8,128)}, f32[8,64,256]{2,1,0:T(8,128)S(1)}) custom-call(f32[8,64,256]{2,1,0:T(8,128)S(1)} %collective-permute-done.8.refs_0_, f32[8,64,256]{2,1,0:T(8,128)S(1)} %collective-permute-done.10.refs_0_.refs_1_, f32[8,64,256]{2,1,0:T(8,128)S(1)} %collective-permute-done.7.refs_0_.refs_1_.refs_2_, ...), custom_call_target="tpu_custom_call" | custom-call | flops 1048576 | bytes 1024 | tf_op jit(solution)/shard_map/half/pallas_call | solution.py:218
  80.9 1.3 collective-permute-start.11
  82.2 0.2 collective-permute-done.13.refs_1_.refs_2_
  82.4 2.4 %collective-permute-start.14 = (f32[8,64,256]{2,1,0:T(8,128)S(1)}, f32[8,64,256]{2,1,0:T(8,128)S(1)}, u32[]{:S(2)}, u32[]{:S(2)}) collective-permute-start(f32[8,64,256]{2,1,0:T(8,128)S(1)} %collective-permute-done.13.refs_1_.refs_2_), channel_id=1, source_target_pairs={{0,1},{1,2},{2,3},{3,4},{4,5},{5,6},{6,7},{7,8},{8,9},{9,10},{10,1... | collective-permute-start | bytes 1572872 | tf_op jit(solution)/shard_map/ppermute | solution.py:333
  84.8 4.8 %collective-permute-done.11.refs_0_.refs_1_.refs_2_ = f32[8,64,256]{2,1,0:T(8,128)S(1)} collective-permute-done((f32[8,64,256]{2,1,0:T(8,128)S(1)}, f32[8,64,256]{2,1,0:T(8,128)S(1)}, u32[]{:S(2)}, u32[]{:S(2)}) %collective-permute-start.11) | collective-permute-done | bytes 524320 | tf_op jit(solution)/shard_map/ppermute | solution.py:333
  89.6 0.8 collective-permute-start.12
  90.4 4.4 %upper.7.refs_3_.refs_4_ = f32[16,64,256]{2,1,0:T(8,128)S(1)} custom-call(f32[8,64,256]{2,1,0:T(8,128)S(1)} %collective-permute-done.11.refs_0_.refs_1_.refs_2_, f32[8,64,256]{2,1,0:T(8,128)S(1)} %collective-permute-done.13.refs_1_.refs_2_, f32[8,64,256]{2,1,0:T(8,128)S(1)} %get-tuple-element.55.refs_2_, f32[8,64,256]{2,1,0:T(8,128)S(1)} %get-tuple-element.56.refs_3_, ...), custom_call_target="tpu_custom_call" | custom-call | flops 1048576 | bytes 1024 | tf_op jit(solution)/shard_map/upper/pallas_call | solution.py:218
  94.9 0.4 collective-permute-done.14.refs_0_.refs_1_
  95.2 3.4 %half.14 = (f32[8,64,256]{2,1,0:T(8,128)S(1)}, f32[8,64,256]{2,1,0:T(8,128)S(1)}) custom-call(f32[8,64,256]{2,1,0:T(8,128)S(1)} %collective-permute-done.14.refs_0_.refs_1_, f32[8,64,256]{2,1,0:T(8,128)S(1)} %collective-permute-done.11.refs_0_.refs_1_.refs_2_, f32[8,64,256]{2,1,0:T(8,128)S(1)} %collective-permute-done.13.refs_1_.refs_2_, ...), custom_call_target="tpu_custom_call" | custom-call | flops 1048576 | bytes 1024 | tf_op jit(solution)/shard_map/half/pallas_call | solution.py:218
  98.7 1.6 %collective-permute-start.16 = (f32[8,64,256]{2,1,0:T(8,128)S(1)}, f32[8,64,256]{2,1,0:T(8,128)S(1)}, u32[]{:S(2)}, u32[]{:S(2)}) collective-permute-start(f32[8,64,256]{2,1,0:T(8,128)S(1)} %get-tuple-element.61), channel_id=1, source_target_pairs={{0,13},{1,2},{2,15},{3,0},{4,1},{5,6},{6,3},{7,4},{8,5},{9,10},{10... | collective-permute-start | bytes 1572872 | tf_op jit(solution)/shard_map/ppermute | solution.py:333
  100.3 0.6 collective-permute-done.12.refs_0_
  100.8 3.4 %half.15 = (f32[8,64,256]{2,1,0:T(8,128)}, f32[8,64,256]{2,1,0:T(8,128)S(1)}) custom-call(f32[8,64,256]{2,1,0:T(8,128)S(1)} %collective-permute-done.12.refs_0_, f32[8,64,256]{2,1,0:T(8,128)S(1)} %collective-permute-done.14.refs_0_.refs_1_, f32[8,64,256]{2,1,0:T(8,128)S(1)} %collective-permute-done.11.refs_0_.refs_1_.refs_2_, ...), custom_call_target="tpu_custom_call" | custom-call | flops 1048576 | bytes 1024 | tf_op jit(solution)/shard_map/half/pallas_call | solution.py:218
  104.3 3.0 %collective-permute-done.16 = f32[8,64,256]{2,1,0:T(8,128)S(1)} collective-permute-done((f32[8,64,256]{2,1,0:T(8,128)S(1)}, f32[8,64,256]{2,1,0:T(8,128)S(1)}, u32[]{:S(2)}, u32[]{:S(2)}) %collective-permute-start.16) | collective-permute-done | bytes 524320 | tf_op jit(solution)/shard_map/ppermute | solution.py:333
  107.3 3.3 %collective-permute-start.17 = (f32[8,64,256]{2,1,0:T(8,128)S(1)}, f32[8,64,256]{2,1,0:T(8,128)S(1)}, u32[]{:S(2)}, u32[]{:S(2)}) collective-permute-start(f32[8,64,256]{2,1,0:T(8,128)S(1)} %collective-permute-done.16), channel_id=1, source_target_pairs={{0,0},{1,1},{2,14},{3,3},{4,4},{5,5},{6,2},{7,7},{8,8},{9,9},{10,6... | collective-permute-start | bytes 1572872 | tf_op jit(solution)/shard_map/ppermute | solution.py:333
  110.6 10.7 %collective-permute-done.15.lo = f32[8,64,256]{2,1,0:T(8,128)S(1)} collective-permute-done((f32[8,64,256]{2,1,0:T(8,128)S(1)}, f32[8,64,256]{2,1,0:T(8,128)S(1)}, u32[]{:S(2)}, u32[]{:S(2)}) %collective-permute-start.15) | collective-permute-done | bytes 524320 | tf_op jit(solution)/shard_map/ppermute | solution.py:333
  121.3 4.0 %collective-permute-done.17.hi = f32[8,64,256]{2,1,0:T(8,128)S(1)} collective-permute-done((f32[8,64,256]{2,1,0:T(8,128)S(1)}, f32[8,64,256]{2,1,0:T(8,128)S(1)}, u32[]{:S(2)}, u32[]{:S(2)}) %collective-permute-start.17) | collective-permute-done | bytes 524320 | tf_op jit(solution)/shard_map/ppermute | solution.py:333
  125.4 1.0 whole.1
  (17 shorter events, 0.2 us)
Async XLA Ops:
  0.0 13.5 %collective-permute-start = (f32[16,64,256]{2,1,0:T(8,128)}, f32[16,64,256]{2,1,0:T(8,128)S(1)}, u32[]{:S(2)}, u32[]{:S(2)}) collective-permute-start(f32[16,64,256]{2,1,0:T(8,128)} %param.9), channel_id=1, source_target_pairs={{0,15},{1,0},{2,1},{3,2},{4,3},{5,4},{6,5},{7,6},{8,7},{9,8},{10,9... | collective-permute-start | bytes 3145736 | tf_op jit(solution)/shard_map/ppermute | solution.py:333
  2.2 2.2 %copy-start = (bf16[1,4,32,64,256]{4,3,2,1,0:T(8,128)(2,1)S(1)}, bf16[1,4,32,64,256]{4,3,2,1,0:T(8,128)(2,1)}, u32[]{:S(2)}) copy-start(bf16[1,4,32,64,256]{4,3,2,1,0:T(8,128)(2,1)} %images.1) | copy-start | bytes 12582916
  4.4 0.7 copy-start.1
  5.1 0.7 copy-start.2
  5.7 0.7 copy-start.3
  6.4 4.6 %copy-start.4 = (f32[16,64,256]{2,1,0:T(8,128)S(1)}, f32[16,64,256]{2,1,0:T(8,128)}, u32[]{:S(2)}) copy-start(f32[16,64,256]{2,1,0:T(8,128)} %param.9) | copy-start | bytes 3145732
  11.1 12.4 %collective-permute-start.2 = (f32[8,64,256]{2,1,0:T(8,128)S(1)}, f32[8,64,256]{2,1,0:T(8,128)S(1)}, u32[]{:S(2)}, u32[]{:S(2)}) collective-permute-start(f32[8,64,256]{2,1,0:T(8,128)S(1)} %get-tuple-element.36.refs_1_.refs_2_), channel_id=1, source_target_pairs={{0,1},{1,2},{2,3},{3,4},{4,5},{5,6},{6,7},{7,8},{8,9},{9,10},{10,1... | collective-permute-start | bytes 1572872 | tf_op jit(solution)/shard_map/ppermute | solution.py:333
  13.5 14.9 %collective-permute-start.1 = (f32[8,64,256]{2,1,0:T(8,128)S(1)}, f32[8,64,256]{2,1,0:T(8,128)S(1)}, u32[]{:S(2)}, u32[]{:S(2)}) collective-permute-start(f32[8,64,256]{2,1,0:T(8,128)S(1)} %get-tuple-element.34.refs_0_.refs_1_.refs_2_), channel_id=1, source_target_pairs={{0,1},{1,2},{2,3},{3,4},{4,5},{5,6},{6,7},{7,8},{8,9},{9,10},{10,1... | collective-permute-start | bytes 1572872 | tf_op jit(solution)/shard_map/ppermute | solution.py:333
  26.8 8.7 %collective-permute-start.5 = (f32[8,64,256]{2,1,0:T(8,128)S(1)}, f32[8,64,256]{2,1,0:T(8,128)S(1)}, u32[]{:S(2)}, u32[]{:S(2)}) collective-permute-start(f32[8,64,256]{2,1,0:T(8,128)S(1)} %get-tuple-element.46.refs_3_), channel_id=1, source_target_pairs={{0,1},{1,2},{2,3},{3,4},{4,5},{5,6},{6,7},{7,8},{8,9},{9,10},{10,1... | collective-permute-start | bytes 1572872 | tf_op jit(solution)/shard_map/ppermute | solution.py:333
  31.8 9.3 %collective-permute-start.3 = (f32[8,64,256]{2,1,0:T(8,128)S(1)}, f32[8,64,256]{2,1,0:T(8,128)S(1)}, u32[]{:S(2)}, u32[]{:S(2)}) collective-permute-start(f32[8,64,256]{2,1,0:T(8,128)S(1)} %get-tuple-element.45.refs_2_), channel_id=1, source_target_pairs={{0,1},{1,2},{2,3},{3,4},{4,5},{5,6},{6,7},{7,8},{8,9},{9,10},{10,1... | collective-permute-start | bytes 1572872 | tf_op jit(solution)/shard_map/ppermute | solution.py:333
  35.5 11.2 %collective-permute-start.6 = (f32[8,64,256]{2,1,0:T(8,128)S(1)}, f32[8,64,256]{2,1,0:T(8,128)S(1)}, u32[]{:S(2)}, u32[]{:S(2)}) collective-permute-start(f32[8,64,256]{2,1,0:T(8,128)S(1)} %collective-permute-done.5.refs_1_.refs_2_), channel_id=1, source_target_pairs={{0,1},{1,2},{2,3},{3,4},{4,5},{5,6},{6,7},{7,8},{8,9},{9,10},{10,1... | collective-permute-start | bytes 1572872 | tf_op jit(solution)/shard_map/ppermute | solution.py:333
  41.1 11.2 %collective-permute-start.4 = (f32[8,64,256]{2,1,0:T(8,128)S(1)}, f32[8,64,256]{2,1,0:T(8,128)S(1)}, u32[]{:S(2)}, u32[]{:S(2)}) collective-permute-start(f32[8,64,256]{2,1,0:T(8,128)S(1)} %collective-permute-done.3.refs_0_.refs_1_.refs_2_), channel_id=1, source_target_pairs={{0,1},{1,2},{2,3},{3,4},{4,5},{5,6},{6,7},{7,8},{8,9},{9,10},{10,1... | collective-permute-start | bytes 1572872 | tf_op jit(solution)/shard_map/ppermute | solution.py:333
  50.2 8.7 %collective-permute-start.9 = (f32[8,64,256]{2,1,0:T(8,128)S(1)}, f32[8,64,256]{2,1,0:T(8,128)S(1)}, u32[]{:S(2)}, u32[]{:S(2)}) collective-permute-start(f32[8,64,256]{2,1,0:T(8,128)S(1)} %get-tuple-element.51.refs_3_), channel_id=1, source_target_pairs={{0,1},{1,2},{2,3},{3,4},{4,5},{5,6},{6,7},{7,8},{8,9},{9,10},{10,1... | collective-permute-start | bytes 1572872 | tf_op jit(solution)/shard_map/ppermute | solution.py:333
  55.8 8.7 %collective-permute-start.7 = (f32[8,64,256]{2,1,0:T(8,128)S(1)}, f32[8,64,256]{2,1,0:T(8,128)S(1)}, u32[]{:S(2)}, u32[]{:S(2)}) collective-permute-start(f32[8,64,256]{2,1,0:T(8,128)S(1)} %get-tuple-element.50.refs_2_), channel_id=1, source_target_pairs={{0,1},{1,2},{2,3},{3,4},{4,5},{5,6},{6,7},{7,8},{8,9},{9,10},{10,1... | collective-permute-start | bytes 1572872 | tf_op jit(solution)/shard_map/ppermute | solution.py:333
  58.8 11.3 %collective-permute-start.10 = (f32[8,64,256]{2,1,0:T(8,128)S(1)}, f32[8,64,256]{2,1,0:T(8,128)S(1)}, u32[]{:S(2)}, u32[]{:S(2)}) collective-permute-start(f32[8,64,256]{2,1,0:T(8,128)S(1)} %collective-permute-done.9.refs_1_.refs_2_), channel_id=1, source_target_pairs={{0,1},{1,2},{2,3},{3,4},{4,5},{5,6},{6,7},{7,8},{8,9},{9,10},{10,1... | collective-permute-start | bytes 1572872 | tf_op jit(solution)/shard_map/ppermute | solution.py:333
  64.5 13.0 %collective-permute-start.8 = (f32[8,64,256]{2,1,0:T(8,128)S(1)}, f32[8,64,256]{2,1,0:T(8,128)S(1)}, u32[]{:S(2)}, u32[]{:S(2)}) collective-permute-start(f32[8,64,256]{2,1,0:T(8,128)S(1)} %collective-permute-done.7.refs_0_.refs_1_.refs_2_), channel_id=1, source_target_pairs={{0,1},{1,2},{2,3},{3,4},{4,5},{5,6},{6,7},{7,8},{8,9},{9,10},{10,1... | collective-permute-start | bytes 1572872 | tf_op jit(solution)/shard_map/ppermute | solution.py:333
  73.5 8.9 %collective-permute-start.13 = (f32[8,64,256]{2,1,0:T(8,128)S(1)}, f32[8,64,256]{2,1,0:T(8,128)S(1)}, u32[]{:S(2)}, u32[]{:S(2)}) collective-permute-start(f32[8,64,256]{2,1,0:T(8,128)S(1)} %get-tuple-element.56.refs_3_), channel_id=1, source_target_pairs={{0,1},{1,2},{2,3},{3,4},{4,5},{5,6},{6,7},{7,8},{8,9},{9,10},{10,1... | collective-permute-start | bytes 1572872 | tf_op jit(solution)/shard_map/ppermute | solution.py:333
  80.9 8.7 %collective-permute-start.11 = (f32[8,64,256]{2,1,0:T(8,128)S(1)}, f32[8,64,256]{2,1,0:T(8,128)S(1)}, u32[]{:S(2)}, u32[]{:S(2)}) collective-permute-start(f32[8,64,256]{2,1,0:T(8,128)S(1)} %get-tuple-element.55.refs_2_), channel_id=1, source_target_pairs={{0,1},{1,2},{2,3},{3,4},{4,5},{5,6},{6,7},{7,8},{8,9},{9,10},{10,1... | collective-permute-start | bytes 1572872 | tf_op jit(solution)/shard_map/ppermute | solution.py:333
  82.4 12.8 %collective-permute-start.14 = (f32[8,64,256]{2,1,0:T(8,128)S(1)}, f32[8,64,256]{2,1,0:T(8,128)S(1)}, u32[]{:S(2)}, u32[]{:S(2)}) collective-permute-start(f32[8,64,256]{2,1,0:T(8,128)S(1)} %collective-permute-done.13.refs_1_.refs_2_), channel_id=1, source_target_pairs={{0,1},{1,2},{2,3},{3,4},{4,5},{5,6},{6,7},{7,8},{8,9},{9,10},{10,1... | collective-permute-start | bytes 1572872 | tf_op jit(solution)/shard_map/ppermute | solution.py:333
  89.6 11.2 %collective-permute-start.12 = (f32[8,64,256]{2,1,0:T(8,128)S(1)}, f32[8,64,256]{2,1,0:T(8,128)S(1)}, u32[]{:S(2)}, u32[]{:S(2)}) collective-permute-start(f32[8,64,256]{2,1,0:T(8,128)S(1)} %collective-permute-done.11.refs_0_.refs_1_.refs_2_), channel_id=1, source_target_pairs={{0,1},{1,2},{2,3},{3,4},{4,5},{5,6},{6,7},{7,8},{8,9},{9,10},{10,1... | collective-permute-start | bytes 1572872 | tf_op jit(solution)/shard_map/ppermute | solution.py:333
  98.7 8.7 %collective-permute-start.16 = (f32[8,64,256]{2,1,0:T(8,128)S(1)}, f32[8,64,256]{2,1,0:T(8,128)S(1)}, u32[]{:S(2)}, u32[]{:S(2)}) collective-permute-start(f32[8,64,256]{2,1,0:T(8,128)S(1)} %get-tuple-element.61), channel_id=1, source_target_pairs={{0,13},{1,2},{2,15},{3,0},{4,1},{5,6},{6,3},{7,4},{8,5},{9,10},{10... | collective-permute-start | bytes 1572872 | tf_op jit(solution)/shard_map/ppermute | solution.py:333
  104.3 17.0 %collective-permute-start.15 = (f32[8,64,256]{2,1,0:T(8,128)S(1)}, f32[8,64,256]{2,1,0:T(8,128)S(1)}, u32[]{:S(2)}, u32[]{:S(2)}) collective-permute-start(f32[8,64,256]{2,1,0:T(8,128)S(1)} %get-tuple-element.60), channel_id=1, source_target_pairs={{0,13},{1,14},{2,15},{3,0},{4,1},{5,2},{6,3},{7,4},{8,5},{9,6},{10... | collective-permute-start | bytes 1572872 | tf_op jit(solution)/shard_map/ppermute | solution.py:333
  107.3 18.0 %collective-permute-start.17 = (f32[8,64,256]{2,1,0:T(8,128)S(1)}, f32[8,64,256]{2,1,0:T(8,128)S(1)}, u32[]{:S(2)}, u32[]{:S(2)}) collective-permute-start(f32[8,64,256]{2,1,0:T(8,128)S(1)} %collective-permute-done.16), channel_id=1, source_target_pairs={{0,0},{1,1},{2,14},{3,3},{4,4},{5,5},{6,2},{7,7},{8,8},{9,9},{10,6... | collective-permute-start | bytes 1572872 | tf_op jit(solution)/shard_map/ppermute | solution.py:333

commit v3 on v2

--- a/solution.py
+++ b/solution.py
@@ -254,53 +254,57 @@
     return call(kernel, "upper", own + above, shared, ops[0::2], [PLANES], scratch)[0]
 
 
-def half_update(start, below, own, ratios, shared, ops):
-    parts = len(below) + len(own)
+def below_and_own(below, own, start):
+    out = []
+    for pieces, first in ((below, start), (own, 0)):
+        at = 0
+        for piece in pieces:
+            n = piece.shape[0]
+            if at + n > first:
+                out.append((piece, max(first - at, 0)))
+            at += n
+    return out
+
+
+def piece_update(start, below, own, ratios, shared, ops):
+    sources = below_and_own(below, own, start)
+    lower = sum(any(piece is p for p in below) for piece, _ in sources)
+    parts = len(sources)
     given = parts + len(ratios)
+    at = 0
+    for i, piece in enumerate(own):
+        if at <= start < at + piece.shape[0]:
+            mine, offset = lower + i, start - at
+        at += piece.shape[0]
 
     def kernel(*refs):
         slab, ends, depth_f, depth_a, row_f, row_a, col_f, col_a = refs[given : given + 8]
-        ratio, updated, spread, mixed, spread_hi, mixed_hi, spread_lo, mixed_lo = refs[given + 8 :]
+        ratio, updated, spread, mixed, spread_a, mixed_a = refs[given + 8 :]
         live = ends[0]
-        scales = [live] * len(below) + [None] * len(own)
-
-        def divide(t):
-            planes = slice(t * QUAD, (t + 1) * QUAD)
-            seen = slab[start + t * QUAD : start + (t + 1) * QUAD].astype(F32)
-            value = seen / col_whole(mixed, col_f, t)
-            ratio[planes] = value * live if start == 0 else value
-
-        def back(t, mixed_t):
-            planes = slice(t * QUAD, (t + 1) * QUAD)
-            updated[planes] = refs[parts - 1][planes] * col_whole(mixed_t, col_a, 0)
-
-        ratio_refs = [(ref, 0) for ref in refs[parts:given]]
-        depth_whole(window([(ref, 0) for ref in refs[:parts]], scales), depth_f, HALF, spread)
-        row_whole(spread, row_f, mixed, 1)
-        divide(1)
+        depth = depth_whole if start in (0, PLANES - QUAD) else depth_pass
+        scales = [live] * lower + [None] * (parts - lower)
+        cells = window([(ref, at) for ref, (_, at) in zip(refs, sources)], scales)
+        depth(cells, depth_f, QUAD, spread)
         row_whole(spread, row_f, mixed, 0)
-        depth_whole(window([(ratio, QUAD)] + ratio_refs), depth_a, QUAD, spread_hi)
-        divide(0)
-        row_whole(spread_hi, row_a, mixed_hi, 0)
-        depth_whole(window([(ratio, 0)] + ratio_refs), depth_a, QUAD, spread_lo)
-        back(1, mixed_hi)
-        row_whole(spread_lo, row_a, mixed_lo, 0)
-        back(0, mixed_lo)
+        value = slab[start : start + QUAD].astype(F32) / col_whole(mixed, col_f, 0)
+        ratio[...] = value * live if start < MARGIN else value
+        cells = window([(ref, 0) for ref in (ratio,) + refs[parts:given]])
+        depth(cells, depth_a, QUAD, spread_a)
+        row_whole(spread_a, row_a, mixed_a, 0)
+        updated[...] = refs[mine][offset : offset + QUAD] * col_whole(mixed_a, col_a, 0)
 
     ranks = ops[0].shape[0]
-    scratch = [
-        shape
-        for tiles in (2, 1, 1)
-        for shape in ((ranks, tiles, TILE, COLS), (tiles * TILE, ranks * COLS))
-    ]
-    return call(kernel, "half", below + own + ratios, shared, ops, [HALF, HALF], scratch)
-
-
-def whole(lo, hi):
-    def kernel(lo, hi, out, sems):
+    scratch = [(ranks, 1, TILE, COLS), (TILE, ranks * COLS)] * 2
+    arrays = [piece for piece, _ in sources] + ratios
+    return call(kernel, "piece", arrays, shared, ops, [QUAD, QUAD], scratch)
+
+
+def whole(pieces):
+    def kernel(*refs):
+        out, sems = refs[-2:]
         copies = [
-            pltpu.make_async_copy(half, out.at[pl.ds(i * HALF, HALF)], sems.at[i])
-            for i, half in enumerate((lo, hi))
+            pltpu.make_async_copy(piece, out.at[pl.ds(i * QUAD, QUAD)], sems.at[i])
+            for i, piece in enumerate(refs[:-2])
         ]
         for copy in copies:
             copy.start()
@@ -310,13 +314,13 @@
     return pl.pallas_call(
         kernel,
         out_shape=jax.ShapeDtypeStruct((PLANES, ROWS, COLS), F32),
-        in_specs=[VMEM] * 2,
+        in_specs=[VMEM] * len(pieces),
         out_specs=HBM,
-        scratch_shapes=[pltpu.SemaphoreType.DMA((2,))],
+        scratch_shapes=[pltpu.SemaphoreType.DMA((len(pieces),))],
         compiler_params=pltpu.CompilerParams(vmem_limit_bytes=20 * 2**20),
         cost_estimate=COST,
         name="whole",
-    )(lo, hi)
+    )(*pieces)
 
 
 def shards(
@@ -343,25 +347,24 @@
     early_lo, _ = lax.optimization_barrier((own_lo, above[0]))
     below_lo = send(early_lo, 1, skip=(count - 1,))
 
+    below, own = [below_lo, below_hi], [own_lo, own_hi]
     for step in range(STEPS):
         last = step == STEPS - 1
         shared = [slabs[step], ends[step]]
-        ratio_up = upper_ratio([own_lo, own_hi], above, shared, ops)
-        ratio_mid, hi = half_update(HALF, [below_hi], [own_lo, own_hi], [ratio_up], shared, ops)
-        next_hi = send(hi, 1 - STEPS, (1, 1)) if last else send(hi, 1)
-        _, lo = half_update(
-            0, [below_lo, below_hi], [own_lo], [ratio_mid, ratio_up], shared, ops
-        )
-        above = [lo, hi]
-        if last:
-            next_hi, _ = lax.optimization_barrier((next_hi, lo))
-            own_lo = send(lo, 1 - STEPS)
-            own_hi = send(next_hi, 0, (2, -STEPS))
-        else:
-            own_lo, own_hi = send(lo, 1), next_hi
-            below_hi = send(own_hi, 1)
-            below_lo = send(own_lo, 1)
-    return whole(own_lo, own_hi)
+        ratios = [upper_ratio(own, above, shared, ops)]
+        updated, arrived = [], []
+        for start in range(PLANES - QUAD, -1, -QUAD):
+            ratio, piece = piece_update(start, below, own, ratios, shared, ops)
+            ratios = [ratio] + ratios
+            updated = [piece] + updated
+            relayed = (1, 1) if start >= HALF else None
+            piece = send(piece, 1 - STEPS, relayed) if last else send(piece, 1)
+            arrived = [piece] + arrived
+        above, own = updated, arrived
+        if not last:
+            below = [send(piece, 1) for piece in own[::-1]][::-1]
+    upper, _ = lax.optimization_barrier((own[HALF // QUAD :], updated[0]))
+    return whole(own[: HALF // QUAD] + [send(piece, 0, (2, -STEPS)) for piece in upper])
 
 
 def solution(mesh):

time: 127 us -> 132 us (1.039); the launches traced: 127 us -> 129 us
  waiting for transfers between devices: 46.5 us -> 23.2 us
  Pallas kernels: 50.7 us -> 66.8 us
  starting transfers between devices: 22.4 us -> 32.1 us
    ppermute x18 -> x33, waiting for transfers between devices: 46.5 us -> 23.2 us  [send(): return lax.ppermute(cells, 'view', pairs)]
    pallas_call x12 -> x20, Pallas kernels: 45.2 us -> 61.3 us  [call(): pl.pallas_call(kernel, out_shape=out, in_specs=[VMEM] * (len(arrays) + le...]
    ppermute x18 -> x33, starting transfers between devices: 22.4 us -> 32.1 us  [send(): return lax.ppermute(cells, 'view', pairs)]
  transfers between devices with their start and end apart: 18 -> 33, of which waited for: 15 -> 10; matrix products, arithmetic and copies ran while one was open for 2% -> 2% of each run, Pallas kernels for 39% -> 51%
where the time goes in v3:
time: 132 us; the launch traced here: 129 us
  Pallas kernels  66.8 us (51%)
  starting transfers between devices  32.1 us (24%)
  waiting for transfers between devices  23.2 us (18%)
  local copies, waits for them, and re-layouts  6.38 us (5%)
    pallas_call x20, Pallas kernels, call(): pl.pallas_call(kernel, out_shape=out, in_specs=[VMEM] * (len(arrays) + le...  61.3 us
    ppermute x33, starting transfers between devices, send(): return lax.ppermute(cells, 'view', pairs)  32.1 us
    ppermute x33, waiting for transfers between devices, send(): return lax.ppermute(cells, 'view', pairs)  23.2 us
    unnamed x13, local copies, waits for them, and re-layouts  6.31 us
    pallas_call x1, Pallas kernels, build(): pl.pallas_call(build_kernel, out_shape=[depth, depth] + [square] * 4 + [s...  4.57 us
  transfers between devices with their start and end apart: 33, of which 10 were waited for; matrix products, arithmetic and copies ran while one was open for 2% of the time, Pallas kernels for 51%

profile of v3, /device:TPU:28, one launch (start us, length us, event | category | flops | bytes accessed | tf_op | source)
XLA Modules:
  0.0 129.1 jit_solution(4052483800750534567)
XLA Ops:
  0.0 0.7 copy.10.row_taps
  0.7 0.7 copy.11.col_taps
  1.4 0.7 copy.9.depth_taps
  2.2 2.2 %copy-done = bf16[1,4,32,64,256]{4,3,2,1,0:T(8,128)(2,1)S(1)} copy-done((bf16[1,4,32,64,256]{4,3,2,1,0:T(8,128)(2,1)S(1)}, bf16[1,4,32,64,256]{4,3,2,1,0:T(8,128)(2,1)}, u32[]{:S(2)}) %copy-start) | copy-done | bytes 4194328
  4.4 0.7 copy-done.1
  5.1 0.7 copy-done.2
  5.7 0.7 copy-done.3
  6.4 4.6 %build.1 = (bf16[6,128,256]{2,1,0:T(8,128)(2,1)S(1)}, bf16[6,128,256]{2,1,0:T(8,128)(2,1)S(1)}, bf16[6,256,256]{2,1,0:T(8,128)(2,1)S(1)}, bf16[6,256,256]{2,1,0:...) custom-call(s32[2]{0:T(128)S(1)} %pad_add_fusion.place, ...), custom_call_target="tpu_custom_call" | custom-call | tf_op jit(solution)/shard_map/build/pallas_call | solution.py:128
  11.1 2.4 %collective-permute-start.2 = (f32[8,64,256]{2,1,0:T(8,128)S(1)}, f32[8,64,256]{2,1,0:T(8,128)S(1)}, u32[]{:S(2)}, u32[]{:S(2)}) collective-permute-start(f32[8,64,256]{2,1,0:T(8,128)S(1)} %get-tuple-element.53.refs_1_.refs_2_.refs_3_), channel_id=1, source_target_pairs={{0,1},{1,2},{2,3},{3,4},{4,5},{5,6},{6,7},{7,8},{8,9},{9,10},{10,1... | collective-permute-start | bytes 1572872 | tf_op jit(solution)/shard_map/ppermute | solution.py:337
  13.5 5.5 %collective-permute-start.1 = (f32[8,64,256]{2,1,0:T(8,128)S(1)}, f32[8,64,256]{2,1,0:T(8,128)S(1)}, u32[]{:S(2)}, u32[]{:S(2)}) collective-permute-start(f32[8,64,256]{2,1,0:T(8,128)S(1)} %get-tuple-element.51.refs_0_.refs_1_.refs_2_), channel_id=1, source_target_pairs={{0,1},{1,2},{2,3},{3,4},{4,5},{5,6},{6,7},{7,8},{8,9},{9,10},{10,1... | collective-permute-start | bytes 1572872 | tf_op jit(solution)/shard_map/ppermute | solution.py:337
  19.0 4.4 %upper.4.refs_3_.refs_4_.refs_6_.refs_7_ = f32[16,64,256]{2,1,0:T(8,128)S(1)} custom-call(f32[8,64,256]{2,1,0:T(8,128)S(1)} %get-tuple-element.51.refs_0_.refs_1_.refs_2_, f32[8,64,256]{2,1,0:T(8,128)S(1)} %get-tuple-element.53.refs_1_.refs_2_.refs_3_, f32[16,64,256]{2,1,0:T(8,128)S(1)} %collective-permute-done.refs_2_, ...), custom_call_target="tpu_custom_call" | custom-call | flops 1048576 | bytes 1024 | tf_op jit(solution)/shard_map/upper/pallas_call | solution.py:218
  23.4 2.3 %piece.16 = (f32[4,64,256]{2,1,0:T(8,128)S(1)}, f32[4,64,256]{2,1,0:T(8,128)S(1)}) custom-call(f32[8,64,256]{2,1,0:T(8,128)S(1)} %collective-permute-done.2.refs_0_.refs_1_, f32[8,64,256]{2,1,0:T(8,128)S(1)} %get-tuple-element.51.refs_0_.refs_1_.refs_2_, f32[8,64,256]{2,1,0:T(8,128)S(1)} %get-tuple-element.53.refs_1_.refs_2_.refs_3_, ...), custom_call_target="tpu_custom_call" | custom-call | flops 1048576 | bytes 1024 | tf_op jit(solution)/shard_map/piece/pallas_call | solution.py:218
  25.7 3.2 %piece.17 = (f32[4,64,256]{2,1,0:T(8,128)S(1)}, f32[4,64,256]{2,1,0:T(8,128)S(1)}) custom-call(f32[8,64,256]{2,1,0:T(8,128)S(1)} %collective-permute-done.2.refs_0_.refs_1_, f32[8,64,256]{2,1,0:T(8,128)S(1)} %get-tuple-element.51.refs_0_.refs_1_.refs_2_, f32[8,64,256]{2,1,0:T(8,128)S(1)} %get-tuple-element.53.refs_1_.refs_2_.refs_3_, ...), custom_call_target="tpu_custom_call" | custom-call | flops 1048576 | bytes 1024 | tf_op jit(solution)/shard_map/piece/pallas_call | solution.py:218
  29.0 3.2 %piece.18 = (f32[4,64,256]{2,1,0:T(8,128)S(1)}, f32[4,64,256]{2,1,0:T(8,128)S(1)}) custom-call(f32[8,64,256]{2,1,0:T(8,128)S(1)} %collective-permute-done.1.refs_0_, f32[8,64,256]{2,1,0:T(8,128)S(1)} %collective-permute-done.2.refs_0_.refs_1_, f32[8,64,256]{2,1,0:T(8,128)S(1)} %get-tuple-element.51.refs_0_.refs_1_.refs_2_, ...), custom_call_target="tpu_custom_call" | custom-call | flops 1048576 | bytes 1024 | tf_op jit(solution)/shard_map/piece/pallas_call | solution.py:218
  32.3 2.3 %piece.19 = (f32[4,64,256]{2,1,0:T(8,128)}, f32[4,64,256]{2,1,0:T(8,128)S(1)}) custom-call(f32[8,64,256]{2,1,0:T(8,128)S(1)} %collective-permute-done.1.refs_0_, f32[8,64,256]{2,1,0:T(8,128)S(1)} %collective-permute-done.2.refs_0_.refs_1_, f32[8,64,256]{2,1,0:T(8,128)S(1)} %get-tuple-element.51.refs_0_.refs_1_.refs_2_, ...), custom_call_target="tpu_custom_call" | custom-call | flops 1048576 | bytes 1024 | tf_op jit(solution)/shard_map/piece/pallas_call | solution.py:218
  34.9 3.0 %collective-permute-start.8 = (f32[4,64,256]{2,1,0:T(8,128)S(1)}, f32[4,64,256]{2,1,0:T(8,128)S(1)}, u32[]{:S(2)}, u32[]{:S(2)}) collective-permute-start(f32[4,64,256]{2,1,0:T(8,128)S(1)} %collective-permute-done.7.refs_2_.refs_3_.refs_4_.refs_5_.refs_6_), channel_id=1, source_target_pairs={{0,1},{1,2},{2,3},{3,4},{4,5},{5,6},{6,7},{7,8},{8,9},{9,10},{10,1... | collective-permute-start | bytes 786440 | tf_op jit(solution)/shard_map/ppermute | solution.py:337
  38.1 2.8 %collective-permute-done.3.refs_0_.refs_1_.refs_2_.refs_3_.refs_4_ = f32[4,64,256]{2,1,0:T(8,128)S(1)} collective-permute-done((f32[4,64,256]{2,1,0:T(8,128)S(1)}, f32[4,64,256]{2,1,0:T(8,128)S(1)}, u32[]{:S(2)}, u32[]{:S(2)}) %collective-permute-start.3) | collective-permute-done | bytes 262176 | tf_op jit(solution)/shard_map/ppermute | solution.py:337
  41.0 4.4 %upper.5.refs_5_.refs_7_.refs_9_.refs_11_ = f32[16,64,256]{2,1,0:T(8,128)S(1)} custom-call(f32[4,64,256]{2,1,0:T(8,128)S(1)} %collective-permute-done.3.refs_0_.refs_1_.refs_2_.refs_3_.refs_4_, f32[4,64,256]{2,1,0:T(8,128)S(1)} %collective-permute-done.5.refs_1_.refs_2_.refs_3_.refs_4_.refs_5_, ...), custom_call_target="tpu_custom_call" | custom-call | flops 1048576 | bytes 1024 | tf_op jit(solution)/shard_map/upper/pallas_call | solution.py:218
  45.5 2.3 %piece.20 = (f32[4,64,256]{2,1,0:T(8,128)S(1)}, f32[4,64,256]{2,1,0:T(8,128)S(1)}) custom-call(f32[4,64,256]{2,1,0:T(8,128)S(1)} %collective-permute-done.10.refs_0_.refs_1_.refs_2_.refs_3_, f32[4,64,256]{2,1,0:T(8,128)S(1)} %collective-permute-done.3.refs_0_.refs_1_.refs_2_.refs_3_.refs_4_, ...), custom_call_target="tpu_custom_call" | custom-call | flops 1048576 | bytes 1024 | tf_op jit(solution)/shard_map/piece/pallas_call | solution.py:218
  47.7 2.9 %collective-permute-start.17 = (f32[4,64,256]{2,1,0:T(8,128)S(1)}, f32[4,64,256]{2,1,0:T(8,128)S(1)}, u32[]{:S(2)}, u32[]{:S(2)}) collective-permute-start(f32[4,64,256]{2,1,0:T(8,128)S(1)} %get-tuple-element.76.refs_7_), channel_id=1, source_target_pairs={{0,1},{1,2},{2,3},{3,4},{4,5},{5,6},{6,7},{7,8},{8,9},{9,10},{10,1... | collective-permute-start | bytes 786440 | tf_op jit(solution)/shard_map/ppermute | solution.py:337
  50.6 3.2 %piece.21 = (f32[4,64,256]{2,1,0:T(8,128)S(1)}, f32[4,64,256]{2,1,0:T(8,128)S(1)}) custom-call(f32[4,64,256]{2,1,0:T(8,128)S(1)} %collective-permute-done.8.refs_0_.refs_1_.refs_2_, f32[4,64,256]{2,1,0:T(8,128)S(1)} %collective-permute-done.10.refs_0_.refs_1_.refs_2_.refs_3_, ...), custom_call_target="tpu_custom_call" | custom-call | flops 1048576 | bytes 1024 | tf_op jit(solution)/shard_map/piece/pallas_call | solution.py:218
  53.9 3.2 %piece.22 = (f32[4,64,256]{2,1,0:T(8,128)S(1)}, f32[4,64,256]{2,1,0:T(8,128)S(1)}) custom-call(f32[4,64,256]{2,1,0:T(8,128)S(1)} %collective-permute-done.6.refs_0_.refs_1_, f32[4,64,256]{2,1,0:T(8,128)S(1)} %collective-permute-done.8.refs_0_.refs_1_.refs_2_, f32[4,64,256]{2,1,0:T(8,128)S(1)} %collective-permute-done.10.refs_0_.refs_1_.refs_2_.refs_3_, ...), custom_call_target="tpu_custom_call" | custom-call | flops 1048576 | bytes 1024 | tf_op jit(solution)/shard_map/piece/pallas_call | solution.py:218
  57.5 2.3 %piece.23 = (f32[4,64,256]{2,1,0:T(8,128)}, f32[4,64,256]{2,1,0:T(8,128)S(1)}) custom-call(f32[4,64,256]{2,1,0:T(8,128)S(1)} %collective-permute-done.4.refs_0_, f32[4,64,256]{2,1,0:T(8,128)S(1)} %collective-permute-done.6.refs_0_.refs_1_, f32[4,64,256]{2,1,0:T(8,128)S(1)} %collective-permute-done.8.refs_0_.refs_1_.refs_2_, ...), custom_call_target="tpu_custom_call" | custom-call | flops 1048576 | bytes 1024 | tf_op jit(solution)/shard_map/piece/pallas_call | solution.py:218
  59.9 1.0 collective-permute-start.18
  61.0 1.9 %collective-permute-done.13.refs_1_.refs_2_.refs_3_.refs_4_.refs_5_ = f32[4,64,256]{2,1,0:T(8,128)S(1)} collective-permute-done((f32[4,64,256]{2,1,0:T(8,128)S(1)}, f32[4,64,256]{2,1,0:T(8,128)S(1)}, u32[]{:S(2)}, u32[]{:S(2)}) %collective-permute-start.13) | collective-permute-done | bytes 262176 | tf_op jit(solution)/shard_map/ppermute | solution.py:337
  63.1 2.6 %collective-permute-done.11.refs_0_.refs_1_.refs_2_.refs_3_.refs_4_ = f32[4,64,256]{2,1,0:T(8,128)S(1)} collective-permute-done((f32[4,64,256]{2,1,0:T(8,128)S(1)}, f32[4,64,256]{2,1,0:T(8,128)S(1)}, u32[]{:S(2)}, u32[]{:S(2)}) %collective-permute-start.11) | collective-permute-done | bytes 262176 | tf_op jit(solution)/shard_map/ppermute | solution.py:337
  66.0 4.4 %upper.6.refs_5_.refs_7_.refs_9_.refs_11_ = f32[16,64,256]{2,1,0:T(8,128)S(1)} custom-call(f32[4,64,256]{2,1,0:T(8,128)S(1)} %collective-permute-done.11.refs_0_.refs_1_.refs_2_.refs_3_.refs_4_, f32[4,64,256]{2,1,0:T(8,128)S(1)} %collective-permute-done.13.refs_1_.refs_2_.refs_3_.refs_4_.refs_5_, ...), custom_call_target="tpu_custom_call" | custom-call | flops 1048576 | bytes 1024 | tf_op jit(solution)/shard_map/upper/pallas_call | solution.py:218
  70.5 2.3 %piece.24 = (f32[4,64,256]{2,1,0:T(8,128)S(1)}, f32[4,64,256]{2,1,0:T(8,128)S(1)}) custom-call(f32[4,64,256]{2,1,0:T(8,128)S(1)} %collective-permute-done.18.refs_0_.refs_1_.refs_2_.refs_3_, f32[4,64,256]{2,1,0:T(8,128)S(1)} %collective-permute-done.11.refs_0_.refs_1_.refs_2_.refs_3_.refs_4_, ...), custom_call_target="tpu_custom_call" | custom-call | flops 1048576 | bytes 1024 | tf_op jit(solution)/shard_map/piece/pallas_call | solution.py:218
  72.7 3.6 %collective-permute-start.25 = (f32[4,64,256]{2,1,0:T(8,128)S(1)}, f32[4,64,256]{2,1,0:T(8,128)S(1)}, u32[]{:S(2)}, u32[]{:S(2)}) collective-permute-start(f32[4,64,256]{2,1,0:T(8,128)S(1)} %get-tuple-element.85.refs_7_), channel_id=1, source_target_pairs={{0,1},{1,2},{2,3},{3,4},{4,5},{5,6},{6,7},{7,8},{8,9},{9,10},{10,1... | collective-permute-start | bytes 786440 | tf_op jit(solution)/shard_map/ppermute | solution.py:337
  76.4 3.2 %piece.25 = (f32[4,64,256]{2,1,0:T(8,128)S(1)}, f32[4,64,256]{2,1,0:T(8,128)S(1)}) custom-call(f32[4,64,256]{2,1,0:T(8,128)S(1)} %collective-permute-done.16.refs_0_.refs_1_.refs_2_, f32[4,64,256]{2,1,0:T(8,128)S(1)} %collective-permute-done.18.refs_0_.refs_1_.refs_2_.refs_3_, ...), custom_call_target="tpu_custom_call" | custom-call | flops 1048576 | bytes 1024 | tf_op jit(solution)/shard_map/piece/pallas_call | solution.py:218
  79.6 3.2 %piece.26 = (f32[4,64,256]{2,1,0:T(8,128)S(1)}, f32[4,64,256]{2,1,0:T(8,128)S(1)}) custom-call(f32[4,64,256]{2,1,0:T(8,128)S(1)} %collective-permute-done.14.refs_0_.refs_1_, f32[4,64,256]{2,1,0:T(8,128)S(1)} %collective-permute-done.16.refs_0_.refs_1_.refs_2_, f32[4,64,256]{2,1,0:T(8,128)S(1)} %collective-permute-done.18.refs_0_.refs_1_.refs_2_.refs_3_, ...), custom_call_target="tpu_custom_call" | custom-call | flops 1048576 | bytes 1024 | tf_op jit(solution)/shard_map/piece/pallas_call | solution.py:218
  82.9 2.3 %piece.27 = (f32[4,64,256]{2,1,0:T(8,128)}, f32[4,64,256]{2,1,0:T(8,128)S(1)}) custom-call(f32[4,64,256]{2,1,0:T(8,128)S(1)} %collective-permute-done.12.refs_0_, f32[4,64,256]{2,1,0:T(8,128)S(1)} %collective-permute-done.14.refs_0_.refs_1_, f32[4,64,256]{2,1,0:T(8,128)S(1)} %collective-permute-done.16.refs_0_.refs_1_.refs_2_, ...), custom_call_target="tpu_custom_call" | custom-call | flops 1048576 | bytes 1024 | tf_op jit(solution)/shard_map/piece/pallas_call | solution.py:218
  85.3 1.4 %collective-permute-start.26 = (f32[4,64,256]{2,1,0:T(8,128)S(1)}, f32[4,64,256]{2,1,0:T(8,128)S(1)}, u32[]{:S(2)}, u32[]{:S(2)}) collective-permute-start(f32[4,64,256]{2,1,0:T(8,128)S(1)} %collective-permute-done.25.refs_3_.refs_4_.refs_5_.refs_6_.refs_7_), channel_id=1, source_target_pairs={{0,1},{1,2},{2,3},{3,4},{4,5},{5,6},{6,7},{7,8},{8,9},{9,10},{10,1... | collective-permute-start | bytes 786440 | tf_op jit(solution)/shard_map/ppermute | solution.py:337
  86.7 1.9 %collective-permute-done.21.refs_1_.refs_2_.refs_3_.refs_4_.refs_5_ = f32[4,64,256]{2,1,0:T(8,128)S(1)} collective-permute-done((f32[4,64,256]{2,1,0:T(8,128)S(1)}, f32[4,64,256]{2,1,0:T(8,128)S(1)}, u32[]{:S(2)}, u32[]{:S(2)}) %collective-permute-start.21) | collective-permute-done | bytes 262176 | tf_op jit(solution)/shard_map/ppermute | solution.py:337
  88.7 2.8 %collective-permute-done.19.refs_0_.refs_1_.refs_2_.refs_3_.refs_4_ = f32[4,64,256]{2,1,0:T(8,128)S(1)} collective-permute-done((f32[4,64,256]{2,1,0:T(8,128)S(1)}, f32[4,64,256]{2,1,0:T(8,128)S(1)}, u32[]{:S(2)}, u32[]{:S(2)}) %collective-permute-start.19) | collective-permute-done | bytes 262176 | tf_op jit(solution)/shard_map/ppermute | solution.py:337
  91.5 4.4 %upper.7.refs_5_.refs_7_.refs_9_.refs_11_ = f32[16,64,256]{2,1,0:T(8,128)S(1)} custom-call(f32[4,64,256]{2,1,0:T(8,128)S(1)} %collective-permute-done.19.refs_0_.refs_1_.refs_2_.refs_3_.refs_4_, f32[4,64,256]{2,1,0:T(8,128)S(1)} %collective-permute-done.21.refs_1_.refs_2_.refs_3_.refs_4_.refs_5_, ...), custom_call_target="tpu_custom_call" | custom-call | flops 1048576 | bytes 1024 | tf_op jit(solution)/shard_map/upper/pallas_call | solution.py:218
  95.9 2.3 %piece.28 = (f32[4,64,256]{2,1,0:T(8,128)S(1)}, f32[4,64,256]{2,1,0:T(8,128)S(1)}) custom-call(f32[4,64,256]{2,1,0:T(8,128)S(1)} %collective-permute-done.26.refs_0_.refs_1_.refs_2_.refs_3_, f32[4,64,256]{2,1,0:T(8,128)S(1)} %collective-permute-done.19.refs_0_.refs_1_.refs_2_.refs_3_.refs_4_, ...), custom_call_target="tpu_custom_call" | custom-call | flops 1048576 | bytes 1024 | tf_op jit(solution)/shard_map/piece/pallas_call | solution.py:218
  98.2 3.2 %piece.29 = (f32[4,64,256]{2,1,0:T(8,128)S(1)}, f32[4,64,256]{2,1,0:T(8,128)S(1)}) custom-call(f32[4,64,256]{2,1,0:T(8,128)S(1)} %collective-permute-done.24.refs_0_.refs_1_.refs_2_, f32[4,64,256]{2,1,0:T(8,128)S(1)} %collective-permute-done.26.refs_0_.refs_1_.refs_2_.refs_3_, ...), custom_call_target="tpu_custom_call" | custom-call | flops 1048576 | bytes 1024 | tf_op jit(solution)/shard_map/piece/pallas_call | solution.py:218
  101.4 3.8 %collective-permute-start.29 = (f32[4,64,256]{2,1,0:T(8,128)S(1)}, f32[4,64,256]{2,1,0:T(8,128)S(1)}, u32[]{:S(2)}, u32[]{:S(2)}) collective-permute-start(f32[4,64,256]{2,1,0:T(8,128)S(1)} %get-tuple-element.93), channel_id=1, source_target_pairs={{0,13},{1,2},{2,15},{3,0},{4,1},{5,6},{6,3},{7,4},{8,5},{9,10},{10... | collective-permute-start | bytes 786440 | tf_op jit(solution)/shard_map/ppermute | solution.py:337
  105.5 3.2 %piece.30 = (f32[4,64,256]{2,1,0:T(8,128)S(1)}, f32[4,64,256]{2,1,0:T(8,128)S(1)}) custom-call(f32[4,64,256]{2,1,0:T(8,128)S(1)} %collective-permute-done.22.refs_0_.refs_1_, f32[4,64,256]{2,1,0:T(8,128)S(1)} %collective-permute-done.24.refs_0_.refs_1_.refs_2_, f32[4,64,256]{2,1,0:T(8,128)S(1)} %collective-permute-done.26.refs_0_.refs_1_.refs_2_.refs_3_, ...), custom_call_target="tpu_custom_call" | custom-call | flops 1048576 | bytes 1024 | tf_op jit(solution)/shard_map/piece/pallas_call | solution.py:218
  108.7 2.3 %piece.31 = (f32[4,64,256]{2,1,0:T(8,128)}, f32[4,64,256]{2,1,0:T(8,128)S(1)}) custom-call(f32[4,64,256]{2,1,0:T(8,128)S(1)} %collective-permute-done.20.refs_0_, f32[4,64,256]{2,1,0:T(8,128)S(1)} %collective-permute-done.22.refs_0_.refs_1_, f32[4,64,256]{2,1,0:T(8,128)S(1)} %collective-permute-done.24.refs_0_.refs_1_.refs_2_, ...), custom_call_target="tpu_custom_call" | custom-call | flops 1048576 | bytes 1024 | tf_op jit(solution)/shard_map/piece/pallas_call | solution.py:218
  111.0 0.8 collective-permute-done.30
  111.9 2.3 %collective-permute-start.31 = (f32[4,64,256]{2,1,0:T(8,128)S(1)}, f32[4,64,256]{2,1,0:T(8,128)S(1)}, u32[]{:S(2)}, u32[]{:S(2)}) collective-permute-start(f32[4,64,256]{2,1,0:T(8,128)S(1)} %collective-permute-done.29), channel_id=1, source_target_pairs={{0,0},{1,1},{2,14},{3,3},{4,4},{5,5},{6,2},{7,7},{8,8},{9,9},{10,6... | collective-permute-start | bytes 786440 | tf_op jit(solution)/shard_map/ppermute | solution.py:337
  114.2 3.5 %collective-permute-start.32 = (f32[4,64,256]{2,1,0:T(8,128)S(1)}, f32[4,64,256]{2,1,0:T(8,128)S(1)}, u32[]{:S(2)}, u32[]{:S(2)}) collective-permute-start(f32[4,64,256]{2,1,0:T(8,128)S(1)} %collective-permute-done.30), channel_id=1, source_target_pairs={{0,0},{1,1},{2,14},{3,3},{4,4},{5,5},{6,2},{7,7},{8,8},{9,9},{10,6... | collective-permute-start | bytes 786440 | tf_op jit(solution)/shard_map/ppermute | solution.py:337
  117.8 4.1 %collective-permute-done.31.refs_2_ = f32[4,64,256]{2,1,0:T(8,128)S(1)} collective-permute-done((f32[4,64,256]{2,1,0:T(8,128)S(1)}, f32[4,64,256]{2,1,0:T(8,128)S(1)}, u32[]{:S(2)}, u32[]{:S(2)}) %collective-permute-start.31) | collective-permute-done | bytes 262176 | tf_op jit(solution)/shard_map/ppermute | solution.py:337
  121.9 2.8 %collective-permute-done.32.refs_3_ = f32[4,64,256]{2,1,0:T(8,128)S(1)} collective-permute-done((f32[4,64,256]{2,1,0:T(8,128)S(1)}, f32[4,64,256]{2,1,0:T(8,128)S(1)}, u32[]{:S(2)}, u32[]{:S(2)}) %collective-permute-start.32) | collective-permute-done | bytes 262176 | tf_op jit(solution)/shard_map/ppermute | solution.py:337
  124.7 3.2 %collective-permute-done.28.refs_1_ = f32[4,64,256]{2,1,0:T(8,128)S(1)} collective-permute-done((f32[4,64,256]{2,1,0:T(8,128)S(1)}, f32[4,64,256]{2,1,0:T(8,128)S(1)}, u32[]{:S(2)}, u32[]{:S(2)}) %collective-permute-start.28) | collective-permute-done | bytes 262176 | tf_op jit(solution)/shard_map/ppermute | solution.py:337
  127.9 1.0 whole.1
  (55 shorter events, 3.0 us)
Async XLA Ops:
  0.0 13.5 %collective-permute-start = (f32[16,64,256]{2,1,0:T(8,128)}, f32[16,64,256]{2,1,0:T(8,128)S(1)}, u32[]{:S(2)}, u32[]{:S(2)}) collective-permute-start(f32[16,64,256]{2,1,0:T(8,128)} %param.9), channel_id=1, source_target_pairs={{0,15},{1,0},{2,1},{3,2},{4,3},{5,4},{6,5},{7,6},{8,7},{9,8},{10,9... | collective-permute-start | bytes 3145736 | tf_op jit(solution)/shard_map/ppermute | solution.py:337
  2.2 2.2 %copy-start = (bf16[1,4,32,64,256]{4,3,2,1,0:T(8,128)(2,1)S(1)}, bf16[1,4,32,64,256]{4,3,2,1,0:T(8,128)(2,1)}, u32[]{:S(2)}) copy-start(bf16[1,4,32,64,256]{4,3,2,1,0:T(8,128)(2,1)} %images.1) | copy-start | bytes 12582916
  4.4 0.7 copy-start.1
  5.1 0.7 copy-start.2
  5.7 0.7 copy-start.3
  6.4 4.6 %copy-start.4 = (f32[16,64,256]{2,1,0:T(8,128)S(1)}, f32[16,64,256]{2,1,0:T(8,128)}, u32[]{:S(2)}) copy-start(f32[16,64,256]{2,1,0:T(8,128)} %param.9) | copy-start | bytes 3145732
  11.1 12.4 %collective-permute-start.2 = (f32[8,64,256]{2,1,0:T(8,128)S(1)}, f32[8,64,256]{2,1,0:T(8,128)S(1)}, u32[]{:S(2)}, u32[]{:S(2)}) collective-permute-start(f32[8,64,256]{2,1,0:T(8,128)S(1)} %get-tuple-element.53.refs_1_.refs_2_.refs_3_), channel_id=1, source_target_pairs={{0,1},{1,2},{2,3},{3,4},{4,5},{5,6},{6,7},{7,8},{8,9},{9,10},{10,1... | collective-permute-start | bytes 1572872 | tf_op jit(solution)/shard_map/ppermute | solution.py:337
  13.5 15.5 %collective-permute-start.1 = (f32[8,64,256]{2,1,0:T(8,128)S(1)}, f32[8,64,256]{2,1,0:T(8,128)S(1)}, u32[]{:S(2)}, u32[]{:S(2)}) collective-permute-start(f32[8,64,256]{2,1,0:T(8,128)S(1)} %get-tuple-element.51.refs_0_.refs_1_.refs_2_), channel_id=1, source_target_pairs={{0,1},{1,2},{2,3},{3,4},{4,5},{5,6},{6,7},{7,8},{8,9},{9,10},{10,1... | collective-permute-start | bytes 1572872 | tf_op jit(solution)/shard_map/ppermute | solution.py:337
  25.7 9.2 %collective-permute-start.9 = (f32[4,64,256]{2,1,0:T(8,128)S(1)}, f32[4,64,256]{2,1,0:T(8,128)S(1)}, u32[]{:S(2)}, u32[]{:S(2)}) collective-permute-start(f32[4,64,256]{2,1,0:T(8,128)S(1)} %get-tuple-element.67.refs_7_), channel_id=1, source_target_pairs={{0,1},{1,2},{2,3},{3,4},{4,5},{5,6},{6,7},{7,8},{8,9},{9,10},{10,1... | collective-permute-start | bytes 786440 | tf_op jit(solution)/shard_map/ppermute | solution.py:337
  28.9 6.0 %collective-permute-start.7 = (f32[4,64,256]{2,1,0:T(8,128)S(1)}, f32[4,64,256]{2,1,0:T(8,128)S(1)}, u32[]{:S(2)}, u32[]{:S(2)}) collective-permute-start(f32[4,64,256]{2,1,0:T(8,128)S(1)} %get-tuple-element.66.refs_6_), channel_id=1, source_target_pairs={{0,1},{1,2},{2,3},{3,4},{4,5},{5,6},{6,7},{7,8},{8,9},{9,10},{10,1... | collective-permute-start | bytes 786440 | tf_op jit(solution)/shard_map/ppermute | solution.py:337
  32.2 5.8 %collective-permute-start.5 = (f32[4,64,256]{2,1,0:T(8,128)S(1)}, f32[4,64,256]{2,1,0:T(8,128)S(1)}, u32[]{:S(2)}, u32[]{:S(2)}) collective-permute-start(f32[4,64,256]{2,1,0:T(8,128)S(1)} %get-tuple-element.65.refs_5_), channel_id=1, source_target_pairs={{0,1},{1,2},{2,3},{3,4},{4,5},{5,6},{6,7},{7,8},{8,9},{9,10},{10,1... | collective-permute-start | bytes 786440 | tf_op jit(solution)/shard_map/ppermute | solution.py:337
  34.6 6.3 %collective-permute-start.3 = (f32[4,64,256]{2,1,0:T(8,128)S(1)}, f32[4,64,256]{2,1,0:T(8,128)S(1)}, u32[]{:S(2)}, u32[]{:S(2)}) collective-permute-start(f32[4,64,256]{2,1,0:T(8,128)S(1)} %get-tuple-element.64.refs_4_), channel_id=1, source_target_pairs={{0,1},{1,2},{2,3},{3,4},{4,5},{5,6},{6,7},{7,8},{8,9},{9,10},{10,1... | collective-permute-start | bytes 786440 | tf_op jit(solution)/shard_map/ppermute | solution.py:337
  34.9 10.6 %collective-permute-start.10 = (f32[4,64,256]{2,1,0:T(8,128)S(1)}, f32[4,64,256]{2,1,0:T(8,128)S(1)}, u32[]{:S(2)}, u32[]{:S(2)}) collective-permute-start(f32[4,64,256]{2,1,0:T(8,128)S(1)} %collective-permute-done.9.refs_3_.refs_4_.refs_5_.refs_6_.refs_7_), channel_id=1, source_target_pairs={{0,1},{1,2},{2,3},{3,4},{4,5},{5,6},{6,7},{7,8},{8,9},{9,10},{10,1... | collective-permute-start | bytes 786440 | tf_op jit(solution)/shard_map/ppermute | solution.py:337
  34.9 15.7 %collective-permute-start.8 = (f32[4,64,256]{2,1,0:T(8,128)S(1)}, f32[4,64,256]{2,1,0:T(8,128)S(1)}, u32[]{:S(2)}, u32[]{:S(2)}) collective-permute-start(f32[4,64,256]{2,1,0:T(8,128)S(1)} %collective-permute-done.7.refs_2_.refs_3_.refs_4_.refs_5_.refs_6_), channel_id=1, source_target_pairs={{0,1},{1,2},{2,3},{3,4},{4,5},{5,6},{6,7},{7,8},{8,9},{9,10},{10,1... | collective-permute-start | bytes 786440 | tf_op jit(solution)/shard_map/ppermute | solution.py:337
  38.1 15.8 %collective-permute-start.6 = (f32[4,64,256]{2,1,0:T(8,128)S(1)}, f32[4,64,256]{2,1,0:T(8,128)S(1)}, u32[]{:S(2)}, u32[]{:S(2)}) collective-permute-start(f32[4,64,256]{2,1,0:T(8,128)S(1)} %collective-permute-done.5.refs_1_.refs_2_.refs_3_.refs_4_.refs_5_), channel_id=1, source_target_pairs={{0,1},{1,2},{2,3},{3,4},{4,5},{5,6},{6,7},{7,8},{8,9},{9,10},{10,1... | collective-permute-start | bytes 786440 | tf_op jit(solution)/shard_map/ppermute | solution.py:337
  40.9 16.6 %collective-permute-start.4 = (f32[4,64,256]{2,1,0:T(8,128)S(1)}, f32[4,64,256]{2,1,0:T(8,128)S(1)}, u32[]{:S(2)}, u32[]{:S(2)}) collective-permute-start(f32[4,64,256]{2,1,0:T(8,128)S(1)} %collective-permute-done.3.refs_0_.refs_1_.refs_2_.refs_3_.refs_4_), channel_id=1, source_target_pairs={{0,1},{1,2},{2,3},{3,4},{4,5},{5,6},{6,7},{7,8},{8,9},{9,10},{10,1... | collective-permute-start | bytes 786440 | tf_op jit(solution)/shard_map/ppermute | solution.py:337
  47.7 12.1 %collective-permute-start.17 = (f32[4,64,256]{2,1,0:T(8,128)S(1)}, f32[4,64,256]{2,1,0:T(8,128)S(1)}, u32[]{:S(2)}, u32[]{:S(2)}) collective-permute-start(f32[4,64,256]{2,1,0:T(8,128)S(1)} %get-tuple-element.76.refs_7_), channel_id=1, source_target_pairs={{0,1},{1,2},{2,3},{3,4},{4,5},{5,6},{6,7},{7,8},{8,9},{9,10},{10,1... | collective-permute-start | bytes 786440 | tf_op jit(solution)/shard_map/ppermute | solution.py:337
  53.8 7.1 %collective-permute-start.15 = (f32[4,64,256]{2,1,0:T(8,128)S(1)}, f32[4,64,256]{2,1,0:T(8,128)S(1)}, u32[]{:S(2)}, u32[]{:S(2)}) collective-permute-start(f32[4,64,256]{2,1,0:T(8,128)S(1)} %get-tuple-element.75.refs_6_), channel_id=1, source_target_pairs={{0,1},{1,2},{2,3},{3,4},{4,5},{5,6},{6,7},{7,8},{8,9},{9,10},{10,1... | collective-permute-start | bytes 786440 | tf_op jit(solution)/shard_map/ppermute | solution.py:337
  57.1 5.8 %collective-permute-start.13 = (f32[4,64,256]{2,1,0:T(8,128)S(1)}, f32[4,64,256]{2,1,0:T(8,128)S(1)}, u32[]{:S(2)}, u32[]{:S(2)}) collective-permute-start(f32[4,64,256]{2,1,0:T(8,128)S(1)} %get-tuple-element.74.refs_5_), channel_id=1, source_target_pairs={{0,1},{1,2},{2,3},{3,4},{4,5},{5,6},{6,7},{7,8},{8,9},{9,10},{10,1... | collective-permute-start | bytes 786440 | tf_op jit(solution)/shard_map/ppermute | solution.py:337
  59.8 5.9 %collective-permute-start.11 = (f32[4,64,256]{2,1,0:T(8,128)S(1)}, f32[4,64,256]{2,1,0:T(8,128)S(1)}, u32[]{:S(2)}, u32[]{:S(2)}) collective-permute-start(f32[4,64,256]{2,1,0:T(8,128)S(1)} %get-tuple-element.73.refs_4_), channel_id=1, source_target_pairs={{0,1},{1,2},{2,3},{3,4},{4,5},{5,6},{6,7},{7,8},{8,9},{9,10},{10,1... | collective-permute-start | bytes 786440 | tf_op jit(solution)/shard_map/ppermute | solution.py:337
  59.9 10.6 %collective-permute-start.18 = (f32[4,64,256]{2,1,0:T(8,128)S(1)}, f32[4,64,256]{2,1,0:T(8,128)S(1)}, u32[]{:S(2)}, u32[]{:S(2)}) collective-permute-start(f32[4,64,256]{2,1,0:T(8,128)S(1)} %collective-permute-done.17.refs_3_.refs_4_.refs_5_.refs_6_.refs_7_), channel_id=1, source_target_pairs={{0,1},{1,2},{2,3},{3,4},{4,5},{5,6},{6,7},{7,8},{8,9},{9,10},{10,1... | collective-permute-start | bytes 786440 | tf_op jit(solution)/shard_map/ppermute | solution.py:337
  60.9 15.5 %collective-permute-start.16 = (f32[4,64,256]{2,1,0:T(8,128)S(1)}, f32[4,64,256]{2,1,0:T(8,128)S(1)}, u32[]{:S(2)}, u32[]{:S(2)}) collective-permute-start(f32[4,64,256]{2,1,0:T(8,128)S(1)} %collective-permute-done.15.refs_2_.refs_3_.refs_4_.refs_5_.refs_6_), channel_id=1, source_target_pairs={{0,1},{1,2},{2,3},{3,4},{4,5},{5,6},{6,7},{7,8},{8,9},{9,10},{10,1... | collective-permute-start | bytes 786440 | tf_op jit(solution)/shard_map/ppermute | solution.py:337
  62.9 16.7 %collective-permute-start.14 = (f32[4,64,256]{2,1,0:T(8,128)S(1)}, f32[4,64,256]{2,1,0:T(8,128)S(1)}, u32[]{:S(2)}, u32[]{:S(2)}) collective-permute-start(f32[4,64,256]{2,1,0:T(8,128)S(1)} %collective-permute-done.13.refs_1_.refs_2_.refs_3_.refs_4_.refs_5_), channel_id=1, source_target_pairs={{0,1},{1,2},{2,3},{3,4},{4,5},{5,6},{6,7},{7,8},{8,9},{9,10},{10,1... | collective-permute-start | bytes 786440 | tf_op jit(solution)/shard_map/ppermute | solution.py:337
  65.7 17.2 %collective-permute-start.12 = (f32[4,64,256]{2,1,0:T(8,128)S(1)}, f32[4,64,256]{2,1,0:T(8,128)S(1)}, u32[]{:S(2)}, u32[]{:S(2)}) collective-permute-start(f32[4,64,256]{2,1,0:T(8,128)S(1)} %collective-permute-done.11.refs_0_.refs_1_.refs_2_.refs_3_.refs_4_), channel_id=1, source_target_pairs={{0,1},{1,2},{2,3},{3,4},{4,5},{5,6},{6,7},{7,8},{8,9},{9,10},{10,1... | collective-permute-start | bytes 786440 | tf_op jit(solution)/shard_map/ppermute | solution.py:337
  72.7 12.5 %collective-permute-start.25 = (f32[4,64,256]{2,1,0:T(8,128)S(1)}, f32[4,64,256]{2,1,0:T(8,128)S(1)}, u32[]{:S(2)}, u32[]{:S(2)}) collective-permute-start(f32[4,64,256]{2,1,0:T(8,128)S(1)} %get-tuple-element.85.refs_7_), channel_id=1, source_target_pairs={{0,1},{1,2},{2,3},{3,4},{4,5},{5,6},{6,7},{7,8},{8,9},{9,10},{10,1... | collective-permute-start | bytes 786440 | tf_op jit(solution)/shard_map/ppermute | solution.py:337
  79.5 7.1 %collective-permute-start.23 = (f32[4,64,256]{2,1,0:T(8,128)S(1)}, f32[4,64,256]{2,1,0:T(8,128)S(1)}, u32[]{:S(2)}, u32[]{:S(2)}) collective-permute-start(f32[4,64,256]{2,1,0:T(8,128)S(1)} %get-tuple-element.84.refs_6_), channel_id=1, source_target_pairs={{0,1},{1,2},{2,3},{3,4},{4,5},{5,6},{6,7},{7,8},{8,9},{9,10},{10,1... | collective-permute-start | bytes 786440 | tf_op jit(solution)/shard_map/ppermute | solution.py:337
  82.8 5.8 %collective-permute-start.21 = (f32[4,64,256]{2,1,0:T(8,128)S(1)}, f32[4,64,256]{2,1,0:T(8,128)S(1)}, u32[]{:S(2)}, u32[]{:S(2)}) collective-permute-start(f32[4,64,256]{2,1,0:T(8,128)S(1)} %get-tuple-element.83.refs_5_), channel_id=1, source_target_pairs={{0,1},{1,2},{2,3},{3,4},{4,5},{5,6},{6,7},{7,8},{8,9},{9,10},{10,1... | collective-permute-start | bytes 786440 | tf_op jit(solution)/shard_map/ppermute | solution.py:337
  85.2 6.3 %collective-permute-start.19 = (f32[4,64,256]{2,1,0:T(8,128)S(1)}, f32[4,64,256]{2,1,0:T(8,128)S(1)}, u32[]{:S(2)}, u32[]{:S(2)}) collective-permute-start(f32[4,64,256]{2,1,0:T(8,128)S(1)} %get-tuple-element.82.refs_4_), channel_id=1, source_target_pairs={{0,1},{1,2},{2,3},{3,4},{4,5},{5,6},{6,7},{7,8},{8,9},{9,10},{10,1... | collective-permute-start | bytes 786440 | tf_op jit(solution)/shard_map/ppermute | solution.py:337
  85.3 10.7 %collective-permute-start.26 = (f32[4,64,256]{2,1,0:T(8,128)S(1)}, f32[4,64,256]{2,1,0:T(8,128)S(1)}, u32[]{:S(2)}, u32[]{:S(2)}) collective-permute-start(f32[4,64,256]{2,1,0:T(8,128)S(1)} %collective-permute-done.25.refs_3_.refs_4_.refs_5_.refs_6_.refs_7_), channel_id=1, source_target_pairs={{0,1},{1,2},{2,3},{3,4},{4,5},{5,6},{6,7},{7,8},{8,9},{9,10},{10,1... | collective-permute-start | bytes 786440 | tf_op jit(solution)/shard_map/ppermute | solution.py:337
  86.7 11.5 %collective-permute-start.24 = (f32[4,64,256]{2,1,0:T(8,128)S(1)}, f32[4,64,256]{2,1,0:T(8,128)S(1)}, u32[]{:S(2)}, u32[]{:S(2)}) collective-permute-start(f32[4,64,256]{2,1,0:T(8,128)S(1)} %collective-permute-done.23.refs_2_.refs_3_.refs_4_.refs_5_.refs_6_), channel_id=1, source_target_pairs={{0,1},{1,2},{2,3},{3,4},{4,5},{5,6},{6,7},{7,8},{8,9},{9,10},{10,1... | collective-permute-start | bytes 786440 | tf_op jit(solution)/shard_map/ppermute | solution.py:337
  88.7 16.8 %collective-permute-start.22 = (f32[4,64,256]{2,1,0:T(8,128)S(1)}, f32[4,64,256]{2,1,0:T(8,128)S(1)}, u32[]{:S(2)}, u32[]{:S(2)}) collective-permute-start(f32[4,64,256]{2,1,0:T(8,128)S(1)} %collective-permute-done.21.refs_1_.refs_2_.refs_3_.refs_4_.refs_5_), channel_id=1, source_target_pairs={{0,1},{1,2},{2,3},{3,4},{4,5},{5,6},{6,7},{7,8},{8,9},{9,10},{10,1... | collective-permute-start | bytes 786440 | tf_op jit(solution)/shard_map/ppermute | solution.py:337
  91.5 17.2 %collective-permute-start.20 = (f32[4,64,256]{2,1,0:T(8,128)S(1)}, f32[4,64,256]{2,1,0:T(8,128)S(1)}, u32[]{:S(2)}, u32[]{:S(2)}) collective-permute-start(f32[4,64,256]{2,1,0:T(8,128)S(1)} %collective-permute-done.19.refs_0_.refs_1_.refs_2_.refs_3_.refs_4_), channel_id=1, source_target_pairs={{0,1},{1,2},{2,3},{3,4},{4,5},{5,6},{6,7},{7,8},{8,9},{9,10},{10,1... | collective-permute-start | bytes 786440 | tf_op jit(solution)/shard_map/ppermute | solution.py:337
  101.4 9.7 %collective-permute-start.29 = (f32[4,64,256]{2,1,0:T(8,128)S(1)}, f32[4,64,256]{2,1,0:T(8,128)S(1)}, u32[]{:S(2)}, u32[]{:S(2)}) collective-permute-start(f32[4,64,256]{2,1,0:T(8,128)S(1)} %get-tuple-element.93), channel_id=1, source_target_pairs={{0,13},{1,2},{2,15},{3,0},{4,1},{5,6},{6,3},{7,4},{8,5},{9,10},{10... | collective-permute-start | bytes 786440 | tf_op jit(solution)/shard_map/ppermute | solution.py:337
  105.2 6.7 %collective-permute-start.30 = (f32[4,64,256]{2,1,0:T(8,128)S(1)}, f32[4,64,256]{2,1,0:T(8,128)S(1)}, u32[]{:S(2)}, u32[]{:S(2)}) collective-permute-start(f32[4,64,256]{2,1,0:T(8,128)S(1)} %get-tuple-element.94), channel_id=1, source_target_pairs={{0,13},{1,2},{2,15},{3,0},{4,1},{5,6},{6,3},{7,4},{8,5},{9,10},{10... | collective-permute-start | bytes 786440 | tf_op jit(solution)/shard_map/ppermute | solution.py:337
  111.0 13.8 %collective-permute-start.27 = (f32[4,64,256]{2,1,0:T(8,128)S(1)}, f32[4,64,256]{2,1,0:T(8,128)S(1)}, u32[]{:S(2)}, u32[]{:S(2)}) collective-permute-start(f32[4,64,256]{2,1,0:T(8,128)S(1)} %get-tuple-element.91), channel_id=1, source_target_pairs={{0,13},{1,14},{2,15},{3,0},{4,1},{5,2},{6,3},{7,4},{8,5},{9,6},{10... | collective-permute-start | bytes 786440 | tf_op jit(solution)/shard_map/ppermute | solution.py:337
  111.9 10.1 %collective-permute-start.31 = (f32[4,64,256]{2,1,0:T(8,128)S(1)}, f32[4,64,256]{2,1,0:T(8,128)S(1)}, u32[]{:S(2)}, u32[]{:S(2)}) collective-permute-start(f32[4,64,256]{2,1,0:T(8,128)S(1)} %collective-permute-done.29), channel_id=1, source_target_pairs={{0,0},{1,1},{2,14},{3,3},{4,4},{5,5},{6,2},{7,7},{8,8},{9,9},{10,6... | collective-permute-start | bytes 786440 | tf_op jit(solution)/shard_map/ppermute | solution.py:337
  114.2 10.5 %collective-permute-start.32 = (f32[4,64,256]{2,1,0:T(8,128)S(1)}, f32[4,64,256]{2,1,0:T(8,128)S(1)}, u32[]{:S(2)}, u32[]{:S(2)}) collective-permute-start(f32[4,64,256]{2,1,0:T(8,128)S(1)} %collective-permute-done.30), channel_id=1, source_target_pairs={{0,0},{1,1},{2,14},{3,3},{4,4},{5,5},{6,2},{7,7},{8,8},{9,9},{10,6... | collective-permute-start | bytes 786440 | tf_op jit(solution)/shard_map/ppermute | solution.py:337
  117.7 10.2 %collective-permute-start.28 = (f32[4,64,256]{2,1,0:T(8,128)S(1)}, f32[4,64,256]{2,1,0:T(8,128)S(1)}, u32[]{:S(2)}, u32[]{:S(2)}) collective-permute-start(f32[4,64,256]{2,1,0:T(8,128)S(1)} %get-tuple-element.92), channel_id=1, source_target_pairs={{0,13},{1,14},{2,15},{3,0},{4,1},{5,2},{6,3},{7,4},{8,5},{9,6},{10... | collective-permute-start | bytes 786440 | tf_op jit(solution)/shard_map/ppermute | solution.py:337

commit v4 on v2

--- a/solution.py
+++ b/solution.py
@@ -91,7 +91,8 @@
         depth_f[r] = rolled(ahead, r, PLANES * GROUP).astype(BF16)
         depth_a[r] = rolled(back, r, PLANES * GROUP).astype(BF16)
 
-    loop(ranks, depth)
+    for r in range(ranks):
+        depth(r)
     i, j = iota(square, 0), iota(square, 1)
     near = jnp.abs(j - i) <= margin
     placed(normal(col_taps), lambda k: (margin - k) & (TILE - 1), ahead)
@@ -101,7 +102,8 @@
         col_f[r] = jnp.where(near, rolled(ahead, r, TILE), 0.0).astype(BF16)
         col_a[r] = jnp.where(near, rolled(back, r, TILE), 0.0).astype(BF16)
 
-    loop(ranks, col)
+    for r in range(ranks):
+        col(r)
     close = near & ((i >> 6) == (j >> 6))
     order_columns = ROWS * ((j >> 3) & (QUAD - 1)) + GROUP * (j >> 5) + (j & (GROUP - 1))
     order_columns = (i == order_columns).astype(F32).astype(BF16)
@@ -114,7 +116,8 @@
         band = jnp.where(close, rolled(back, r, TILE), 0.0).astype(BF16)
         row_a[r] = dot(band, order_columns).astype(BF16)
 
-    loop(ranks, row)
+    for r in range(ranks):
+        row(r)
     for copy in copies:
         copy.wait()
 
@@ -227,7 +230,7 @@
     )(*arrays, *shared, *ops)
 
 
-def upper_ratio(own, above, shared, ops):
+def upper_ratio(own, above, shared, ops, unrolled):
     parts = len(own) + len(above)
     tiles = PLANES // QUAD
 
@@ -236,7 +239,7 @@
         live = ends[1]
         scales = [None] * len(own) + [live] * len(above)
         cells = window([(ref, 0) for ref in refs[:parts]], scales)
-        depth_pass(cells, depth, PLANES, spread)
+        (depth_whole if unrolled else depth_pass)(cells, depth, PLANES, spread)
 
         def pair(i):
             for t in (i,):
@@ -246,7 +249,14 @@
                 seen = slab[pl.ds(PLANES + t * QUAD, QUAD)].astype(F32)
                 ratio[planes] = seen / col_pass(mixed, col, t)
 
-        loop(tiles, pair)
+        if unrolled:
+            for t in range(tiles):
+                row_whole(spread, row, mixed, t)
+            for t in range(tiles):
+                seen = slab[PLANES + t * QUAD : PLANES + (t + 1) * QUAD].astype(F32)
+                ratio[t * QUAD : (t + 1) * QUAD] = seen / col_whole(mixed, col, t)
+        else:
+            loop(tiles, pair)
         ratio[HALF:] = ratio[HALF:] * live
 
     ranks = ops[0].shape[0]
@@ -332,7 +342,7 @@
                 pairs.append((i, (i + way) % count))
         return lax.ppermute(cells, "view", pairs)
 
-    above = [send(start_estimate, -1)]
+    above = [send(start_estimate, -1, skip=(0,))]
     place = jnp.stack([lax.axis_index("view"), count]).astype(jnp.int32)
     ops, slabs, ends = build(
         place, view_order, psf_ranks, rank_weight, depth_taps, row_taps, col_taps, images
@@ -346,7 +356,7 @@
     for step in range(STEPS):
         last = step == STEPS - 1
         shared = [slabs[step], ends[step]]
-        ratio_up = upper_ratio([own_lo, own_hi], above, shared, ops)
+        ratio_up = upper_ratio([own_lo, own_hi], above, shared, ops, step == 0)
         ratio_mid, hi = half_update(HALF, [below_hi], [own_lo, own_hi], [ratio_up], shared, ops)
         next_hi = send(hi, 1 - STEPS, (1, 1)) if last else send(hi, 1)
         _, lo = half_update(

time: 127 us -> 125 us (0.984)
  Pallas kernels: 50.7 us -> 46.9 us
  waiting for transfers between devices: 46.5 us -> 48.5 us
    pallas_call x1, Pallas kernels: 4.57 us -> 2.52 us  [build(): pl.pallas_call(build_kernel, out_shape=[depth, depth] + [square] * 4 + [s...]
    ppermute x18, waiting for transfers between devices: 46.5 us -> 48.5 us  [send(): return lax.ppermute(cells, 'view', pairs)]
    pallas_call x12, Pallas kernels: 45.2 us -> 43.4 us  [call(): pl.pallas_call(kernel, out_shape=out, in_specs=[VMEM] * (len(arrays) + le...]
  transfers between devices with their start and end apart: 18 -> 18, of which waited for: 15 -> 15; matrix products, arithmetic and copies ran while one was open for 2% -> 2% of each run, Pallas kernels for 39% -> 37%
where the time goes in v4:
time: 125 us
  waiting for transfers between devices  48.5 us (39%)
  Pallas kernels  46.9 us (38%)
  starting transfers between devices  22.6 us (18%)
  local copies, waits for them, and re-layouts  6.38 us (5%)
    ppermute x18, waiting for transfers between devices, send(): return lax.ppermute(cells, 'view', pairs)  48.5 us
    pallas_call x12, Pallas kernels, call(): pl.pallas_call(kernel, out_shape=out, in_specs=[VMEM] * (len(arrays) + le...  43.4 us
    ppermute x18, starting transfers between devices, send(): return lax.ppermute(cells, 'view', pairs)  22.6 us
    unnamed x13, local copies, waits for them, and re-layouts  6.31 us
    pallas_call x1, Pallas kernels, build(): pl.pallas_call(build_kernel, out_shape=[depth, depth] + [square] * 4 + [s...  2.52 us
  transfers between devices with their start and end apart: 18, of which 15 were waited for; matrix products, arithmetic and copies ran while one was open for 2% of the time, Pallas kernels for 37%

profile of v4, /device:TPU:28, one launch (start us, length us, event | category | flops | bytes accessed | tf_op | source)
XLA Modules:
  0.0 124.8 jit_solution(15470440542776655241)
XLA Ops:
  0.0 1.9 %collective-permute-start = (f32[16,64,256]{2,1,0:T(8,128)}, f32[16,64,256]{2,1,0:T(8,128)S(1)}, u32[]{:S(2)}, u32[]{:S(2)}) collective-permute-start(f32[16,64,256]{2,1,0:T(8,128)} %param.9), channel_id=1, source_target_pairs={{1,0},{2,1},{3,2},{4,3},{5,4},{6,5},{7,6},{8,7},{9,8},{10,9},{11,1... | collective-permute-start | bytes 3145736 | tf_op jit(solution)/shard_map/ppermute | solution.py:343
  1.9 0.7 copy.9.depth_taps
  2.6 0.7 copy.10.row_taps
  3.3 0.7 copy.11.col_taps
  4.1 2.2 %copy-done = bf16[1,4,32,64,256]{4,3,2,1,0:T(8,128)(2,1)S(1)} copy-done((bf16[1,4,32,64,256]{4,3,2,1,0:T(8,128)(2,1)S(1)}, bf16[1,4,32,64,256]{4,3,2,1,0:T(8,128)(2,1)}, u32[]{:S(2)}) %copy-start) | copy-done | bytes 4194328
  6.3 0.7 copy-done.1
  7.0 0.7 copy-done.2
  7.7 0.7 copy-done.3
  8.3 2.5 %build.1 = (bf16[6,128,256]{2,1,0:T(8,128)(2,1)S(1)}, bf16[6,128,256]{2,1,0:T(8,128)(2,1)S(1)}, bf16[6,256,256]{2,1,0:T(8,128)(2,1)S(1)}, bf16[6,256,256]{2,1,0:...) custom-call(s32[2]{0:T(128)S(1)} %pad_add_fusion.place, ...), custom_call_target="tpu_custom_call" | custom-call | tf_op jit(solution)/shard_map/build/pallas_call | solution.py:131
  10.9 2.5 %collective-permute-start.2 = (f32[8,64,256]{2,1,0:T(8,128)S(1)}, f32[8,64,256]{2,1,0:T(8,128)S(1)}, u32[]{:S(2)}, u32[]{:S(2)}) collective-permute-start(f32[8,64,256]{2,1,0:T(8,128)S(1)} %get-tuple-element.36.refs_1_.refs_2_), channel_id=1, source_target_pairs={{0,1},{1,2},{2,3},{3,4},{4,5},{5,6},{6,7},{7,8},{8,9},{9,10},{10,1... | collective-permute-start | bytes 1572872 | tf_op jit(solution)/shard_map/ppermute | solution.py:343
  13.4 1.1 collective-permute-done.refs_2_
  14.5 1.9 %collective-permute-start.1 = (f32[8,64,256]{2,1,0:T(8,128)S(1)}, f32[8,64,256]{2,1,0:T(8,128)S(1)}, u32[]{:S(2)}, u32[]{:S(2)}) collective-permute-start(f32[8,64,256]{2,1,0:T(8,128)S(1)} %get-tuple-element.34.refs_0_.refs_1_.refs_2_), channel_id=1, source_target_pairs={{0,1},{1,2},{2,3},{3,4},{4,5},{5,6},{6,7},{7,8},{8,9},{9,10},{10,1... | collective-permute-start | bytes 1572872 | tf_op jit(solution)/shard_map/ppermute | solution.py:343
  16.4 2.7 %upper.4.refs_3_.refs_4_ = f32[16,64,256]{2,1,0:T(8,128)S(1)} custom-call(f32[8,64,256]{2,1,0:T(8,128)S(1)} %get-tuple-element.34.refs_0_.refs_1_.refs_2_, f32[8,64,256]{2,1,0:T(8,128)S(1)} %get-tuple-element.36.refs_1_.refs_2_, f32[16,64,256]{2,1,0:T(8,128)S(1)} %collective-permute-done.refs_2_, ...), custom_call_target="tpu_custom_call" | custom-call | flops 1048576 | bytes 1024 | tf_op jit(solution)/shard_map/upper/pallas_call | solution.py:221
  19.1 2.3 %collective-permute-done.2.refs_0_.refs_1_ = f32[8,64,256]{2,1,0:T(8,128)S(1)} collective-permute-done((f32[8,64,256]{2,1,0:T(8,128)S(1)}, f32[8,64,256]{2,1,0:T(8,128)S(1)}, u32[]{:S(2)}, u32[]{:S(2)}) %collective-permute-start.2) | collective-permute-done | bytes 524320 | tf_op jit(solution)/shard_map/ppermute | solution.py:343
  21.4 3.4 %half.8 = (f32[8,64,256]{2,1,0:T(8,128)S(1)}, f32[8,64,256]{2,1,0:T(8,128)S(1)}) custom-call(f32[8,64,256]{2,1,0:T(8,128)S(1)} %collective-permute-done.2.refs_0_.refs_1_, f32[8,64,256]{2,1,0:T(8,128)S(1)} %get-tuple-element.34.refs_0_.refs_1_.refs_2_, f32[8,64,256]{2,1,0:T(8,128)S(1)} %get-tuple-element.36.refs_1_.refs_2_, ...), custom_call_target="tpu_custom_call" | custom-call | flops 1048576 | bytes 1024 | tf_op jit(solution)/shard_map/half/pallas_call | solution.py:221
  24.9 2.1 %collective-permute-done.1.refs_0_ = f32[8,64,256]{2,1,0:T(8,128)S(1)} collective-permute-done((f32[8,64,256]{2,1,0:T(8,128)S(1)}, f32[8,64,256]{2,1,0:T(8,128)S(1)}, u32[]{:S(2)}, u32[]{:S(2)}) %collective-permute-start.1) | collective-permute-done | bytes 524320 | tf_op jit(solution)/shard_map/ppermute | solution.py:343
  27.0 3.5 %half.9 = (f32[8,64,256]{2,1,0:T(8,128)}, f32[8,64,256]{2,1,0:T(8,128)S(1)}) custom-call(f32[8,64,256]{2,1,0:T(8,128)S(1)} %collective-permute-done.1.refs_0_, f32[8,64,256]{2,1,0:T(8,128)S(1)} %collective-permute-done.2.refs_0_.refs_1_, f32[8,64,256]{2,1,0:T(8,128)S(1)} %get-tuple-element.34.refs_0_.refs_1_.refs_2_, ...), custom_call_target="tpu_custom_call" | custom-call | flops 1048576 | bytes 1024 | tf_op jit(solution)/shard_map/half/pallas_call | solution.py:221
  30.6 2.9 %collective-permute-done.5.refs_1_.refs_2_ = f32[8,64,256]{2,1,0:T(8,128)S(1)} collective-permute-done((f32[8,64,256]{2,1,0:T(8,128)S(1)}, f32[8,64,256]{2,1,0:T(8,128)S(1)}, u32[]{:S(2)}, u32[]{:S(2)}) %collective-permute-start.5) | collective-permute-done | bytes 524320 | tf_op jit(solution)/shard_map/ppermute | solution.py:343
  33.5 5.7 %collective-permute-done.3.refs_0_.refs_1_.refs_2_ = f32[8,64,256]{2,1,0:T(8,128)S(1)} collective-permute-done((f32[8,64,256]{2,1,0:T(8,128)S(1)}, f32[8,64,256]{2,1,0:T(8,128)S(1)}, u32[]{:S(2)}, u32[]{:S(2)}) %collective-permute-start.3) | collective-permute-done | bytes 524320 | tf_op jit(solution)/shard_map/ppermute | solution.py:343
  39.2 4.4 %upper.5.refs_3_.refs_4_ = f32[16,64,256]{2,1,0:T(8,128)S(1)} custom-call(f32[8,64,256]{2,1,0:T(8,128)S(1)} %collective-permute-done.3.refs_0_.refs_1_.refs_2_, f32[8,64,256]{2,1,0:T(8,128)S(1)} %collective-permute-done.5.refs_1_.refs_2_, f32[8,64,256]{2,1,0:T(8,128)S(1)} %get-tuple-element.45.refs_2_, f32[8,64,256]{2,1,0:T(8,128)S(1)} %get-tuple-element.46.refs_3_, ...), custom_call_target="tpu_custom_call" | custom-call | flops 1048576 | bytes 1024 | tf_op jit(solution)/shard_map/upper/pallas_call | solution.py:221
  43.6 1.2 collective-permute-done.6.refs_0_.refs_1_
  44.8 3.4 %half.10 = (f32[8,64,256]{2,1,0:T(8,128)S(1)}, f32[8,64,256]{2,1,0:T(8,128)S(1)}) custom-call(f32[8,64,256]{2,1,0:T(8,128)S(1)} %collective-permute-done.6.refs_0_.refs_1_, f32[8,64,256]{2,1,0:T(8,128)S(1)} %collective-permute-done.3.refs_0_.refs_1_.refs_2_, f32[8,64,256]{2,1,0:T(8,128)S(1)} %collective-permute-done.5.refs_1_.refs_2_, ...), custom_call_target="tpu_custom_call" | custom-call | flops 1048576 | bytes 1024 | tf_op jit(solution)/shard_map/half/pallas_call | solution.py:221
  48.2 1.2 collective-permute-start.9
  49.4 1.0 collective-permute-done.4.refs_0_
  50.4 3.5 %half.11 = (f32[8,64,256]{2,1,0:T(8,128)}, f32[8,64,256]{2,1,0:T(8,128)S(1)}) custom-call(f32[8,64,256]{2,1,0:T(8,128)S(1)} %collective-permute-done.4.refs_0_, f32[8,64,256]{2,1,0:T(8,128)S(1)} %collective-permute-done.6.refs_0_.refs_1_, f32[8,64,256]{2,1,0:T(8,128)S(1)} %collective-permute-done.3.refs_0_.refs_1_.refs_2_, ...), custom_call_target="tpu_custom_call" | custom-call | flops 1048576 | bytes 1024 | tf_op jit(solution)/shard_map/half/pallas_call | solution.py:221
  53.9 0.3 collective-permute-start.7
  54.2 2.7 %collective-permute-done.9.refs_1_.refs_2_ = f32[8,64,256]{2,1,0:T(8,128)S(1)} collective-permute-done((f32[8,64,256]{2,1,0:T(8,128)S(1)}, f32[8,64,256]{2,1,0:T(8,128)S(1)}, u32[]{:S(2)}, u32[]{:S(2)}) %collective-permute-start.9) | collective-permute-done | bytes 524320 | tf_op jit(solution)/shard_map/ppermute | solution.py:343
  56.9 5.7 %collective-permute-done.7.refs_0_.refs_1_.refs_2_ = f32[8,64,256]{2,1,0:T(8,128)S(1)} collective-permute-done((f32[8,64,256]{2,1,0:T(8,128)S(1)}, f32[8,64,256]{2,1,0:T(8,128)S(1)}, u32[]{:S(2)}, u32[]{:S(2)}) %collective-permute-start.7) | collective-permute-done | bytes 524320 | tf_op jit(solution)/shard_map/ppermute | solution.py:343
  62.5 4.4 %upper.6.refs_3_.refs_4_ = f32[16,64,256]{2,1,0:T(8,128)S(1)} custom-call(f32[8,64,256]{2,1,0:T(8,128)S(1)} %collective-permute-done.7.refs_0_.refs_1_.refs_2_, f32[8,64,256]{2,1,0:T(8,128)S(1)} %collective-permute-done.9.refs_1_.refs_2_, f32[8,64,256]{2,1,0:T(8,128)S(1)} %get-tuple-element.50.refs_2_, f32[8,64,256]{2,1,0:T(8,128)S(1)} %get-tuple-element.51.refs_3_, ...), custom_call_target="tpu_custom_call" | custom-call | flops 1048576 | bytes 1024 | tf_op jit(solution)/shard_map/upper/pallas_call | solution.py:221
  67.0 1.2 collective-permute-done.10.refs_0_.refs_1_
  68.1 3.4 %half.12 = (f32[8,64,256]{2,1,0:T(8,128)S(1)}, f32[8,64,256]{2,1,0:T(8,128)S(1)}) custom-call(f32[8,64,256]{2,1,0:T(8,128)S(1)} %collective-permute-done.10.refs_0_.refs_1_, f32[8,64,256]{2,1,0:T(8,128)S(1)} %collective-permute-done.7.refs_0_.refs_1_.refs_2_, f32[8,64,256]{2,1,0:T(8,128)S(1)} %collective-permute-done.9.refs_1_.refs_2_, ...), custom_call_target="tpu_custom_call" | custom-call | flops 1048576 | bytes 1024 | tf_op jit(solution)/shard_map/half/pallas_call | solution.py:221
  71.6 4.2 %collective-permute-start.13 = (f32[8,64,256]{2,1,0:T(8,128)S(1)}, f32[8,64,256]{2,1,0:T(8,128)S(1)}, u32[]{:S(2)}, u32[]{:S(2)}) collective-permute-start(f32[8,64,256]{2,1,0:T(8,128)S(1)} %get-tuple-element.56.refs_3_), channel_id=1, source_target_pairs={{0,1},{1,2},{2,3},{3,4},{4,5},{5,6},{6,7},{7,8},{8,9},{9,10},{10,1... | collective-permute-start | bytes 1572872 | tf_op jit(solution)/shard_map/ppermute | solution.py:343
  75.8 3.4 %half.13 = (f32[8,64,256]{2,1,0:T(8,128)}, f32[8,64,256]{2,1,0:T(8,128)S(1)}) custom-call(f32[8,64,256]{2,1,0:T(8,128)S(1)} %collective-permute-done.8.refs_0_, f32[8,64,256]{2,1,0:T(8,128)S(1)} %collective-permute-done.10.refs_0_.refs_1_, f32[8,64,256]{2,1,0:T(8,128)S(1)} %collective-permute-done.7.refs_0_.refs_1_.refs_2_, ...), custom_call_target="tpu_custom_call" | custom-call | flops 1048576 | bytes 1024 | tf_op jit(solution)/shard_map/half/pallas_call | solution.py:221
  79.3 1.2 collective-permute-start.11
  80.5 2.6 %collective-permute-start.14 = (f32[8,64,256]{2,1,0:T(8,128)S(1)}, f32[8,64,256]{2,1,0:T(8,128)S(1)}, u32[]{:S(2)}, u32[]{:S(2)}) collective-permute-start(f32[8,64,256]{2,1,0:T(8,128)S(1)} %collective-permute-done.13.refs_1_.refs_2_), channel_id=1, source_target_pairs={{0,1},{1,2},{2,3},{3,4},{4,5},{5,6},{6,7},{7,8},{8,9},{9,10},{10,1... | collective-permute-start | bytes 1572872 | tf_op jit(solution)/shard_map/ppermute | solution.py:343
  83.1 4.8 %collective-permute-done.11.refs_0_.refs_1_.refs_2_ = f32[8,64,256]{2,1,0:T(8,128)S(1)} collective-permute-done((f32[8,64,256]{2,1,0:T(8,128)S(1)}, f32[8,64,256]{2,1,0:T(8,128)S(1)}, u32[]{:S(2)}, u32[]{:S(2)}) %collective-permute-start.11) | collective-permute-done | bytes 524320 | tf_op jit(solution)/shard_map/ppermute | solution.py:343
  87.9 0.8 collective-permute-start.12
  88.7 4.4 %upper.7.refs_3_.refs_4_ = f32[16,64,256]{2,1,0:T(8,128)S(1)} custom-call(f32[8,64,256]{2,1,0:T(8,128)S(1)} %collective-permute-done.11.refs_0_.refs_1_.refs_2_, f32[8,64,256]{2,1,0:T(8,128)S(1)} %collective-permute-done.13.refs_1_.refs_2_, f32[8,64,256]{2,1,0:T(8,128)S(1)} %get-tuple-element.55.refs_2_, f32[8,64,256]{2,1,0:T(8,128)S(1)} %get-tuple-element.56.refs_3_, ...), custom_call_target="tpu_custom_call" | custom-call | flops 1048576 | bytes 1024 | tf_op jit(solution)/shard_map/upper/pallas_call | solution.py:221
  93.2 0.4 collective-permute-done.14.refs_0_.refs_1_
  93.5 3.4 %half.14 = (f32[8,64,256]{2,1,0:T(8,128)S(1)}, f32[8,64,256]{2,1,0:T(8,128)S(1)}) custom-call(f32[8,64,256]{2,1,0:T(8,128)S(1)} %collective-permute-done.14.refs_0_.refs_1_, f32[8,64,256]{2,1,0:T(8,128)S(1)} %collective-permute-done.11.refs_0_.refs_1_.refs_2_, f32[8,64,256]{2,1,0:T(8,128)S(1)} %collective-permute-done.13.refs_1_.refs_2_, ...), custom_call_target="tpu_custom_call" | custom-call | flops 1048576 | bytes 1024 | tf_op jit(solution)/shard_map/half/pallas_call | solution.py:221
  97.0 3.2 %collective-permute-start.16 = (f32[8,64,256]{2,1,0:T(8,128)S(1)}, f32[8,64,256]{2,1,0:T(8,128)S(1)}, u32[]{:S(2)}, u32[]{:S(2)}) collective-permute-start(f32[8,64,256]{2,1,0:T(8,128)S(1)} %get-tuple-element.61), channel_id=1, source_target_pairs={{0,13},{1,2},{2,15},{3,0},{4,1},{5,6},{6,3},{7,4},{8,5},{9,10},{10... | collective-permute-start | bytes 1572872 | tf_op jit(solution)/shard_map/ppermute | solution.py:343
  100.1 3.4 %half.15 = (f32[8,64,256]{2,1,0:T(8,128)}, f32[8,64,256]{2,1,0:T(8,128)S(1)}) custom-call(f32[8,64,256]{2,1,0:T(8,128)S(1)} %collective-permute-done.12.refs_0_, f32[8,64,256]{2,1,0:T(8,128)S(1)} %collective-permute-done.14.refs_0_.refs_1_, f32[8,64,256]{2,1,0:T(8,128)S(1)} %collective-permute-done.11.refs_0_.refs_1_.refs_2_, ...), custom_call_target="tpu_custom_call" | custom-call | flops 1048576 | bytes 1024 | tf_op jit(solution)/shard_map/half/pallas_call | solution.py:221
  103.6 0.2 collective-permute-start.15
  103.8 3.0 %collective-permute-done.16 = f32[8,64,256]{2,1,0:T(8,128)S(1)} collective-permute-done((f32[8,64,256]{2,1,0:T(8,128)S(1)}, f32[8,64,256]{2,1,0:T(8,128)S(1)}, u32[]{:S(2)}, u32[]{:S(2)}) %collective-permute-start.16) | collective-permute-done | bytes 524320 | tf_op jit(solution)/shard_map/ppermute | solution.py:343
  106.8 2.3 %collective-permute-start.17 = (f32[8,64,256]{2,1,0:T(8,128)S(1)}, f32[8,64,256]{2,1,0:T(8,128)S(1)}, u32[]{:S(2)}, u32[]{:S(2)}) collective-permute-start(f32[8,64,256]{2,1,0:T(8,128)S(1)} %collective-permute-done.16), channel_id=1, source_target_pairs={{0,0},{1,1},{2,14},{3,3},{4,4},{5,5},{6,2},{7,7},{8,8},{9,9},{10,6... | collective-permute-start | bytes 1572872 | tf_op jit(solution)/shard_map/ppermute | solution.py:343
  109.2 11.4 %collective-permute-done.15.lo = f32[8,64,256]{2,1,0:T(8,128)S(1)} collective-permute-done((f32[8,64,256]{2,1,0:T(8,128)S(1)}, f32[8,64,256]{2,1,0:T(8,128)S(1)}, u32[]{:S(2)}, u32[]{:S(2)}) %collective-permute-start.15) | collective-permute-done | bytes 524320 | tf_op jit(solution)/shard_map/ppermute | solution.py:343
  120.6 3.1 %collective-permute-done.17.hi = f32[8,64,256]{2,1,0:T(8,128)S(1)} collective-permute-done((f32[8,64,256]{2,1,0:T(8,128)S(1)}, f32[8,64,256]{2,1,0:T(8,128)S(1)}, u32[]{:S(2)}, u32[]{:S(2)}) %collective-permute-start.17) | collective-permute-done | bytes 524320 | tf_op jit(solution)/shard_map/ppermute | solution.py:343
  123.7 1.0 whole.1
  (17 shorter events, 0.3 us)
Async XLA Ops:
  0.0 14.5 %collective-permute-start = (f32[16,64,256]{2,1,0:T(8,128)}, f32[16,64,256]{2,1,0:T(8,128)S(1)}, u32[]{:S(2)}, u32[]{:S(2)}) collective-permute-start(f32[16,64,256]{2,1,0:T(8,128)} %param.9), channel_id=1, source_target_pairs={{1,0},{2,1},{3,2},{4,3},{5,4},{6,5},{7,6},{8,7},{9,8},{10,9},{11,1... | collective-permute-start | bytes 3145736 | tf_op jit(solution)/shard_map/ppermute | solution.py:343
  4.1 2.2 %copy-start = (bf16[1,4,32,64,256]{4,3,2,1,0:T(8,128)(2,1)S(1)}, bf16[1,4,32,64,256]{4,3,2,1,0:T(8,128)(2,1)}, u32[]{:S(2)}) copy-start(bf16[1,4,32,64,256]{4,3,2,1,0:T(8,128)(2,1)} %images.1) | copy-start | bytes 12582916
  6.3 0.7 copy-start.1
  7.0 0.7 copy-start.2
  7.7 0.7 copy-start.3
  8.3 2.5 %copy-start.4 = (f32[16,64,256]{2,1,0:T(8,128)S(1)}, f32[16,64,256]{2,1,0:T(8,128)}, u32[]{:S(2)}) copy-start(f32[16,64,256]{2,1,0:T(8,128)} %param.9) | copy-start | bytes 3145732
  10.9 10.5 %collective-permute-start.2 = (f32[8,64,256]{2,1,0:T(8,128)S(1)}, f32[8,64,256]{2,1,0:T(8,128)S(1)}, u32[]{:S(2)}, u32[]{:S(2)}) collective-permute-start(f32[8,64,256]{2,1,0:T(8,128)S(1)} %get-tuple-element.36.refs_1_.refs_2_), channel_id=1, source_target_pairs={{0,1},{1,2},{2,3},{3,4},{4,5},{5,6},{6,7},{7,8},{8,9},{9,10},{10,1... | collective-permute-start | bytes 1572872 | tf_op jit(solution)/shard_map/ppermute | solution.py:343
  14.5 12.5 %collective-permute-start.1 = (f32[8,64,256]{2,1,0:T(8,128)S(1)}, f32[8,64,256]{2,1,0:T(8,128)S(1)}, u32[]{:S(2)}, u32[]{:S(2)}) collective-permute-start(f32[8,64,256]{2,1,0:T(8,128)S(1)} %get-tuple-element.34.refs_0_.refs_1_.refs_2_), channel_id=1, source_target_pairs={{0,1},{1,2},{2,3},{3,4},{4,5},{5,6},{6,7},{7,8},{8,9},{9,10},{10,1... | collective-permute-start | bytes 1572872 | tf_op jit(solution)/shard_map/ppermute | solution.py:343
  24.8 8.7 %collective-permute-start.5 = (f32[8,64,256]{2,1,0:T(8,128)S(1)}, f32[8,64,256]{2,1,0:T(8,128)S(1)}, u32[]{:S(2)}, u32[]{:S(2)}) collective-permute-start(f32[8,64,256]{2,1,0:T(8,128)S(1)} %get-tuple-element.46.refs_3_), channel_id=1, source_target_pairs={{0,1},{1,2},{2,3},{3,4},{4,5},{5,6},{6,7},{7,8},{8,9},{9,10},{10,1... | collective-permute-start | bytes 1572872 | tf_op jit(solution)/shard_map/ppermute | solution.py:343
  30.5 8.7 %collective-permute-start.3 = (f32[8,64,256]{2,1,0:T(8,128)S(1)}, f32[8,64,256]{2,1,0:T(8,128)S(1)}, u32[]{:S(2)}, u32[]{:S(2)}) collective-permute-start(f32[8,64,256]{2,1,0:T(8,128)S(1)} %get-tuple-element.45.refs_2_), channel_id=1, source_target_pairs={{0,1},{1,2},{2,3},{3,4},{4,5},{5,6},{6,7},{7,8},{8,9},{9,10},{10,1... | collective-permute-start | bytes 1572872 | tf_op jit(solution)/shard_map/ppermute | solution.py:343
  33.5 11.3 %collective-permute-start.6 = (f32[8,64,256]{2,1,0:T(8,128)S(1)}, f32[8,64,256]{2,1,0:T(8,128)S(1)}, u32[]{:S(2)}, u32[]{:S(2)}) collective-permute-start(f32[8,64,256]{2,1,0:T(8,128)S(1)} %collective-permute-done.5.refs_1_.refs_2_), channel_id=1, source_target_pairs={{0,1},{1,2},{2,3},{3,4},{4,5},{5,6},{6,7},{7,8},{8,9},{9,10},{10,1... | collective-permute-start | bytes 1572872 | tf_op jit(solution)/shard_map/ppermute | solution.py:343
  39.2 11.2 %collective-permute-start.4 = (f32[8,64,256]{2,1,0:T(8,128)S(1)}, f32[8,64,256]{2,1,0:T(8,128)S(1)}, u32[]{:S(2)}, u32[]{:S(2)}) collective-permute-start(f32[8,64,256]{2,1,0:T(8,128)S(1)} %collective-permute-done.3.refs_0_.refs_1_.refs_2_), channel_id=1, source_target_pairs={{0,1},{1,2},{2,3},{3,4},{4,5},{5,6},{6,7},{7,8},{8,9},{9,10},{10,1... | collective-permute-start | bytes 1572872 | tf_op jit(solution)/shard_map/ppermute | solution.py:343
  48.2 8.7 %collective-permute-start.9 = (f32[8,64,256]{2,1,0:T(8,128)S(1)}, f32[8,64,256]{2,1,0:T(8,128)S(1)}, u32[]{:S(2)}, u32[]{:S(2)}) collective-permute-start(f32[8,64,256]{2,1,0:T(8,128)S(1)} %get-tuple-element.51.refs_3_), channel_id=1, source_target_pairs={{0,1},{1,2},{2,3},{3,4},{4,5},{5,6},{6,7},{7,8},{8,9},{9,10},{10,1... | collective-permute-start | bytes 1572872 | tf_op jit(solution)/shard_map/ppermute | solution.py:343
  53.9 8.7 %collective-permute-start.7 = (f32[8,64,256]{2,1,0:T(8,128)S(1)}, f32[8,64,256]{2,1,0:T(8,128)S(1)}, u32[]{:S(2)}, u32[]{:S(2)}) collective-permute-start(f32[8,64,256]{2,1,0:T(8,128)S(1)} %get-tuple-element.50.refs_2_), channel_id=1, source_target_pairs={{0,1},{1,2},{2,3},{3,4},{4,5},{5,6},{6,7},{7,8},{8,9},{9,10},{10,1... | collective-permute-start | bytes 1572872 | tf_op jit(solution)/shard_map/ppermute | solution.py:343
  56.9 11.3 %collective-permute-start.10 = (f32[8,64,256]{2,1,0:T(8,128)S(1)}, f32[8,64,256]{2,1,0:T(8,128)S(1)}, u32[]{:S(2)}, u32[]{:S(2)}) collective-permute-start(f32[8,64,256]{2,1,0:T(8,128)S(1)} %collective-permute-done.9.refs_1_.refs_2_), channel_id=1, source_target_pairs={{0,1},{1,2},{2,3},{3,4},{4,5},{5,6},{6,7},{7,8},{8,9},{9,10},{10,1... | collective-permute-start | bytes 1572872 | tf_op jit(solution)/shard_map/ppermute | solution.py:343
  62.5 13.3 %collective-permute-start.8 = (f32[8,64,256]{2,1,0:T(8,128)S(1)}, f32[8,64,256]{2,1,0:T(8,128)S(1)}, u32[]{:S(2)}, u32[]{:S(2)}) collective-permute-start(f32[8,64,256]{2,1,0:T(8,128)S(1)} %collective-permute-done.7.refs_0_.refs_1_.refs_2_), channel_id=1, source_target_pairs={{0,1},{1,2},{2,3},{3,4},{4,5},{5,6},{6,7},{7,8},{8,9},{9,10},{10,1... | collective-permute-start | bytes 1572872 | tf_op jit(solution)/shard_map/ppermute | solution.py:343
  71.6 8.9 %collective-permute-start.13 = (f32[8,64,256]{2,1,0:T(8,128)S(1)}, f32[8,64,256]{2,1,0:T(8,128)S(1)}, u32[]{:S(2)}, u32[]{:S(2)}) collective-permute-start(f32[8,64,256]{2,1,0:T(8,128)S(1)} %get-tuple-element.56.refs_3_), channel_id=1, source_target_pairs={{0,1},{1,2},{2,3},{3,4},{4,5},{5,6},{6,7},{7,8},{8,9},{9,10},{10,1... | collective-permute-start | bytes 1572872 | tf_op jit(solution)/shard_map/ppermute | solution.py:343
  79.3 8.7 %collective-permute-start.11 = (f32[8,64,256]{2,1,0:T(8,128)S(1)}, f32[8,64,256]{2,1,0:T(8,128)S(1)}, u32[]{:S(2)}, u32[]{:S(2)}) collective-permute-start(f32[8,64,256]{2,1,0:T(8,128)S(1)} %get-tuple-element.55.refs_2_), channel_id=1, source_target_pairs={{0,1},{1,2},{2,3},{3,4},{4,5},{5,6},{6,7},{7,8},{8,9},{9,10},{10,1... | collective-permute-start | bytes 1572872 | tf_op jit(solution)/shard_map/ppermute | solution.py:343
  80.5 13.0 %collective-permute-start.14 = (f32[8,64,256]{2,1,0:T(8,128)S(1)}, f32[8,64,256]{2,1,0:T(8,128)S(1)}, u32[]{:S(2)}, u32[]{:S(2)}) collective-permute-start(f32[8,64,256]{2,1,0:T(8,128)S(1)} %collective-permute-done.13.refs_1_.refs_2_), channel_id=1, source_target_pairs={{0,1},{1,2},{2,3},{3,4},{4,5},{5,6},{6,7},{7,8},{8,9},{9,10},{10,1... | collective-permute-start | bytes 1572872 | tf_op jit(solution)/shard_map/ppermute | solution.py:343
  87.9 12.2 %collective-permute-start.12 = (f32[8,64,256]{2,1,0:T(8,128)S(1)}, f32[8,64,256]{2,1,0:T(8,128)S(1)}, u32[]{:S(2)}, u32[]{:S(2)}) collective-permute-start(f32[8,64,256]{2,1,0:T(8,128)S(1)} %collective-permute-done.11.refs_0_.refs_1_.refs_2_), channel_id=1, source_target_pairs={{0,1},{1,2},{2,3},{3,4},{4,5},{5,6},{6,7},{7,8},{8,9},{9,10},{10,1... | collective-permute-start | bytes 1572872 | tf_op jit(solution)/shard_map/ppermute | solution.py:343
  97.0 9.9 %collective-permute-start.16 = (f32[8,64,256]{2,1,0:T(8,128)S(1)}, f32[8,64,256]{2,1,0:T(8,128)S(1)}, u32[]{:S(2)}, u32[]{:S(2)}) collective-permute-start(f32[8,64,256]{2,1,0:T(8,128)S(1)} %get-tuple-element.61), channel_id=1, source_target_pairs={{0,13},{1,2},{2,15},{3,0},{4,1},{5,6},{6,3},{7,4},{8,5},{9,10},{10... | collective-permute-start | bytes 1572872 | tf_op jit(solution)/shard_map/ppermute | solution.py:343
  103.6 17.0 %collective-permute-start.15 = (f32[8,64,256]{2,1,0:T(8,128)S(1)}, f32[8,64,256]{2,1,0:T(8,128)S(1)}, u32[]{:S(2)}, u32[]{:S(2)}) collective-permute-start(f32[8,64,256]{2,1,0:T(8,128)S(1)} %get-tuple-element.60), channel_id=1, source_target_pairs={{0,13},{1,14},{2,15},{3,0},{4,1},{5,2},{6,3},{7,4},{8,5},{9,6},{10... | collective-permute-start | bytes 1572872 | tf_op jit(solution)/shard_map/ppermute | solution.py:343
  106.8 16.8 %collective-permute-start.17 = (f32[8,64,256]{2,1,0:T(8,128)S(1)}, f32[8,64,256]{2,1,0:T(8,128)S(1)}, u32[]{:S(2)}, u32[]{:S(2)}) collective-permute-start(f32[8,64,256]{2,1,0:T(8,128)S(1)} %collective-permute-done.16), channel_id=1, source_target_pairs={{0,0},{1,1},{2,14},{3,3},{4,4},{5,5},{6,2},{7,7},{8,8},{9,9},{10,6... | collective-permute-start | bytes 1572872 | tf_op jit(solution)/shard_map/ppermute | solution.py:343

commit v5 on v4

--- a/solution.py
+++ b/solution.py
@@ -270,14 +270,15 @@
 
     def kernel(*refs):
         slab, ends, depth_f, depth_a, row_f, row_a, col_f, col_a = refs[given : given + 8]
-        ratio, updated, spread, mixed, spread_hi, mixed_hi, spread_lo, mixed_lo = refs[given + 8 :]
+        ratio, updated, spread, mixed, spread_f, mixed_f = refs[given + 8 : given + 14]
+        spread_hi, mixed_hi, spread_lo, mixed_lo = refs[given + 14 :]
         live = ends[0]
         scales = [live] * len(below) + [None] * len(own)
 
-        def divide(t):
+        def divide(t, mixed_t):
             planes = slice(t * QUAD, (t + 1) * QUAD)
             seen = slab[start + t * QUAD : start + (t + 1) * QUAD].astype(F32)
-            value = seen / col_whole(mixed, col_f, t)
+            value = seen / col_whole(mixed_t, col_f, 0)
             ratio[planes] = value * live if start == 0 else value
 
         def back(t, mixed_t):
@@ -285,12 +286,14 @@
             updated[planes] = refs[parts - 1][planes] * col_whole(mixed_t, col_a, 0)
 
         ratio_refs = [(ref, 0) for ref in refs[parts:given]]
-        depth_whole(window([(ref, 0) for ref in refs[:parts]], scales), depth_f, HALF, spread)
-        row_whole(spread, row_f, mixed, 1)
-        divide(1)
+        above_first = [(ref, 0) for ref in refs[1:parts]]
+        depth_whole(window([(refs[0], QUAD)] + above_first, scales), depth_f, QUAD, spread)
         row_whole(spread, row_f, mixed, 0)
+        depth_whole(window([(refs[0], 0)] + above_first, scales), depth_f, QUAD, spread_f)
+        divide(1, mixed)
+        row_whole(spread_f, row_f, mixed_f, 0)
         depth_whole(window([(ratio, QUAD)] + ratio_refs), depth_a, QUAD, spread_hi)
-        divide(0)
+        divide(0, mixed_f)
         row_whole(spread_hi, row_a, mixed_hi, 0)
         depth_whole(window([(ratio, 0)] + ratio_refs), depth_a, QUAD, spread_lo)
         back(1, mixed_hi)
@@ -298,11 +301,7 @@
         back(0, mixed_lo)
 
     ranks = ops[0].shape[0]
-    scratch = [
-        shape
-        for tiles in (2, 1, 1)
-        for shape in ((ranks, tiles, TILE, COLS), (tiles * TILE, ranks * COLS))
-    ]
+    scratch = [(ranks, 1, TILE, COLS), (TILE, ranks * COLS)] * 4
     return call(kernel, "half", below + own + ratios, shared, ops, [HALF, HALF], scratch)
 
 

time: 125 us -> 124 us (level)
  Pallas kernels: 46.9 us -> 44.6 us
    pallas_call x12, Pallas kernels: 43.4 us -> 41.1 us  [call(): pl.pallas_call(kernel, out_shape=out, in_specs=[VMEM] * (len(arrays) + le...]
  transfers between devices with their start and end apart: 18 -> 18, of which waited for: 15 -> 16; matrix products, arithmetic and copies ran while one was open for 2% -> 2% of each run, Pallas kernels for 37% -> 35%
where the time goes in v5:
time: 124 us
  waiting for transfers between devices  49.1 us (40%)
  Pallas kernels  44.6 us (36%)
  starting transfers between devices  23.1 us (19%)
  local copies, waits for them, and re-layouts  6.38 us (5%)
    ppermute x18, waiting for transfers between devices, send(): return lax.ppermute(cells, 'view', pairs)  49.1 us
    pallas_call x12, Pallas kernels, call(): pl.pallas_call(kernel, out_shape=out, in_specs=[VMEM] * (len(arrays) + le...  41.1 us
    ppermute x18, starting transfers between devices, send(): return lax.ppermute(cells, 'view', pairs)  23.1 us
    unnamed x13, local copies, waits for them, and re-layouts  6.31 us
    pallas_call x1, Pallas kernels, build(): pl.pallas_call(build_kernel, out_shape=[depth, depth] + [square] * 4 + [s...  2.52 us
  transfers between devices with their start and end apart: 18, of which 16 were waited for; matrix products, arithmetic and copies ran while one was open for 2% of the time, Pallas kernels for 35%

profile of v5, /device:TPU:28, one launch (start us, length us, event | category | flops | bytes accessed | tf_op | source)
XLA Modules:
  0.0 123.6 jit_solution(14917087257867931012)
XLA Ops:
  0.0 1.9 %collective-permute-start = (f32[16,64,256]{2,1,0:T(8,128)}, f32[16,64,256]{2,1,0:T(8,128)S(1)}, u32[]{:S(2)}, u32[]{:S(2)}) collective-permute-start(f32[16,64,256]{2,1,0:T(8,128)} %param.9), channel_id=1, source_target_pairs={{1,0},{2,1},{3,2},{4,3},{5,4},{6,5},{7,6},{8,7},{9,8},{10,9},{11,1... | collective-permute-start | bytes 3145736 | tf_op jit(solution)/shard_map/ppermute | solution.py:342
  1.9 0.7 copy.9.depth_taps
  2.6 0.7 copy.10.row_taps
  3.3 0.7 copy.11.col_taps
  4.1 0.1 pad_add_fusion.place
  4.1 2.2 %copy-done = bf16[1,4,32,64,256]{4,3,2,1,0:T(8,128)(2,1)S(1)} copy-done((bf16[1,4,32,64,256]{4,3,2,1,0:T(8,128)(2,1)S(1)}, bf16[1,4,32,64,256]{4,3,2,1,0:T(8,128)(2,1)}, u32[]{:S(2)}) %copy-start) | copy-done | bytes 4194328
  6.3 0.7 copy-done.1
  7.0 0.7 copy-done.2
  7.7 0.7 copy-done.3
  8.3 2.5 %build.1 = (bf16[6,128,256]{2,1,0:T(8,128)(2,1)S(1)}, bf16[6,128,256]{2,1,0:T(8,128)(2,1)S(1)}, bf16[6,256,256]{2,1,0:T(8,128)(2,1)S(1)}, bf16[6,256,256]{2,1,0:...) custom-call(s32[2]{0:T(128)S(1)} %pad_add_fusion.place, ...), custom_call_target="tpu_custom_call" | custom-call | tf_op jit(solution)/shard_map/build/pallas_call | solution.py:131
  10.9 2.5 %collective-permute-start.2 = (f32[8,64,256]{2,1,0:T(8,128)S(1)}, f32[8,64,256]{2,1,0:T(8,128)S(1)}, u32[]{:S(2)}, u32[]{:S(2)}) collective-permute-start(f32[8,64,256]{2,1,0:T(8,128)S(1)} %get-tuple-element.36.refs_1_.refs_2_), channel_id=1, source_target_pairs={{0,1},{1,2},{2,3},{3,4},{4,5},{5,6},{6,7},{7,8},{8,9},{9,10},{10,1... | collective-permute-start | bytes 1572872 | tf_op jit(solution)/shard_map/ppermute | solution.py:342
  13.4 1.1 collective-permute-done.refs_2_
  14.5 1.9 %collective-permute-start.1 = (f32[8,64,256]{2,1,0:T(8,128)S(1)}, f32[8,64,256]{2,1,0:T(8,128)S(1)}, u32[]{:S(2)}, u32[]{:S(2)}) collective-permute-start(f32[8,64,256]{2,1,0:T(8,128)S(1)} %get-tuple-element.34.refs_0_.refs_1_.refs_2_), channel_id=1, source_target_pairs={{0,1},{1,2},{2,3},{3,4},{4,5},{5,6},{6,7},{7,8},{8,9},{9,10},{10,1... | collective-permute-start | bytes 1572872 | tf_op jit(solution)/shard_map/ppermute | solution.py:342
  16.4 2.7 %upper.4.refs_3_.refs_4_ = f32[16,64,256]{2,1,0:T(8,128)S(1)} custom-call(f32[8,64,256]{2,1,0:T(8,128)S(1)} %get-tuple-element.34.refs_0_.refs_1_.refs_2_, f32[8,64,256]{2,1,0:T(8,128)S(1)} %get-tuple-element.36.refs_1_.refs_2_, f32[16,64,256]{2,1,0:T(8,128)S(1)} %collective-permute-done.refs_2_, ...), custom_call_target="tpu_custom_call" | custom-call | flops 1048576 | bytes 1024 | tf_op jit(solution)/shard_map/upper/pallas_call | solution.py:221
  19.1 2.3 %collective-permute-done.2.refs_0_.refs_1_ = f32[8,64,256]{2,1,0:T(8,128)S(1)} collective-permute-done((f32[8,64,256]{2,1,0:T(8,128)S(1)}, f32[8,64,256]{2,1,0:T(8,128)S(1)}, u32[]{:S(2)}, u32[]{:S(2)}) %collective-permute-start.2) | collective-permute-done | bytes 524320 | tf_op jit(solution)/shard_map/ppermute | solution.py:342
  21.4 3.1 %half.8 = (f32[8,64,256]{2,1,0:T(8,128)S(1)}, f32[8,64,256]{2,1,0:T(8,128)S(1)}) custom-call(f32[8,64,256]{2,1,0:T(8,128)S(1)} %collective-permute-done.2.refs_0_.refs_1_, f32[8,64,256]{2,1,0:T(8,128)S(1)} %get-tuple-element.34.refs_0_.refs_1_.refs_2_, f32[8,64,256]{2,1,0:T(8,128)S(1)} %get-tuple-element.36.refs_1_.refs_2_, ...), custom_call_target="tpu_custom_call" | custom-call | flops 1048576 | bytes 1024 | tf_op jit(solution)/shard_map/half/pallas_call | solution.py:221
  24.6 2.4 %collective-permute-done.1.refs_0_ = f32[8,64,256]{2,1,0:T(8,128)S(1)} collective-permute-done((f32[8,64,256]{2,1,0:T(8,128)S(1)}, f32[8,64,256]{2,1,0:T(8,128)S(1)}, u32[]{:S(2)}, u32[]{:S(2)}) %collective-permute-start.1) | collective-permute-done | bytes 524320 | tf_op jit(solution)/shard_map/ppermute | solution.py:342
  27.0 3.2 %half.9 = (f32[8,64,256]{2,1,0:T(8,128)}, f32[8,64,256]{2,1,0:T(8,128)S(1)}) custom-call(f32[8,64,256]{2,1,0:T(8,128)S(1)} %collective-permute-done.1.refs_0_, f32[8,64,256]{2,1,0:T(8,128)S(1)} %collective-permute-done.2.refs_0_.refs_1_, f32[8,64,256]{2,1,0:T(8,128)S(1)} %get-tuple-element.34.refs_0_.refs_1_.refs_2_, ...), custom_call_target="tpu_custom_call" | custom-call | flops 1048576 | bytes 1024 | tf_op jit(solution)/shard_map/half/pallas_call | solution.py:221
  30.3 2.9 %collective-permute-done.5.refs_1_.refs_2_ = f32[8,64,256]{2,1,0:T(8,128)S(1)} collective-permute-done((f32[8,64,256]{2,1,0:T(8,128)S(1)}, f32[8,64,256]{2,1,0:T(8,128)S(1)}, u32[]{:S(2)}, u32[]{:S(2)}) %collective-permute-start.5) | collective-permute-done | bytes 524320 | tf_op jit(solution)/shard_map/ppermute | solution.py:342
  33.2 5.6 %collective-permute-done.3.refs_0_.refs_1_.refs_2_ = f32[8,64,256]{2,1,0:T(8,128)S(1)} collective-permute-done((f32[8,64,256]{2,1,0:T(8,128)S(1)}, f32[8,64,256]{2,1,0:T(8,128)S(1)}, u32[]{:S(2)}, u32[]{:S(2)}) %collective-permute-start.3) | collective-permute-done | bytes 524320 | tf_op jit(solution)/shard_map/ppermute | solution.py:342
  38.9 4.4 %upper.5.refs_3_.refs_4_ = f32[16,64,256]{2,1,0:T(8,128)S(1)} custom-call(f32[8,64,256]{2,1,0:T(8,128)S(1)} %collective-permute-done.3.refs_0_.refs_1_.refs_2_, f32[8,64,256]{2,1,0:T(8,128)S(1)} %collective-permute-done.5.refs_1_.refs_2_, f32[8,64,256]{2,1,0:T(8,128)S(1)} %get-tuple-element.45.refs_2_, f32[8,64,256]{2,1,0:T(8,128)S(1)} %get-tuple-element.46.refs_3_, ...), custom_call_target="tpu_custom_call" | custom-call | flops 1048576 | bytes 1024 | tf_op jit(solution)/shard_map/upper/pallas_call | solution.py:221
  43.3 1.2 collective-permute-done.6.refs_0_.refs_1_
  44.5 3.1 %half.10 = (f32[8,64,256]{2,1,0:T(8,128)S(1)}, f32[8,64,256]{2,1,0:T(8,128)S(1)}) custom-call(f32[8,64,256]{2,1,0:T(8,128)S(1)} %collective-permute-done.6.refs_0_.refs_1_, f32[8,64,256]{2,1,0:T(8,128)S(1)} %collective-permute-done.3.refs_0_.refs_1_.refs_2_, f32[8,64,256]{2,1,0:T(8,128)S(1)} %collective-permute-done.5.refs_1_.refs_2_, ...), custom_call_target="tpu_custom_call" | custom-call | flops 1048576 | bytes 1024 | tf_op jit(solution)/shard_map/half/pallas_call | solution.py:221
  47.6 1.3 %collective-permute-start.9 = (f32[8,64,256]{2,1,0:T(8,128)S(1)}, f32[8,64,256]{2,1,0:T(8,128)S(1)}, u32[]{:S(2)}, u32[]{:S(2)}) collective-permute-start(f32[8,64,256]{2,1,0:T(8,128)S(1)} %get-tuple-element.51.refs_3_), channel_id=1, source_target_pairs={{0,1},{1,2},{2,3},{3,4},{4,5},{5,6},{6,7},{7,8},{8,9},{9,10},{10,1... | collective-permute-start | bytes 1572872 | tf_op jit(solution)/shard_map/ppermute | solution.py:342
  48.8 1.2 %collective-permute-done.4.refs_0_ = f32[8,64,256]{2,1,0:T(8,128)S(1)} collective-permute-done((f32[8,64,256]{2,1,0:T(8,128)S(1)}, f32[8,64,256]{2,1,0:T(8,128)S(1)}, u32[]{:S(2)}, u32[]{:S(2)}) %collective-permute-start.4) | collective-permute-done | bytes 524320 | tf_op jit(solution)/shard_map/ppermute | solution.py:342
  50.1 3.2 %half.11 = (f32[8,64,256]{2,1,0:T(8,128)}, f32[8,64,256]{2,1,0:T(8,128)S(1)}) custom-call(f32[8,64,256]{2,1,0:T(8,128)S(1)} %collective-permute-done.4.refs_0_, f32[8,64,256]{2,1,0:T(8,128)S(1)} %collective-permute-done.6.refs_0_.refs_1_, f32[8,64,256]{2,1,0:T(8,128)S(1)} %collective-permute-done.3.refs_0_.refs_1_.refs_2_, ...), custom_call_target="tpu_custom_call" | custom-call | flops 1048576 | bytes 1024 | tf_op jit(solution)/shard_map/half/pallas_call | solution.py:221
  53.3 2.9 %collective-permute-done.9.refs_1_.refs_2_ = f32[8,64,256]{2,1,0:T(8,128)S(1)} collective-permute-done((f32[8,64,256]{2,1,0:T(8,128)S(1)}, f32[8,64,256]{2,1,0:T(8,128)S(1)}, u32[]{:S(2)}, u32[]{:S(2)}) %collective-permute-start.9) | collective-permute-done | bytes 524320 | tf_op jit(solution)/shard_map/ppermute | solution.py:342
  56.2 5.6 %collective-permute-done.7.refs_0_.refs_1_.refs_2_ = f32[8,64,256]{2,1,0:T(8,128)S(1)} collective-permute-done((f32[8,64,256]{2,1,0:T(8,128)S(1)}, f32[8,64,256]{2,1,0:T(8,128)S(1)}, u32[]{:S(2)}, u32[]{:S(2)}) %collective-permute-start.7) | collective-permute-done | bytes 524320 | tf_op jit(solution)/shard_map/ppermute | solution.py:342
  61.9 4.4 %upper.6.refs_3_.refs_4_ = f32[16,64,256]{2,1,0:T(8,128)S(1)} custom-call(f32[8,64,256]{2,1,0:T(8,128)S(1)} %collective-permute-done.7.refs_0_.refs_1_.refs_2_, f32[8,64,256]{2,1,0:T(8,128)S(1)} %collective-permute-done.9.refs_1_.refs_2_, f32[8,64,256]{2,1,0:T(8,128)S(1)} %get-tuple-element.50.refs_2_, f32[8,64,256]{2,1,0:T(8,128)S(1)} %get-tuple-element.51.refs_3_, ...), custom_call_target="tpu_custom_call" | custom-call | flops 1048576 | bytes 1024 | tf_op jit(solution)/shard_map/upper/pallas_call | solution.py:221
  66.3 1.2 collective-permute-done.10.refs_0_.refs_1_
  67.5 3.1 %half.12 = (f32[8,64,256]{2,1,0:T(8,128)S(1)}, f32[8,64,256]{2,1,0:T(8,128)S(1)}) custom-call(f32[8,64,256]{2,1,0:T(8,128)S(1)} %collective-permute-done.10.refs_0_.refs_1_, f32[8,64,256]{2,1,0:T(8,128)S(1)} %collective-permute-done.7.refs_0_.refs_1_.refs_2_, f32[8,64,256]{2,1,0:T(8,128)S(1)} %collective-permute-done.9.refs_1_.refs_2_, ...), custom_call_target="tpu_custom_call" | custom-call | flops 1048576 | bytes 1024 | tf_op jit(solution)/shard_map/half/pallas_call | solution.py:221
  70.6 4.2 %collective-permute-start.13 = (f32[8,64,256]{2,1,0:T(8,128)S(1)}, f32[8,64,256]{2,1,0:T(8,128)S(1)}, u32[]{:S(2)}, u32[]{:S(2)}) collective-permute-start(f32[8,64,256]{2,1,0:T(8,128)S(1)} %get-tuple-element.56.refs_3_), channel_id=1, source_target_pairs={{0,1},{1,2},{2,3},{3,4},{4,5},{5,6},{6,7},{7,8},{8,9},{9,10},{10,1... | collective-permute-start | bytes 1572872 | tf_op jit(solution)/shard_map/ppermute | solution.py:342
  74.9 3.2 %half.13 = (f32[8,64,256]{2,1,0:T(8,128)}, f32[8,64,256]{2,1,0:T(8,128)S(1)}) custom-call(f32[8,64,256]{2,1,0:T(8,128)S(1)} %collective-permute-done.8.refs_0_, f32[8,64,256]{2,1,0:T(8,128)S(1)} %collective-permute-done.10.refs_0_.refs_1_, f32[8,64,256]{2,1,0:T(8,128)S(1)} %collective-permute-done.7.refs_0_.refs_1_.refs_2_, ...), custom_call_target="tpu_custom_call" | custom-call | flops 1048576 | bytes 1024 | tf_op jit(solution)/shard_map/half/pallas_call | solution.py:221
  78.1 1.3 %collective-permute-start.11 = (f32[8,64,256]{2,1,0:T(8,128)S(1)}, f32[8,64,256]{2,1,0:T(8,128)S(1)}, u32[]{:S(2)}, u32[]{:S(2)}) collective-permute-start(f32[8,64,256]{2,1,0:T(8,128)S(1)} %get-tuple-element.55.refs_2_), channel_id=1, source_target_pairs={{0,1},{1,2},{2,3},{3,4},{4,5},{5,6},{6,7},{7,8},{8,9},{9,10},{10,1... | collective-permute-start | bytes 1572872 | tf_op jit(solution)/shard_map/ppermute | solution.py:342
  79.3 0.2 collective-permute-done.13.refs_1_.refs_2_
  79.5 2.7 %collective-permute-start.14 = (f32[8,64,256]{2,1,0:T(8,128)S(1)}, f32[8,64,256]{2,1,0:T(8,128)S(1)}, u32[]{:S(2)}, u32[]{:S(2)}) collective-permute-start(f32[8,64,256]{2,1,0:T(8,128)S(1)} %collective-permute-done.13.refs_1_.refs_2_), channel_id=1, source_target_pairs={{0,1},{1,2},{2,3},{3,4},{4,5},{5,6},{6,7},{7,8},{8,9},{9,10},{10,1... | collective-permute-start | bytes 1572872 | tf_op jit(solution)/shard_map/ppermute | solution.py:342
  82.2 4.5 %collective-permute-done.11.refs_0_.refs_1_.refs_2_ = f32[8,64,256]{2,1,0:T(8,128)S(1)} collective-permute-done((f32[8,64,256]{2,1,0:T(8,128)S(1)}, f32[8,64,256]{2,1,0:T(8,128)S(1)}, u32[]{:S(2)}, u32[]{:S(2)}) %collective-permute-start.11) | collective-permute-done | bytes 524320 | tf_op jit(solution)/shard_map/ppermute | solution.py:342
  86.7 1.1 collective-permute-start.12
  87.8 4.4 %upper.7.refs_3_.refs_4_ = f32[16,64,256]{2,1,0:T(8,128)S(1)} custom-call(f32[8,64,256]{2,1,0:T(8,128)S(1)} %collective-permute-done.11.refs_0_.refs_1_.refs_2_, f32[8,64,256]{2,1,0:T(8,128)S(1)} %collective-permute-done.13.refs_1_.refs_2_, f32[8,64,256]{2,1,0:T(8,128)S(1)} %get-tuple-element.55.refs_2_, f32[8,64,256]{2,1,0:T(8,128)S(1)} %get-tuple-element.56.refs_3_, ...), custom_call_target="tpu_custom_call" | custom-call | flops 1048576 | bytes 1024 | tf_op jit(solution)/shard_map/upper/pallas_call | solution.py:221
  92.3 3.1 %half.14 = (f32[8,64,256]{2,1,0:T(8,128)S(1)}, f32[8,64,256]{2,1,0:T(8,128)S(1)}) custom-call(f32[8,64,256]{2,1,0:T(8,128)S(1)} %collective-permute-done.14.refs_0_.refs_1_, f32[8,64,256]{2,1,0:T(8,128)S(1)} %collective-permute-done.11.refs_0_.refs_1_.refs_2_, f32[8,64,256]{2,1,0:T(8,128)S(1)} %collective-permute-done.13.refs_1_.refs_2_, ...), custom_call_target="tpu_custom_call" | custom-call | flops 1048576 | bytes 1024 | tf_op jit(solution)/shard_map/half/pallas_call | solution.py:221
  95.5 3.4 %collective-permute-start.16 = (f32[8,64,256]{2,1,0:T(8,128)S(1)}, f32[8,64,256]{2,1,0:T(8,128)S(1)}, u32[]{:S(2)}, u32[]{:S(2)}) collective-permute-start(f32[8,64,256]{2,1,0:T(8,128)S(1)} %get-tuple-element.61), channel_id=1, source_target_pairs={{0,13},{1,2},{2,15},{3,0},{4,1},{5,6},{6,3},{7,4},{8,5},{9,10},{10... | collective-permute-start | bytes 1572872 | tf_op jit(solution)/shard_map/ppermute | solution.py:342
  98.9 3.2 %half.15 = (f32[8,64,256]{2,1,0:T(8,128)}, f32[8,64,256]{2,1,0:T(8,128)S(1)}) custom-call(f32[8,64,256]{2,1,0:T(8,128)S(1)} %collective-permute-done.12.refs_0_, f32[8,64,256]{2,1,0:T(8,128)S(1)} %collective-permute-done.14.refs_0_.refs_1_, f32[8,64,256]{2,1,0:T(8,128)S(1)} %collective-permute-done.11.refs_0_.refs_1_.refs_2_, ...), custom_call_target="tpu_custom_call" | custom-call | flops 1048576 | bytes 1024 | tf_op jit(solution)/shard_map/half/pallas_call | solution.py:221
  102.1 0.3 collective-permute-start.15
  102.3 3.2 %collective-permute-done.16 = f32[8,64,256]{2,1,0:T(8,128)S(1)} collective-permute-done((f32[8,64,256]{2,1,0:T(8,128)S(1)}, f32[8,64,256]{2,1,0:T(8,128)S(1)}, u32[]{:S(2)}, u32[]{:S(2)}) %collective-permute-start.16) | collective-permute-done | bytes 524320 | tf_op jit(solution)/shard_map/ppermute | solution.py:342
  105.6 2.4 %collective-permute-start.17 = (f32[8,64,256]{2,1,0:T(8,128)S(1)}, f32[8,64,256]{2,1,0:T(8,128)S(1)}, u32[]{:S(2)}, u32[]{:S(2)}) collective-permute-start(f32[8,64,256]{2,1,0:T(8,128)S(1)} %collective-permute-done.16), channel_id=1, source_target_pairs={{0,0},{1,1},{2,14},{3,3},{4,4},{5,5},{6,2},{7,7},{8,8},{9,9},{10,6... | collective-permute-start | bytes 1572872 | tf_op jit(solution)/shard_map/ppermute | solution.py:342
  108.0 11.1 %collective-permute-done.15.lo = f32[8,64,256]{2,1,0:T(8,128)S(1)} collective-permute-done((f32[8,64,256]{2,1,0:T(8,128)S(1)}, f32[8,64,256]{2,1,0:T(8,128)S(1)}, u32[]{:S(2)}, u32[]{:S(2)}) %collective-permute-start.15) | collective-permute-done | bytes 524320 | tf_op jit(solution)/shard_map/ppermute | solution.py:342
  119.1 3.4 %collective-permute-done.17.hi = f32[8,64,256]{2,1,0:T(8,128)S(1)} collective-permute-done((f32[8,64,256]{2,1,0:T(8,128)S(1)}, f32[8,64,256]{2,1,0:T(8,128)S(1)}, u32[]{:S(2)}, u32[]{:S(2)}) %collective-permute-start.17) | collective-permute-done | bytes 524320 | tf_op jit(solution)/shard_map/ppermute | solution.py:342
  122.5 1.0 whole.1
  (17 shorter events, 0.3 us)
Async XLA Ops:
  0.0 14.5 %collective-permute-start = (f32[16,64,256]{2,1,0:T(8,128)}, f32[16,64,256]{2,1,0:T(8,128)S(1)}, u32[]{:S(2)}, u32[]{:S(2)}) collective-permute-start(f32[16,64,256]{2,1,0:T(8,128)} %param.9), channel_id=1, source_target_pairs={{1,0},{2,1},{3,2},{4,3},{5,4},{6,5},{7,6},{8,7},{9,8},{10,9},{11,1... | collective-permute-start | bytes 3145736 | tf_op jit(solution)/shard_map/ppermute | solution.py:342
  4.1 2.2 %copy-start = (bf16[1,4,32,64,256]{4,3,2,1,0:T(8,128)(2,1)S(1)}, bf16[1,4,32,64,256]{4,3,2,1,0:T(8,128)(2,1)}, u32[]{:S(2)}) copy-start(bf16[1,4,32,64,256]{4,3,2,1,0:T(8,128)(2,1)} %images.1) | copy-start | bytes 12582916
  6.3 0.7 copy-start.1
  7.0 0.7 copy-start.2
  7.7 0.7 copy-start.3
  8.3 2.5 %copy-start.4 = (f32[16,64,256]{2,1,0:T(8,128)S(1)}, f32[16,64,256]{2,1,0:T(8,128)}, u32[]{:S(2)}) copy-start(f32[16,64,256]{2,1,0:T(8,128)} %param.9) | copy-start | bytes 3145732
  10.9 10.5 %collective-permute-start.2 = (f32[8,64,256]{2,1,0:T(8,128)S(1)}, f32[8,64,256]{2,1,0:T(8,128)S(1)}, u32[]{:S(2)}, u32[]{:S(2)}) collective-permute-start(f32[8,64,256]{2,1,0:T(8,128)S(1)} %get-tuple-element.36.refs_1_.refs_2_), channel_id=1, source_target_pairs={{0,1},{1,2},{2,3},{3,4},{4,5},{5,6},{6,7},{7,8},{8,9},{9,10},{10,1... | collective-permute-start | bytes 1572872 | tf_op jit(solution)/shard_map/ppermute | solution.py:342
  14.5 12.5 %collective-permute-start.1 = (f32[8,64,256]{2,1,0:T(8,128)S(1)}, f32[8,64,256]{2,1,0:T(8,128)S(1)}, u32[]{:S(2)}, u32[]{:S(2)}) collective-permute-start(f32[8,64,256]{2,1,0:T(8,128)S(1)} %get-tuple-element.34.refs_0_.refs_1_.refs_2_), channel_id=1, source_target_pairs={{0,1},{1,2},{2,3},{3,4},{4,5},{5,6},{6,7},{7,8},{8,9},{9,10},{10,1... | collective-permute-start | bytes 1572872 | tf_op jit(solution)/shard_map/ppermute | solution.py:342
  24.5 8.7 %collective-permute-start.5 = (f32[8,64,256]{2,1,0:T(8,128)S(1)}, f32[8,64,256]{2,1,0:T(8,128)S(1)}, u32[]{:S(2)}, u32[]{:S(2)}) collective-permute-start(f32[8,64,256]{2,1,0:T(8,128)S(1)} %get-tuple-element.46.refs_3_), channel_id=1, source_target_pairs={{0,1},{1,2},{2,3},{3,4},{4,5},{5,6},{6,7},{7,8},{8,9},{9,10},{10,1... | collective-permute-start | bytes 1572872 | tf_op jit(solution)/shard_map/ppermute | solution.py:342
  30.2 8.6 %collective-permute-start.3 = (f32[8,64,256]{2,1,0:T(8,128)S(1)}, f32[8,64,256]{2,1,0:T(8,128)S(1)}, u32[]{:S(2)}, u32[]{:S(2)}) collective-permute-start(f32[8,64,256]{2,1,0:T(8,128)S(1)} %get-tuple-element.45.refs_2_), channel_id=1, source_target_pairs={{0,1},{1,2},{2,3},{3,4},{4,5},{5,6},{6,7},{7,8},{8,9},{9,10},{10,1... | collective-permute-start | bytes 1572872 | tf_op jit(solution)/shard_map/ppermute | solution.py:342
  33.2 11.3 %collective-permute-start.6 = (f32[8,64,256]{2,1,0:T(8,128)S(1)}, f32[8,64,256]{2,1,0:T(8,128)S(1)}, u32[]{:S(2)}, u32[]{:S(2)}) collective-permute-start(f32[8,64,256]{2,1,0:T(8,128)S(1)} %collective-permute-done.5.refs_1_.refs_2_), channel_id=1, source_target_pairs={{0,1},{1,2},{2,3},{3,4},{4,5},{5,6},{6,7},{7,8},{8,9},{9,10},{10,1... | collective-permute-start | bytes 1572872 | tf_op jit(solution)/shard_map/ppermute | solution.py:342
  38.8 11.2 %collective-permute-start.4 = (f32[8,64,256]{2,1,0:T(8,128)S(1)}, f32[8,64,256]{2,1,0:T(8,128)S(1)}, u32[]{:S(2)}, u32[]{:S(2)}) collective-permute-start(f32[8,64,256]{2,1,0:T(8,128)S(1)} %collective-permute-done.3.refs_0_.refs_1_.refs_2_), channel_id=1, source_target_pairs={{0,1},{1,2},{2,3},{3,4},{4,5},{5,6},{6,7},{7,8},{8,9},{9,10},{10,1... | collective-permute-start | bytes 1572872 | tf_op jit(solution)/shard_map/ppermute | solution.py:342
  47.6 8.7 %collective-permute-start.9 = (f32[8,64,256]{2,1,0:T(8,128)S(1)}, f32[8,64,256]{2,1,0:T(8,128)S(1)}, u32[]{:S(2)}, u32[]{:S(2)}) collective-permute-start(f32[8,64,256]{2,1,0:T(8,128)S(1)} %get-tuple-element.51.refs_3_), channel_id=1, source_target_pairs={{0,1},{1,2},{2,3},{3,4},{4,5},{5,6},{6,7},{7,8},{8,9},{9,10},{10,1... | collective-permute-start | bytes 1572872 | tf_op jit(solution)/shard_map/ppermute | solution.py:342
  53.2 8.6 %collective-permute-start.7 = (f32[8,64,256]{2,1,0:T(8,128)S(1)}, f32[8,64,256]{2,1,0:T(8,128)S(1)}, u32[]{:S(2)}, u32[]{:S(2)}) collective-permute-start(f32[8,64,256]{2,1,0:T(8,128)S(1)} %get-tuple-element.50.refs_2_), channel_id=1, source_target_pairs={{0,1},{1,2},{2,3},{3,4},{4,5},{5,6},{6,7},{7,8},{8,9},{9,10},{10,1... | collective-permute-start | bytes 1572872 | tf_op jit(solution)/shard_map/ppermute | solution.py:342
  56.2 11.3 %collective-permute-start.10 = (f32[8,64,256]{2,1,0:T(8,128)S(1)}, f32[8,64,256]{2,1,0:T(8,128)S(1)}, u32[]{:S(2)}, u32[]{:S(2)}) collective-permute-start(f32[8,64,256]{2,1,0:T(8,128)S(1)} %collective-permute-done.9.refs_1_.refs_2_), channel_id=1, source_target_pairs={{0,1},{1,2},{2,3},{3,4},{4,5},{5,6},{6,7},{7,8},{8,9},{9,10},{10,1... | collective-permute-start | bytes 1572872 | tf_op jit(solution)/shard_map/ppermute | solution.py:342
  61.9 13.0 %collective-permute-start.8 = (f32[8,64,256]{2,1,0:T(8,128)S(1)}, f32[8,64,256]{2,1,0:T(8,128)S(1)}, u32[]{:S(2)}, u32[]{:S(2)}) collective-permute-start(f32[8,64,256]{2,1,0:T(8,128)S(1)} %collective-permute-done.7.refs_0_.refs_1_.refs_2_), channel_id=1, source_target_pairs={{0,1},{1,2},{2,3},{3,4},{4,5},{5,6},{6,7},{7,8},{8,9},{9,10},{10,1... | collective-permute-start | bytes 1572872 | tf_op jit(solution)/shard_map/ppermute | solution.py:342
  70.6 8.9 %collective-permute-start.13 = (f32[8,64,256]{2,1,0:T(8,128)S(1)}, f32[8,64,256]{2,1,0:T(8,128)S(1)}, u32[]{:S(2)}, u32[]{:S(2)}) collective-permute-start(f32[8,64,256]{2,1,0:T(8,128)S(1)} %get-tuple-element.56.refs_3_), channel_id=1, source_target_pairs={{0,1},{1,2},{2,3},{3,4},{4,5},{5,6},{6,7},{7,8},{8,9},{9,10},{10,1... | collective-permute-start | bytes 1572872 | tf_op jit(solution)/shard_map/ppermute | solution.py:342
  78.1 8.6 %collective-permute-start.11 = (f32[8,64,256]{2,1,0:T(8,128)S(1)}, f32[8,64,256]{2,1,0:T(8,128)S(1)}, u32[]{:S(2)}, u32[]{:S(2)}) collective-permute-start(f32[8,64,256]{2,1,0:T(8,128)S(1)} %get-tuple-element.55.refs_2_), channel_id=1, source_target_pairs={{0,1},{1,2},{2,3},{3,4},{4,5},{5,6},{6,7},{7,8},{8,9},{9,10},{10,1... | collective-permute-start | bytes 1572872 | tf_op jit(solution)/shard_map/ppermute | solution.py:342
  79.5 12.8 %collective-permute-start.14 = (f32[8,64,256]{2,1,0:T(8,128)S(1)}, f32[8,64,256]{2,1,0:T(8,128)S(1)}, u32[]{:S(2)}, u32[]{:S(2)}) collective-permute-start(f32[8,64,256]{2,1,0:T(8,128)S(1)} %collective-permute-done.13.refs_1_.refs_2_), channel_id=1, source_target_pairs={{0,1},{1,2},{2,3},{3,4},{4,5},{5,6},{6,7},{7,8},{8,9},{9,10},{10,1... | collective-permute-start | bytes 1572872 | tf_op jit(solution)/shard_map/ppermute | solution.py:342
  86.7 12.2 %collective-permute-start.12 = (f32[8,64,256]{2,1,0:T(8,128)S(1)}, f32[8,64,256]{2,1,0:T(8,128)S(1)}, u32[]{:S(2)}, u32[]{:S(2)}) collective-permute-start(f32[8,64,256]{2,1,0:T(8,128)S(1)} %collective-permute-done.11.refs_0_.refs_1_.refs_2_), channel_id=1, source_target_pairs={{0,1},{1,2},{2,3},{3,4},{4,5},{5,6},{6,7},{7,8},{8,9},{9,10},{10,1... | collective-permute-start | bytes 1572872 | tf_op jit(solution)/shard_map/ppermute | solution.py:342
  95.5 10.1 %collective-permute-start.16 = (f32[8,64,256]{2,1,0:T(8,128)S(1)}, f32[8,64,256]{2,1,0:T(8,128)S(1)}, u32[]{:S(2)}, u32[]{:S(2)}) collective-permute-start(f32[8,64,256]{2,1,0:T(8,128)S(1)} %get-tuple-element.61), channel_id=1, source_target_pairs={{0,13},{1,2},{2,15},{3,0},{4,1},{5,6},{6,3},{7,4},{8,5},{9,10},{10... | collective-permute-start | bytes 1572872 | tf_op jit(solution)/shard_map/ppermute | solution.py:342
  102.1 17.0 %collective-permute-start.15 = (f32[8,64,256]{2,1,0:T(8,128)S(1)}, f32[8,64,256]{2,1,0:T(8,128)S(1)}, u32[]{:S(2)}, u32[]{:S(2)}) collective-permute-start(f32[8,64,256]{2,1,0:T(8,128)S(1)} %get-tuple-element.60), channel_id=1, source_target_pairs={{0,13},{1,14},{2,15},{3,0},{4,1},{5,2},{6,3},{7,4},{8,5},{9,6},{10... | collective-permute-start | bytes 1572872 | tf_op jit(solution)/shard_map/ppermute | solution.py:342
  105.6 16.9 %collective-permute-start.17 = (f32[8,64,256]{2,1,0:T(8,128)S(1)}, f32[8,64,256]{2,1,0:T(8,128)S(1)}, u32[]{:S(2)}, u32[]{:S(2)}) collective-permute-start(f32[8,64,256]{2,1,0:T(8,128)S(1)} %collective-permute-done.16), channel_id=1, source_target_pairs={{0,0},{1,1},{2,14},{3,3},{4,4},{5,5},{6,2},{7,7},{8,8},{9,9},{10,6... | collective-permute-start | bytes 1572872 | tf_op jit(solution)/shard_map/ppermute | solution.py:342
